TPU v7x, 256 devices: a whole 4x4x8 slice. The times are simulated.
256 devices in a mesh: dp: 16 (over z, core), seq: 16 (over x, y).
Axes of the slice: x: 4, y: 4, z: 8, core: 2. Of those that a mesh axis runs over, the one named last changes fastest.
Arguments:
- queries: bfloat16 [16, 2048, 1024], P('dp', 'seq'), may hold values from -8 to 8
- grad_out: bfloat16 [16, 2048, 1024], P('dp', 'seq'), may hold values from -54 to 54
- image_kv: bfloat16 [1024, 256, 256], P(('dp', 'seq')), may hold values from -36 to 36
- image_tiles: int32 [1024], replicated, may hold values from 1 to 4
- doc_images: int32 [16, 6], replicated, may hold values from 0 to 1023, as said below
- doc_counts: int32 [16], replicated, may hold values from 1 to 6
- gate: float32 [1], replicated, may hold values from 0.3 to 1.2
Outputs:
- gated_out: bfloat16 [16, 2048, 1024], P('dp', 'seq')
- grad_queries: bfloat16 [16, 2048, 1024], P('dp', 'seq')
- grad_image_kv: float32 [1024, 256, 256], P(('dp', 'seq'))
- grad_gate: float32 [1], replicated
Inputs may be any that keep to these rules, and one draw needn't show every extreme that they name: `doc_images`: row d names only images of group d, ids (d) * 64 to (d + 1) * 64 - 1; the 6 ids of a row are distinct; entries at positions doc_counts[d] and beyond are not read.
All inputs are finite; a program needn't handle non-finite values.
Results may differ from a plain program's by a relative error of at most 0.007.
The roundings to bfloat16 on the way count: a program that leaves them out, or rounds other values in their place, can miss the bound.
Values may be sent and summed in bfloat16 or wider, within the bound.
No kernel may reach another device: no remote copies, remote signals or barrier semaphores. Data moves between devices by JAX's collectives and lax.ppermute only.
A program may use at most 64 MiB of HBM per device.

v0:
```python
import jax
import jax.numpy as jnp
from jax import lax
from jax.sharding import PartitionSpec as P

TILES = 4


def per_device(queries, grad_out, image_kv, image_tiles, doc_images, doc_counts, gate):
    doc_grp, tok_dev, width = queries.shape
    img_dev, img_tok, kv_width = image_kv.shape
    head_dim = kv_width // 2
    heads = width // head_dim
    max_img = doc_images.shape[1]
    seq_size = lax.axis_size("seq")
    group_img = img_dev * seq_size
    group_index = lax.axis_index("dp")
    cite = doc_grp * max_img
    own_lists = lax.dynamic_slice_in_dim(doc_images, group_index * doc_grp, doc_grp, 0)
    own_counts = lax.dynamic_slice_in_dim(doc_counts, group_index * doc_grp, doc_grp, 0)
    cited_ids = own_lists.reshape(cite)
    slot_ids = cited_ids - group_index * group_img
    slot_live = (jnp.arange(max_img, dtype=jnp.int32)[None, :] < own_counts[:, None]).reshape(cite)
    table_index = jnp.arange(image_tiles.shape[0], dtype=jnp.int32)
    slot_tiles = jnp.sum(
        jnp.where(cited_ids[:, None] == table_index[None, :], image_tiles[None, :], 0), axis=1
    )
    tile_index = jnp.arange(img_tok, dtype=jnp.int32) // (img_tok // TILES)
    tanh_gate = jnp.tanh(gate[0])
    score_scale = head_dim ** (-0.5)
    kv_store = lax.all_gather(image_kv, "seq", axis=0, tiled=True)

    def slot_block(slot_pos):
        block = lax.dynamic_index_in_dim(kv_store, slot_ids[slot_pos], 0, keepdims=False)
        live_keys = tile_index < slot_tiles[slot_pos]
        return (block[:, :head_dim], block[:, head_dim:], live_keys)

    def score_block(query_rows, key_block, live_keys):
        scores = (
            jnp.einsum("thd,kd->thk", query_rows, key_block, preferred_element_type=jnp.float32)
            * score_scale
        )
        return jnp.where(live_keys[None, None, :], scores, -jnp.inf)

    slot_grads = jnp.zeros((cite, img_tok, kv_width), jnp.float32)
    query_rows = queries[0].reshape(tok_dev, heads, head_dim)
    count = own_counts[0]

    def first_pass(slot_pos, carry):
        row_top, row_total = carry
        key_block, value_block, live_keys = slot_block(0 + slot_pos)
        scores = score_block(query_rows, key_block, live_keys)
        new_top = jnp.maximum(row_top, jnp.max(scores, axis=-1))
        row_total = row_total * jnp.exp(row_top - new_top) + jnp.sum(
            jnp.exp(scores - new_top[:, :, None]), axis=-1
        )
        return (new_top, row_total)

    start_top = jnp.full((tok_dev, heads), -jnp.inf, jnp.float32)
    start_total = jnp.zeros((tok_dev, heads), jnp.float32)
    row_top, row_total = lax.fori_loop(0, count, first_pass, (start_top, start_total))
    lse = (row_top + jnp.log(row_total))[:, :, None]

    def second_pass(slot_pos, attn):
        key_block, value_block, live_keys = slot_block(0 + slot_pos)
        probs_low = jnp.exp(score_block(query_rows, key_block, live_keys) - lse).astype(
            jnp.bfloat16
        )
        return attn + jnp.einsum(
            "thk,kd->thd", probs_low, value_block, preferred_element_type=jnp.float32
        )

    attn = lax.fori_loop(0, count, second_pass, jnp.zeros((tok_dev, heads, head_dim), jnp.float32))
    gated_list = [(tanh_gate * attn).astype(jnp.bfloat16).reshape(tok_dev, width)]
    cot_full = grad_out[0].reshape(tok_dev, heads, head_dim).astype(jnp.float32)
    gate_local = jnp.sum(cot_full * attn)
    dattn = tanh_gate * cot_full
    dattn_low = dattn.astype(jnp.bfloat16)
    delta = jnp.sum(dattn * attn, axis=-1, keepdims=True)

    def third_pass(slot_pos, carry):
        dquery, grads = carry
        key_block, value_block, live_keys = slot_block(0 + slot_pos)
        probs = jnp.exp(score_block(query_rows, key_block, live_keys) - lse)
        probs_low = probs.astype(jnp.bfloat16)
        dprob = jnp.einsum(
            "thd,kd->thk", dattn_low, value_block, preferred_element_type=jnp.float32
        )
        dscore = (probs * (dprob - delta)).astype(jnp.bfloat16)
        dquery = dquery + jnp.einsum(
            "thk,kd->thd", dscore, key_block, preferred_element_type=jnp.float32
        )
        dkeys = (
            jnp.einsum("thk,thd->kd", dscore, query_rows, preferred_element_type=jnp.float32)
            * score_scale
        )
        dvalues = jnp.einsum(
            "thk,thd->kd", probs_low, dattn_low, preferred_element_type=jnp.float32
        )
        grads = lax.dynamic_update_index_in_dim(
            grads, jnp.concatenate([dkeys, dvalues], axis=-1), 0 + slot_pos, 0
        )
        return (dquery, grads)

    start_dquery = jnp.zeros((tok_dev, heads, head_dim), jnp.float32)
    dquery, slot_grads = lax.fori_loop(0, count, third_pass, (start_dquery, slot_grads))
    dquery_list = [(dquery * score_scale).astype(jnp.bfloat16).reshape(tok_dev, width)]
    gated_out = jnp.stack(gated_list, axis=0)
    grad_queries = jnp.stack(dquery_list, axis=0)
    image_rows = jnp.arange(img_dev * lax.axis_size("seq"), dtype=jnp.int32)
    selector = ((image_rows[:, None] == slot_ids[None, :]) & slot_live[None, :]).astype(jnp.float32)
    grad_image_kv = lax.psum_scatter(
        jnp.einsum("gc,ckf->gkf", selector, slot_grads, precision=lax.Precision.HIGHEST),
        "seq",
        scatter_dimension=0,
        tiled=True,
    )
    gate_total = lax.psum(gate_local, ("dp", "seq"))
    norm_factor = float(doc_grp * lax.axis_size("dp") * tok_dev * seq_size * width) ** (-0.5)
    grad_gate = ((1.0 - tanh_gate * tanh_gate) * gate_total * norm_factor).reshape(1)
    return (gated_out, grad_queries, grad_image_kv, grad_gate)


def solution(mesh):
    return jax.shard_map(
        per_device,
        mesh=mesh,
        in_specs=(
            P("dp", "seq", None),
            P("dp", "seq", None),
            P(("dp", "seq"), None, None),
            P(),
            P(),
            P(),
            P(),
        ),
        out_specs=(P("dp", "seq", None), P("dp", "seq", None), P(("dp", "seq"), None, None), P()),
        check_vma=False,
    )
```

profile of v0, /device:TPU:32, one launch (start us, length us, event | category | flops | bytes accessed | tf_op | source)
XLA Modules:
  0.0 396.7 jit_solution(16116330426259282267)
XLA Ops:
  7.2 0.7 all-gather.2.cloned.1.call-update
  8.7 1.1 copy.49
  10.0 1.1 copy.54
  11.9 0.7 iota_compare_fusion.2
  12.7 76.2 %all-gather.2.cloned.1.call-done = bf16[64,256,256]{2,1,0:T(8,128)(2,1)} async-done(((bf16[4,256,256]{2,1,0:T(8,128)(2,1)}), bf16[64,256,256]{2,1,0:T(8,128)(2,1)}) %all-gather.2.cloned.1.call-update) | async-done | bytes 8388624 | tf_op jit(solution)/shard_map/all_gather | solution.py:31
  88.9 6.4 %while.37 = (s32[]{:T(128)}, f32[128,8]{0,1:T(8,128)S(1)}, f32[128,8]{0,1:T(8,128)S(1)}, s32[]{:T(128)}, s32[6]{0:T(128)S(1)}, /*index=5*/s32[6]{0:T(128)S(1)}, ...) while((s32[]{:T(128)}, f32[128,8]{0,1:T(8,128)S(1)}, ...), condition=%wide.region_4.5_spmd.clone, body=%wide.region_1.4_spmd.clone.sunk | while | flops 68423944 | bytes 2741217 | solution.py:61
  93.2 0.9 dynamic-slice_bitcast_fusion.6
  95.4 6.5 %while.38 = (s32[]{:T(128)}, f32[128,8,128]{2,0,1:T(8,128)S(1)}, s32[]{:T(128)}, s32[6]{0:T(128)S(1)}, s32[6]{0:T(128)S(1)}, /*index=5*/bf16[64,256,256]{2,1,0:T...) while((s32[]{:T(128)}, f32[128,8,128]{2,0,1:T(8,128)S(1)}, ...), condition=%wide.region_6.7_spmd.clone, body=%wide.region_5.6_spmd.clone.sunk | while | flops 135399680 | bytes 1708769 | solution.py:73
  98.9 0.7 fusion.70
  99.5 0.9 dynamic-slice_bitcast_fusion.7
  100.5 0.7 fusion.71
  102.1 0.8 multiply_reduce_fusion
  102.9 1.5 broadcast_in_dim.74.clone
  104.4 15.1 %while.39 = (s32[]{:T(128)}, f32[128,8,128]{2,0,1:T(8,128)S(1)}, f32[6,256,256]{2,0,1:T(8,128)}, s32[]{:T(128)}, s32[6]{0:T(128)S(1)}, /*index=5*/s32[6]{0:T(128...) while((s32[]{:T(128)}, f32[128,8,128]{2,0,1:T(8,128)S(1)}, ...), condition=%wide.region_9.10_spmd.clone, body=%wide.region_8.9_spmd.clone.sunk | while | flops 337611008 | bytes 9118717 | solution.py:106
  105.7 0.6 dynamic_slice.67
  108.3 0.7 fusion.79
  109.0 0.9 dynamic-slice_bitcast_fusion.8
  111.7 6.9 %dynamic_update_slice.6 = f32[6,256,256]{2,0,1:T(8,128)} dynamic-update-slice(f32[6,256,256]{2,0,1:T(8,128)} %get-tuple-element.608, f32[1,256,256]{2,0,1:T(1,128)S(1)} %copy.72, s32[]{:T(128)S(6)} %select_n.132, s32[]{:T(128)} %constant.74.clone.1..sunk.2, s32[]{:T(128)} %constant.74.clone.1..sunk.2) | dynamic-update-slice | bytes 524292 | tf_op jit(solution)/shard_map/while/body/jit(dynamic_update_index_in_dim)/dynamic_update_slice | solution.py:100
  119.5 8.5 %fusion.35 = f32[64,256,256]{2,0,1:T(8,128)S(1)} fusion(f32[6,256,256]{2,0,1:T(8,128)} %get-tuple-element.169, s32[6]{0:T(128)S(1)} %get-tuple-element.287, pred[6]{0:T(512)(128)(4,1)S(1)} %iota_compare_fusion.2), kind=kOutput, calls=%fused_computation.72 | convolution fusion | flops 301990656 | bytes 18350110 | tf_op jit(solution)/shard_map/gc,ckf->gkf/dot_general | solution.py:113
  128.0 19.3 %copy.58 = f32[64,256,256]{2,1,0:T(8,128)} copy(f32[64,256,256]{2,0,1:T(8,128)S(1)} %fusion.35) | data formatting | bytes 33554432 | tf_op jit(solution)/shard_map/gc,ckf->gkf/dot_general | solution.py:113
  147.3 205.9 %psum.7 = f32[]{:T(128)} all-reduce(f32[]{:T(128)} %get-tuple-element.285), channel_id=1, replica_groups=mesh['dp'=16,'seq'=16] {'dp','seq'}, use_global_device_ids=true, to_apply=%region_12.13 | all-reduce | flops 1 | bytes 8 | tf_op jit(solution)/shard_map/psum | solution.py:118
  353.2 0.8 copy.66
  354.3 0.8 stack_reshape.7
  355.8 33.0 %reduce-scatter.2.cloned.1.call-done = f32[4,256,256]{2,1,0:T(8,128)} async-done(((f32[64,256,256]{2,1,0:T(8,128)}), f32[4,256,256]{2,1,0:T(8,128)}) %reduce-scatter.2.cloned.1.call-update) | async-done | bytes 1048592 | tf_op jit(solution)/shard_map/reduce_scatter | solution.py:112
  (40 shorter events, 7.5 us)
Async XLA Ops:
  7.2 3.9 copy-start.2
  7.2 4.5 %copy-start.1 = (s32[16,6]{0,1:T(8,128)S(1)}, s32[16,6]{0,1:T(8,128)}, u32[]{:S(2)}) copy-start(s32[16,6]{0,1:T(8,128)} %param.17) | copy-start | bytes 1156
  7.2 5.3 %copy-start = (s32[1024]{0:T(1024)S(1)}, s32[1024]{0:T(1024)}, u32[]{:S(2)}) copy-start(s32[1024]{0:T(1024)} %param.16) | copy-start | bytes 12292
  7.2 81.7 %all-gather.2.cloned.1.call-start = ((), (), s32[]{:S(2)}) async-start(), calls=%async_computation.1 | async-start | bytes 8912896 | tf_op jit(solution)/shard_map/all_gather | solution.py:31
  7.9 380.8 %reduce-scatter.2.cloned.1.call-start = ((), (), s32[]{:S(2)}) async-start(), calls=%async_computation.2 | async-start | bytes 17825792 | tf_op jit(solution)/shard_map/reduce_scatter | solution.py:112
Sparse Core Ops, SparseCore 0:
  10.5 78.4 all-gather.1
  147.4 241.2 reduce-scatter.1
where the time goes:
time: 400 us; the launch traced here: 397 us
  blocking collectives  206 us (52%)
  waiting for transfers between devices  110 us (28%)
  local copies, waits for them, and re-layouts  39.3 us (10%)
  between operations  16.7 us (4%)
  matrix products  11.2 us (3%)
  loops' own time  9.86 us (2%)
    psum x1, blocking collectives, per_device(): gate_total = lax.psum(gate_local, ('dp', 'seq'))  206 us
    all_gather x1, waiting for transfers between devices, per_device(): kv_store = lax.all_gather(image_kv, 'seq', axis=0, tiled=True)  76.2 us
    reduce_scatter x1, waiting for transfers between devices, per_device(): lax.psum_scatter(jnp.einsum('gc,ckf->gkf', selector, slot_grads, precisio...  33 us
    dot_general x1, local copies, waits for them, and re-layouts, per_device(): jnp.einsum('gc,ckf->gkf', selector, slot_grads, precision=lax.Precision.H...  19.3 us
    dot_general x1, matrix products, per_device(): jnp.einsum('gc,ckf->gkf', selector, slot_grads, precision=lax.Precision.H...  8.5 us
  transfers between devices with their start and end apart: 2, of which 2 were waited for; matrix products, arithmetic and copies ran while one was open for 1% of the time, Pallas kernels for 0%

commit v1 on v0

v1 whole, which is shorter than its diff:
```python
import functools

import jax
import jax.numpy as jnp
from jax import lax
from jax.experimental import pallas as pl
from jax.experimental.pallas import tpu as pltpu
from jax.sharding import PartitionSpec as P

TILES = 4
CHUNK = 16
KEY_BLOCK = 256
ROW_BLOCK = 256
F32 = jnp.float32
BF16 = jnp.bfloat16

SMEM = functools.partial(pl.BlockSpec, memory_space=pltpu.SMEM)
VMEM = functools.partial(pl.BlockSpec, memory_space=pltpu.VMEM)


def contract(a, b, dim_a, dim_b):
    return lax.dot_general(a, b, (((dim_a,), (dim_b,)), ((), ())), preferred_element_type=F32)


def slot_place(docs, counts, group, slot, group_img, img_dev):
    live = slot < counts[group]
    local = jnp.where(live, docs[group, slot] - group * group_img, 0)
    return live, lax.div(local, img_dev), lax.rem(local, img_dev)


def select_kernel(docs, counts, chunks_ref, out_ref):
    group = lax.axis_index("dp")
    parts = chunks_ref.shape[0]
    img_dev = chunks_ref.shape[1] // CHUNK
    for slot in range(docs.shape[1]):
        _, owner, place = slot_place(docs, counts, group, slot, parts * img_dev, img_dev)
        rows = pl.ds(pl.multiple_of(place * CHUNK, CHUNK), CHUNK)
        chunk = chunks_ref[owner, rows, :]
        for part in range(parts):
            out_ref[part, slot * CHUNK : (slot + 1) * CHUNK, :] = chunk


def attention_kernel(
    docs, counts, tiles, gate,
    kv_ref, query_ref, cot_ref,
    gated_ref, dquery_ref, dkv_ref,
    query_rows, dattn_rows, cot_t, kv_rows, exp_t, prob_t, dscore_t, attn_t, dquery_t, dkv_rows,
    top_part, total_part,
):
    group = lax.axis_index("dp")
    parts = kv_ref.shape[0]
    slots = docs.shape[1]
    head_dim = kv_ref.shape[2] // 2
    heads = query_ref.shape[1] // head_dim
    tok = query_ref.shape[0]
    rows = heads * tok
    scale = head_dim ** (-0.5)
    img_tok = parts * CHUNK
    tile_tok = img_tok // TILES
    col_blocks = [slice(c, c + ROW_BLOCK) for c in range(0, rows, ROW_BLOCK)]
    head_cols = [slice(h * head_dim, (h + 1) * head_dim) for h in range(heads)]
    head_rows = [slice(h * tok, (h + 1) * tok) for h in range(heads)]
    tanh_gate = jnp.tanh(jnp.full((1, rows), gate[0], F32))
    tanh_narrow = tanh_gate[:, :head_dim]

    kv_rows[...] = jnp.zeros_like(kv_rows)
    starts, live_tiles = [], []
    start = jnp.int32(0)
    for slot in range(slots):
        live = slot < counts[group]
        count = jnp.where(live, tiles[jnp.where(live, docs[group, slot], 0)], 0)
        starts.append(start)
        live_tiles.append(count)
        for part in range(parts):
            at = pl.ds(pl.multiple_of(start * tile_tok + part * CHUNK, CHUNK), CHUNK)
            kv_rows[at, :] = kv_ref[part, slot * CHUNK : (slot + 1) * CHUNK, :]
        start = start + count
    live_keys = start * tile_tok
    blocks = lax.div(live_keys + (KEY_BLOCK - 1), KEY_BLOCK)

    for cols, at in zip(head_cols, head_rows, strict=True):
        query_rows[at, :] = query_ref[:, cols]
        cot = cot_ref[:, cols].astype(F32)
        dattn_rows[at, :] = (tanh_narrow * cot).astype(BF16)
        cot_t[:, at] = cot.T

    top_part[...] = jnp.full_like(top_part, -jnp.inf)
    total_part[...] = jnp.zeros_like(total_part)
    attn_t[...] = jnp.zeros_like(attn_t)
    dquery_t[...] = jnp.zeros_like(dquery_t)

    def block_rows(block):
        return pl.ds(pl.multiple_of(block * KEY_BLOCK, KEY_BLOCK), KEY_BLOCK)

    def fold(x, op):
        return op(x.reshape(KEY_BLOCK // 8, 8, x.shape[1]), axis=0)

    def score_pass(block, carry):
        at = block_rows(block)
        keys = kv_rows[at, :head_dim]
        key_index = lax.broadcasted_iota(jnp.int32, (KEY_BLOCK, ROW_BLOCK), 0)
        live = key_index < live_keys - block * KEY_BLOCK
        for cols in col_blocks:
            scores = contract(keys, query_rows[cols, :], 1, 1) * scale
            scores = jnp.where(live, scores, -jnp.inf)
            exp_t[at, cols] = scores
            top_part[:, cols] = jnp.maximum(top_part[:, cols], fold(scores, jnp.max))
        return carry

    lax.fori_loop(0, blocks, score_pass, 0)
    top = jnp.max(top_part[...], axis=0, keepdims=True)

    def exp_pass(block, carry):
        at = block_rows(block)
        for cols in col_blocks:
            raised = jnp.exp(exp_t[at, cols] - top[:, cols])
            exp_t[at, cols] = raised
            total_part[:, cols] += fold(raised, jnp.sum)
        return carry

    lax.fori_loop(0, blocks, exp_pass, 0)
    inverse = 1.0 / jnp.sum(total_part[...], axis=0, keepdims=True)

    def attn_pass(block, carry):
        at = block_rows(block)
        values = kv_rows[at, head_dim:]
        for cols in col_blocks:
            probs_low = (exp_t[at, cols] * inverse[:, cols]).astype(BF16)
            prob_t[at, cols] = probs_low
            attn_t[:, cols] += contract(values, probs_low, 0, 0)
        return carry

    lax.fori_loop(0, blocks, attn_pass, 0)
    gate_rows = jnp.sum(cot_t[...] * attn_t[...], axis=0, keepdims=True)
    delta = tanh_gate * gate_rows

    def grad_pass(block, carry):
        at = block_rows(block)
        keys, values = kv_rows[at, :head_dim], kv_rows[at, head_dim:]
        for cols in col_blocks:
            probs = exp_t[at, cols] * inverse[:, cols]
            dprob = contract(values, dattn_rows[cols, :], 1, 1)
            dscore = (probs * (dprob - delta[:, cols])).astype(BF16)
            dscore_t[:, cols] = dscore
            dquery_t[:, cols] += contract(keys, dscore, 0, 0)
        dkeys = contract(dscore_t[...], query_rows[...], 1, 0) * scale
        dvalues = contract(prob_t[at, :], dattn_rows[...], 1, 0)
        dkv_rows[at, :head_dim] = dkeys.astype(BF16)
        dkv_rows[at, head_dim:] = dvalues.astype(BF16)
        return carry

    lax.fori_loop(0, blocks, grad_pass, 0)

    for cols, at in zip(head_cols, head_rows, strict=True):
        gated_ref[:, cols] = (attn_t[:, at].T * tanh_narrow).astype(BF16)
        dquery_ref[:, cols] = (dquery_t[:, at].T * scale).astype(BF16)

    for slot in range(slots):
        for part in range(parts):
            row = starts[slot] * tile_tok + part * CHUNK
            grads = dkv_rows[pl.ds(pl.multiple_of(row, CHUNK), CHUNK), :]
            live = part * CHUNK < live_tiles[slot] * tile_tok
            dkv_ref[part, slot * CHUNK : (slot + 1) * CHUNK, :] = jnp.where(
                live, grads, jnp.zeros_like(grads)
            )
    term = jnp.broadcast_to(jnp.sum(gate_rows, axis=1, keepdims=True), (CHUNK, 2 * head_dim))
    high = term.astype(BF16).astype(F32)
    middle = (term - high).astype(BF16).astype(F32)
    low = term - high - middle
    index = lax.broadcasted_iota(jnp.int32, term.shape, 0)
    split = jnp.where(index == 0, high, jnp.where(index == 1, middle, low)).astype(BF16)
    for part in range(parts):
        dkv_ref[part, slots * CHUNK :, :] = split


def sum_kernel(docs, counts, partial_ref, out_ref, gate_ref):
    group = lax.axis_index("dp")
    parts = partial_ref.shape[0]
    slots = docs.shape[1]
    img_dev = out_ref.shape[1] // CHUNK
    out_ref[...] = jnp.zeros_like(out_ref)
    for slot in range(slots + 1):
        at = slice(slot * CHUNK, (slot + 1) * CHUNK)
        total = partial_ref[0, at, :].astype(F32)
        for part in range(1, parts):
            total = total + partial_ref[part, at, :].astype(F32)
        if slot == slots:
            gate_sum = total[0:1, :128] + total[1:2, :128] + total[2:3, :128]
            gate_ref[...] = jnp.broadcast_to(gate_sum, gate_ref.shape)
        else:
            live, owner, place = slot_place(docs, counts, group, slot, parts * img_dev, img_dev)
            rows = pl.ds(pl.multiple_of(place * CHUNK, CHUNK), CHUNK)

            @pl.when(live)
            def _():
                out_ref[owner, rows, :] = total.astype(BF16)


def sum_over(x, axis):
    size = lax.axis_size(axis)
    step = 1
    while step < size:
        x = x + lax.ppermute(x, axis, [(i, i ^ step) for i in range(size)])
        step *= 2
    return x


def per_device(queries, grad_out, image_kv, image_tiles, doc_images, doc_counts, gate):
    _, tok, width = queries.shape
    img_dev, img_tok, kv_width = image_kv.shape
    head_dim = kv_width // 2
    rows = tok * (width // head_dim)
    slots = doc_images.shape[1]
    parts = lax.axis_size("seq")
    keys = slots * img_tok
    sent = slots * CHUNK

    chunks = image_kv.reshape(img_dev, parts, CHUNK, kv_width).transpose(1, 0, 2, 3)
    chunks = lax.all_to_all(chunks.reshape(parts, img_dev * CHUNK, kv_width), "seq", 0, 0)
    cited = pl.pallas_call(
        select_kernel,
        out_shape=jax.ShapeDtypeStruct((parts, sent, kv_width), BF16),
        in_specs=[SMEM(), SMEM(), VMEM()],
        out_specs=VMEM(),
        name="select_cited",
    )(doc_images, doc_counts, chunks)
    kv_cited = lax.all_to_all(cited, "seq", 0, 0)

    gated, dquery, partial = pl.pallas_call(
        attention_kernel,
        out_shape=(
            jax.ShapeDtypeStruct((tok, width), BF16),
            jax.ShapeDtypeStruct((tok, width), BF16),
            jax.ShapeDtypeStruct((parts, sent + CHUNK, kv_width), BF16),
        ),
        in_specs=[SMEM()] * 4 + [VMEM()] * 3,
        out_specs=(VMEM(), VMEM(), VMEM()),
        scratch_shapes=[
            pltpu.VMEM((rows, head_dim), BF16),
            pltpu.VMEM((rows, head_dim), BF16),
            pltpu.VMEM((head_dim, rows), F32),
            pltpu.VMEM((keys, kv_width), BF16),
            pltpu.VMEM((keys, rows), F32),
            pltpu.VMEM((keys, rows), BF16),
            pltpu.VMEM((KEY_BLOCK, rows), BF16),
            pltpu.VMEM((head_dim, rows), F32),
            pltpu.VMEM((head_dim, rows), F32),
            pltpu.VMEM((keys, kv_width), BF16),
            pltpu.VMEM((8, rows), F32),
            pltpu.VMEM((8, rows), F32),
        ],
        compiler_params=pltpu.CompilerParams(vmem_limit_bytes=40 * 1024 * 1024),
        name="attention",
    )(doc_images, doc_counts, image_tiles, gate, kv_cited, queries[0], grad_out[0])

    partial = lax.all_to_all(partial, "seq", 0, 0)
    summed, gate_sum = pl.pallas_call(
        sum_kernel,
        out_shape=(
            jax.ShapeDtypeStruct((parts, img_dev * CHUNK, kv_width), BF16),
            jax.ShapeDtypeStruct((8, 128), F32),
        ),
        in_specs=[SMEM(), SMEM(), VMEM()],
        out_specs=(VMEM(), VMEM()),
        name="sum_partials",
    )(doc_images, doc_counts, partial)
    owned = lax.all_to_all(summed, "seq", 0, 0)
    grad_image_kv = (
        owned.reshape(parts, img_dev, CHUNK, kv_width)
        .transpose(1, 0, 2, 3)
        .reshape(img_dev, img_tok, kv_width)
        .astype(F32)
    )

    gate_total = sum_over(gate_sum, "dp")[0, :1]
    tanh_gate = jnp.tanh(gate)
    norm_factor = float(lax.axis_size("dp") * tok * parts * width) ** (-0.5)
    grad_gate = (1.0 - tanh_gate * tanh_gate) * gate_total * norm_factor
    return gated[None], dquery[None], grad_image_kv, grad_gate


def solution(mesh):
    return jax.shard_map(
        per_device,
        mesh=mesh,
        in_specs=(
            P("dp", "seq", None),
            P("dp", "seq", None),
            P(("dp", "seq"), None, None),
            P(),
            P(),
            P(),
            P(),
        ),
        out_specs=(P("dp", "seq", None), P("dp", "seq", None), P(("dp", "seq"), None, None), P()),
        check_vma=False,
    )
```

time: 400 us -> 95.4 us (0.24)
  blocking collectives: 206 us -> 15.4 us
  waiting for transfers between devices: 110 us -> 30.5 us
  local copies, waits for them, and re-layouts: 39.3 us -> 5.61 us
  starting transfers between devices: 0.08 us -> 28.6 us
  between operations: 16.7 us -> 3.22 us
  matrix products: 11.2 us -> 0 us
  Pallas kernels: 0 us -> 10.6 us
  loops' own time: 9.86 us -> 0 us
    psum x1 -> x0, blocking collectives: 206 us -> none  [per_device(): gate_total = lax.psum(gate_local, ('dp', 'seq'))]
    all_gather x1 -> x0, waiting for transfers between devices: 76.2 us -> none  [per_device(): kv_store = lax.all_gather(image_kv, 'seq', axis=0, tiled=True)]
    reduce_scatter x1 -> x0, waiting for transfers between devices: 33 us -> none  [per_device(): lax.psum_scatter(jnp.einsum('gc,ckf->gkf', selector, slot_grads, precisio...]
    all_to_all x0 -> x3, waiting for transfers between devices: none -> 23.2 us  [the longest x1 12.4 us: per_device(): kv_cited = lax.all_to_all(cited, 'seq', 0, 0)]
    dot_general x1 -> x0, local copies, waits for them, and re-layouts: 19.3 us -> none  [per_device(): jnp.einsum('gc,ckf->gkf', selector, slot_grads, precision=lax.Precision.H...]
    all_to_all x0 -> x1, blocking collectives: none -> 15.4 us  [per_device(): partial = lax.all_to_all(partial, 'seq', 0, 0)]
    all_to_all x0 -> x3, starting transfers between devices: none -> 14.8 us  [the longest x1 7.17 us: per_device(): lax.all_to_all(chunks.reshape(parts, img_dev * CHUNK, kv_width), 'seq', 0...]
    ppermute x0 -> x4, starting transfers between devices: none -> 13.8 us  [sum_over(): x = x + lax.ppermute(x, axis, [(i, i ^ step) for i in range(size)])]
  transfers between devices with their start and end apart: 2 -> 7, of which waited for: 2 -> 6; matrix products, arithmetic and copies ran while one was open for 1% -> 1% of each run, Pallas kernels for 0% -> 0%
where the time goes in v1:
time: 95.4 us; the launch traced here: 94.1 us
  waiting for transfers between devices  30.5 us (32%)
  starting transfers between devices  28.6 us (30%)
  blocking collectives  15.4 us (16%)
  Pallas kernels  10.6 us (11%)
  local copies, waits for them, and re-layouts  5.61 us (6%)
  between operations  3.22 us (3%)
    all_to_all x1, blocking collectives, per_device(): partial = lax.all_to_all(partial, 'seq', 0, 0)  15.4 us
    ppermute x4, starting transfers between devices, sum_over(): x = x + lax.ppermute(x, axis, [(i, i ^ step) for i in range(size)])  13.8 us
    all_to_all x1, waiting for transfers between devices, per_device(): kv_cited = lax.all_to_all(cited, 'seq', 0, 0)  12.4 us
    all_to_all x1, waiting for transfers between devices, per_device(): lax.all_to_all(chunks.reshape(parts, img_dev * CHUNK, kv_width), 'seq', 0...  10.8 us
    ppermute x4, waiting for transfers between devices, sum_over(): x = x + lax.ppermute(x, axis, [(i, i ^ step) for i in range(size)])  7.33 us
    all_to_all x1, starting transfers between devices, per_device(): lax.all_to_all(chunks.reshape(parts, img_dev * CHUNK, kv_width), 'seq', 0...  7.17 us
    pallas_call x1, Pallas kernels, per_device(): pl.pallas_call(attention_kernel, out_shape=(jax.ShapeDtypeStruct((tok, wi...  6.41 us
    all_to_all x1, starting transfers between devices, per_device(): owned = lax.all_to_all(summed, 'seq', 0, 0)  3.85 us
  transfers between devices with their start and end apart: 7, of which 6 were waited for; matrix products, arithmetic and copies ran while one was open for 1% of the time, Pallas kernels for 0%

profile of v1, /device:TPU:32, one launch (start us, length us, event | category | flops | bytes accessed | tf_op | source)
XLA Modules:
  0.0 94.1 jit_solution(14263957993974706464)
XLA Ops:
  0.6 1.9 %copy.11 = bf16[4,16,16,256]{3,2,0,1:T(8,128)(2,1)} copy(bf16[4,16,16,256]{3,2,1,0:T(8,128)(2,1)} %bitcast.18) | data formatting | bytes 1048576 | tf_op jit(solution)/shard_map/reshape | solution.py:218
  2.5 7.2 %all-to-all-start = ((bf16[16,64,256]{2,1,0:T(8,128)(2,1)}), bf16[16,64,256]{2,1,0:T(8,128)(2,1)S(1)}, u32[]{:S(2)}, u32[]{:S(2)}) async-start(bf16[16,64,256]{2,1,0:T(8,128)(2,1)} %bitcast.2), calls=%async_computation | async-start | bytes 1048576 | tf_op jit(solution)/shard_map/all_to_all | solution.py:219
  9.7 0.7 copy.13.docs
  10.4 10.8 %all-to-all-done.chunks_ref = bf16[16,64,256]{2,1,0:T(8,128)(2,1)S(1)} async-done(((bf16[16,64,256]{2,1,0:T(8,128)(2,1)}), bf16[16,64,256]{2,1,0:T(8,128)(2,1)S(1)}, u32[]{:S(2)}, u32[]{:S(2)}) %all-to-all-start) | async-done | bytes 524320 | tf_op jit(solution)/shard_map/all_to_all | solution.py:219
  21.2 0.8 copy-done.5
  22.0 2.0 %select_cited.1 = bf16[16,96,256]{2,1,0:T(8,128)(2,1)} custom-call(s32[16,6]{1,0:T(8,128)} %copy.13.docs, s32[16]{0:T(128)} %counts.5, bf16[16,64,256]{2,1,0:T(8,128)(2,1)} %copy-done.5), custom_call_target="tpu_custom_call" | custom-call | tf_op jit(solution)/shard_map/select_cited/pallas_call | solution.py:220
  24.0 3.8 %all-to-all-start.1 = ((bf16[16,96,256]{2,1,0:T(8,128)(2,1)}), bf16[16,96,256]{2,1,0:T(8,128)(2,1)S(1)}, u32[]{:S(2)}, u32[]{:S(2)}) async-start(bf16[16,96,256]{2,1,0:T(8,128)(2,1)} %select_cited.1), calls=%async_computation.1 | async-start | bytes 1572864 | tf_op jit(solution)/shard_map/all_to_all | solution.py:227
  28.5 12.4 %all-to-all-done.1.kv_ref = bf16[16,96,256]{2,1,0:T(8,128)(2,1)S(1)} async-done(((bf16[16,96,256]{2,1,0:T(8,128)(2,1)}), bf16[16,96,256]{2,1,0:T(8,128)(2,1)S(1)}, u32[]{:S(2)}, u32[]{:S(2)}) %all-to-all-start.1) | async-done | bytes 786464 | tf_op jit(solution)/shard_map/all_to_all | solution.py:227
  40.9 0.6 copy-done.3
  41.5 6.4 %attention.1 = (bf16[128,1024]{1,0:T(8,128)(2,1)}, bf16[128,1024]{1,0:T(8,128)(2,1)}, bf16[16,112,256]{2,1,0:T(8,128)(2,1)S(1)}) custom-call(s32[16,6]{1,0:T(8,128)S(1)} %copy-done.2, s32[16]{0:T(128)S(1)} %copy-done.3, s32[1024]{0:T(1024)S(1)} %copy-done.4, f32[1]{0:T(128)S(6)} %copy.16.gate, bf16[16,96,256]{2,1,0:T(8,128)(2,1)S(1)} %all-to-all-done.1.kv_ref, ...), custom_call_target="tpu_custom_call" | custom-call | tf_op jit(solution)/shard_map/attention/pallas_call | solution.py:229
  47.9 15.4 %all_to_all.20.partial_ref = bf16[16,112,256]{2,1,0:T(8,128)(2,1)} all-to-all(bf16[16,112,256]{2,1,0:T(8,128)(2,1)S(1)} %get-tuple-element.11), channel_id=1, replica_groups=mesh['dp'=16,'seq'=16] {'seq'}, dimensions={0} | all-to-all | bytes 1835008 | tf_op jit(solution)/shard_map/all_to_all | solution.py:256
  63.3 2.1 %sum_partials.1 = (bf16[16,64,256]{2,1,0:T(8,128)(2,1)}, f32[8,128]{1,0:T(8,128)}) custom-call(s32[16,6]{1,0:T(8,128)} %copy.13.docs, s32[16]{0:T(128)} %counts.5, bf16[16,112,256]{2,1,0:T(8,128)(2,1)} %all_to_all.20.partial_ref), custom_call_target="tpu_custom_call" | custom-call | tf_op jit(solution)/shard_map/sum_partials/pallas_call | solution.py:257
  65.5 3.8 %all-to-all-start.3 = ((bf16[16,64,256]{2,1,0:T(8,128)(2,1)}), bf16[16,64,256]{2,1,0:T(8,128)(2,1)S(1)}, u32[]{:S(2)}, u32[]{:S(2)}) async-start(bf16[16,64,256]{2,1,0:T(8,128)(2,1)} %get-tuple-element.12), calls=%async_computation.3 | async-start | bytes 1048576 | tf_op jit(solution)/shard_map/all_to_all | solution.py:267
  69.3 0.1 collective-permute-start
  69.4 1.2 %collective-permute-done = f32[8,128]{1,0:T(8,128)S(1)} collective-permute-done((f32[8,128]{1,0:T(8,128)S(1)}, f32[8,128]{1,0:T(8,128)S(1)}, u32[]{:S(2)}, u32[]{:S(2)}) %collective-permute-start) | collective-permute-done | bytes 4128 | tf_op jit(solution)/shard_map/ppermute | solution.py:203
  70.6 4.2 %collective-permute-start.1 = (f32[8,128]{1,0:T(8,128)S(1)}, f32[8,128]{1,0:T(8,128)S(1)}, u32[]{:S(2)}, u32[]{:S(2)}) collective-permute-start(f32[8,128]{1,0:T(8,128)S(1)} %add.12), channel_id=1, source_target_pairs={{0,32},{16,48},{32,0},{48,16},{64,96},{80,112},{96,64},{112,80},{1... | collective-permute-start | bytes 12296 | tf_op jit(solution)/shard_map/ppermute | solution.py:203
  74.8 1.6 %collective-permute-done.1 = f32[8,128]{1,0:T(8,128)S(1)} collective-permute-done((f32[8,128]{1,0:T(8,128)S(1)}, f32[8,128]{1,0:T(8,128)S(1)}, u32[]{:S(2)}, u32[]{:S(2)}) %collective-permute-start.1) | collective-permute-done | bytes 4128 | tf_op jit(solution)/shard_map/ppermute | solution.py:203
  76.4 1.4 %collective-permute-start.2 = (f32[8,128]{1,0:T(8,128)S(1)}, f32[8,128]{1,0:T(8,128)S(1)}, u32[]{:S(2)}, u32[]{:S(2)}) collective-permute-start(f32[8,128]{1,0:T(8,128)S(1)} %add.13), channel_id=1, source_target_pairs={{0,64},{16,80},{32,96},{48,112},{64,0},{80,16},{96,32},{112,48},{1... | collective-permute-start | bytes 12296 | tf_op jit(solution)/shard_map/ppermute | solution.py:203
  77.8 3.1 %collective-permute-done.2 = f32[8,128]{1,0:T(8,128)S(1)} collective-permute-done((f32[8,128]{1,0:T(8,128)S(1)}, f32[8,128]{1,0:T(8,128)S(1)}, u32[]{:S(2)}, u32[]{:S(2)}) %collective-permute-start.2) | collective-permute-done | bytes 4128 | tf_op jit(solution)/shard_map/ppermute | solution.py:203
  80.9 8.1 %collective-permute-start.3 = (f32[8,128]{1,0:T(8,128)S(1)}, f32[8,128]{1,0:T(8,128)S(1)}, u32[]{:S(2)}, u32[]{:S(2)}) collective-permute-start(f32[8,128]{1,0:T(8,128)S(1)} %add.14), channel_id=1, source_target_pairs={{0,128},{16,144},{32,160},{48,176},{64,192},{80,208},{96,224},{112... | collective-permute-start | bytes 12296 | tf_op jit(solution)/shard_map/ppermute | solution.py:203
  89.0 1.5 %collective-permute-done.3 = f32[8,128]{1,0:T(8,128)S(1)} collective-permute-done((f32[8,128]{1,0:T(8,128)S(1)}, f32[8,128]{1,0:T(8,128)S(1)}, u32[]{:S(2)}, u32[]{:S(2)}) %collective-permute-start.3) | collective-permute-done | bytes 4128 | tf_op jit(solution)/shard_map/ppermute | solution.py:203
  90.6 0.5 slice.3
  91.8 0.1 convert_bitcast_fusion
  91.9 1.1 %copy.15 = f32[4,16,16,256]{3,2,1,0:T(8,128)} copy(f32[4,16,16,256]{3,2,0,1:T(8,128)S(1)} %convert_bitcast_fusion) | data formatting | bytes 2097152 | tf_op jit(solution)/shard_map/convert_element_type | solution.py:272
  (19 shorter events, 0.0 us)
Async XLA Ops:
  2.5 7.2 %copy-start.6 = (s32[16,6]{0,1:T(8,128)S(1)}, s32[16,6]{0,1:T(8,128)}, u32[]{:S(2)}) copy-start(s32[16,6]{0,1:T(8,128)} %param.11) | copy-start | bytes 1156
  2.5 18.7 %all-to-all-start = ((bf16[16,64,256]{2,1,0:T(8,128)(2,1)}), bf16[16,64,256]{2,1,0:T(8,128)(2,1)S(1)}, u32[]{:S(2)}, u32[]{:S(2)}) async-start(bf16[16,64,256]{2,1,0:T(8,128)(2,1)} %bitcast.2), calls=%async_computation | async-start | bytes 1048576 | tf_op jit(solution)/shard_map/all_to_all | solution.py:219
  21.2 0.8 copy-start.5
  24.0 16.8 %copy-start = (bf16[1,128,1024]{2,1,0:T(8,128)(2,1)S(1)}, bf16[1,128,1024]{2,1,0:T(8,128)(2,1)}, u32[]{:S(2)}) copy-start(bf16[1,128,1024]{2,1,0:T(8,128)(2,1)} %param.7) | copy-start | bytes 786436
  24.0 16.8 %copy-start.1 = (bf16[1,128,1024]{2,1,0:T(8,128)(2,1)S(1)}, bf16[1,128,1024]{2,1,0:T(8,128)(2,1)}, u32[]{:S(2)}) copy-start(bf16[1,128,1024]{2,1,0:T(8,128)(2,1)} %param.8) | copy-start | bytes 786436
  24.0 16.8 %copy-start.2 = (s32[16,6]{1,0:T(8,128)S(1)}, s32[16,6]{1,0:T(8,128)}, u32[]{:S(2)}) copy-start(s32[16,6]{1,0:T(8,128)} %copy.13.docs) | copy-start | bytes 1156
  24.0 16.8 %all-to-all-start.1 = ((bf16[16,96,256]{2,1,0:T(8,128)(2,1)}), bf16[16,96,256]{2,1,0:T(8,128)(2,1)S(1)}, u32[]{:S(2)}, u32[]{:S(2)}) async-start(bf16[16,96,256]{2,1,0:T(8,128)(2,1)} %select_cited.1), calls=%async_computation.1 | async-start | bytes 1572864 | tf_op jit(solution)/shard_map/all_to_all | solution.py:227
  27.8 13.1 %copy-start.4 = (s32[1024]{0:T(1024)S(1)}, s32[1024]{0:T(1024)}, u32[]{:S(2)}) copy-start(s32[1024]{0:T(1024)} %tiles.1) | copy-start | bytes 12292
  40.9 0.7 copy-start.3
  65.5 3.9 %copy-start.7 = (f32[8,128]{1,0:T(8,128)S(1)}, f32[8,128]{1,0:T(8,128)}, u32[]{:S(2)}) copy-start(f32[8,128]{1,0:T(8,128)} %get-tuple-element.13) | copy-start | bytes 12292
  65.5 26.3 %all-to-all-start.3 = ((bf16[16,64,256]{2,1,0:T(8,128)(2,1)}), bf16[16,64,256]{2,1,0:T(8,128)(2,1)S(1)}, u32[]{:S(2)}, u32[]{:S(2)}) async-start(bf16[16,64,256]{2,1,0:T(8,128)(2,1)} %get-tuple-element.12), calls=%async_computation.3 | async-start | bytes 1048576 | tf_op jit(solution)/shard_map/all_to_all | solution.py:267
  69.3 1.3 %collective-permute-start = (f32[8,128]{1,0:T(8,128)S(1)}, f32[8,128]{1,0:T(8,128)S(1)}, u32[]{:S(2)}, u32[]{:S(2)}) collective-permute-start(f32[8,128]{1,0:T(8,128)S(1)} %copy-done.7), channel_id=1, source_target_pairs={{0,16},{16,0},{32,48},{48,32},{64,80},{80,64},{96,112},{112,96},{1... | collective-permute-start | bytes 12296 | tf_op jit(solution)/shard_map/ppermute | solution.py:203
  70.6 5.8 %collective-permute-start.1 = (f32[8,128]{1,0:T(8,128)S(1)}, f32[8,128]{1,0:T(8,128)S(1)}, u32[]{:S(2)}, u32[]{:S(2)}) collective-permute-start(f32[8,128]{1,0:T(8,128)S(1)} %add.12), channel_id=1, source_target_pairs={{0,32},{16,48},{32,0},{48,16},{64,96},{80,112},{96,64},{112,80},{1... | collective-permute-start | bytes 12296 | tf_op jit(solution)/shard_map/ppermute | solution.py:203
  76.4 4.5 %collective-permute-start.2 = (f32[8,128]{1,0:T(8,128)S(1)}, f32[8,128]{1,0:T(8,128)S(1)}, u32[]{:S(2)}, u32[]{:S(2)}) collective-permute-start(f32[8,128]{1,0:T(8,128)S(1)} %add.13), channel_id=1, source_target_pairs={{0,64},{16,80},{32,96},{48,112},{64,0},{80,16},{96,32},{112,48},{1... | collective-permute-start | bytes 12296 | tf_op jit(solution)/shard_map/ppermute | solution.py:203
  80.9 9.7 %collective-permute-start.3 = (f32[8,128]{1,0:T(8,128)S(1)}, f32[8,128]{1,0:T(8,128)S(1)}, u32[]{:S(2)}, u32[]{:S(2)}) collective-permute-start(f32[8,128]{1,0:T(8,128)S(1)} %add.14), channel_id=1, source_target_pairs={{0,128},{16,144},{32,160},{48,176},{64,192},{80,208},{96,224},{112... | collective-permute-start | bytes 12296 | tf_op jit(solution)/shard_map/ppermute | solution.py:203

commit v2 on v1

v2 whole, which is shorter than its diff:
```python
import functools

import jax
import jax.numpy as jnp
from jax import lax
from jax.experimental import pallas as pl
from jax.experimental.pallas import tpu as pltpu
from jax.sharding import PartitionSpec as P

TILES = 4
CHUNK = 16
KEY_BLOCK = 256
ROW_BLOCK = 256
F32 = jnp.float32
BF16 = jnp.bfloat16

SMEM = functools.partial(pl.BlockSpec, memory_space=pltpu.SMEM)
VMEM = functools.partial(pl.BlockSpec, memory_space=pltpu.VMEM)


def contract(a, b, dim_a, dim_b):
    return lax.dot_general(a, b, (((dim_a,), (dim_b,)), ((), ())), preferred_element_type=F32)


def slot_place(docs, counts, group, slot, group_img, img_dev):
    live = slot < counts[group]
    local = jnp.where(live, docs[slot, group] - group * group_img, 0)
    return live, lax.div(local, img_dev), lax.rem(local, img_dev)


def pack_kernel(image_ref, out_ref, sems):
    copies = [
        pltpu.make_async_copy(
            image_ref.at[img], out_ref.at[:, img * CHUNK : (img + 1) * CHUNK, :], sems.at[img]
        )
        for img in range(image_ref.shape[0])
    ]
    for copy in copies:
        copy.start()
    for copy in copies:
        copy.wait()


def select_kernel(docs, counts, chunks_ref, out_ref):
    group = lax.axis_index("dp")
    parts = chunks_ref.shape[0]
    img_dev = chunks_ref.shape[1] // CHUNK
    for slot in range(docs.shape[0]):
        _, owner, place = slot_place(docs, counts, group, slot, parts * img_dev, img_dev)
        rows = pl.ds(pl.multiple_of(place * CHUNK, CHUNK), CHUNK)
        chunk = chunks_ref[owner, rows, :]
        for part in range(parts):
            out_ref[part, slot * CHUNK : (slot + 1) * CHUNK, :] = chunk


def prepare_kernel(gate, query_ref, cot_ref, query_rows, dattn_rows, cot_t):
    tok = query_ref.shape[0]
    head_dim = query_rows.shape[1]
    tanh_gate = jnp.tanh(jnp.full((1, head_dim), gate[0], F32))
    for head in range(query_ref.shape[1] // head_dim):
        cols = slice(head * head_dim, (head + 1) * head_dim)
        at = slice(head * tok, (head + 1) * tok)
        query_rows[at, :] = query_ref[:, cols]
        cot = cot_ref[:, cols].astype(F32)
        dattn_rows[at, :] = (tanh_gate * cot).astype(BF16)
        cot_t[:, at] = cot.T


def finish_kernel(gate, attn_t, dquery_t, gated_ref, dquery_ref):
    tok = gated_ref.shape[0]
    head_dim = attn_t.shape[0]
    tanh_gate = jnp.tanh(jnp.full((1, head_dim), gate[0], F32))
    for head in range(gated_ref.shape[1] // head_dim):
        cols = slice(head * head_dim, (head + 1) * head_dim)
        at = slice(head * tok, (head + 1) * tok)
        gated_ref[:, cols] = (attn_t[:, at].T * tanh_gate).astype(BF16)
        dquery_ref[:, cols] = (dquery_t[:, at].T * head_dim ** (-0.5)).astype(BF16)


def attention_kernel(
    docs, counts, tiles, gate,
    kv_ref, query_rows, dattn_rows, cot_t,
    attn_t, dquery_t, dkv_ref, gate_ref,
    kv_rows, exp_t, prob_t, dscore_t, dkv_rows, top_part, total_part,
):
    group = lax.axis_index("dp")
    parts = kv_ref.shape[0]
    slots = docs.shape[0]
    rows, head_dim = query_rows.shape
    scale = head_dim ** (-0.5)
    img_tok = parts * CHUNK
    tile_tok = img_tok // TILES
    col_blocks = [slice(c, c + ROW_BLOCK) for c in range(0, rows, ROW_BLOCK)]

    kv_rows[...] = jnp.zeros_like(kv_rows)
    starts, live_tiles = [], []
    start = jnp.int32(0)
    for slot in range(slots):
        live = slot < counts[group]
        count = jnp.where(live, tiles[jnp.where(live, docs[slot, group], 0)], 0)
        starts.append(start)
        live_tiles.append(count)
        for part in range(parts):
            at = pl.ds(pl.multiple_of(start * tile_tok + part * CHUNK, CHUNK), CHUNK)
            kv_rows[at, :] = kv_ref[part, slot * CHUNK : (slot + 1) * CHUNK, :]
        start = start + count
    live_keys = start * tile_tok
    blocks = lax.div(live_keys + (KEY_BLOCK - 1), KEY_BLOCK)

    top_part[...] = jnp.full_like(top_part, -jnp.inf)
    total_part[...] = jnp.zeros_like(total_part)
    attn_t[...] = jnp.zeros_like(attn_t)
    dquery_t[...] = jnp.zeros_like(dquery_t)

    def block_rows(block):
        return pl.ds(pl.multiple_of(block * KEY_BLOCK, KEY_BLOCK), KEY_BLOCK)

    def fold(x, op):
        return op(x.reshape(KEY_BLOCK // 8, 8, x.shape[1]), axis=0)

    def score_pass(block, carry):
        at = block_rows(block)
        keys = kv_rows[at, :head_dim]
        key_index = lax.broadcasted_iota(jnp.int32, (KEY_BLOCK, ROW_BLOCK), 0)
        live = key_index < live_keys - block * KEY_BLOCK
        for cols in col_blocks:
            scores = contract(keys, query_rows[cols, :], 1, 1) * scale
            scores = jnp.where(live, scores, -jnp.inf)
            exp_t[at, cols] = scores
            top_part[:, cols] = jnp.maximum(top_part[:, cols], fold(scores, jnp.max))
        return carry

    lax.fori_loop(0, blocks, score_pass, 0)
    top = jnp.max(top_part[...], axis=0, keepdims=True)

    def exp_pass(block, carry):
        at = block_rows(block)
        for cols in col_blocks:
            raised = jnp.exp(exp_t[at, cols] - top[:, cols])
            exp_t[at, cols] = raised
            total_part[:, cols] += fold(raised, jnp.sum)
        return carry

    lax.fori_loop(0, blocks, exp_pass, 0)
    inverse = 1.0 / jnp.sum(total_part[...], axis=0, keepdims=True)

    def attn_pass(block, carry):
        at = block_rows(block)
        values = kv_rows[at, head_dim:]
        for cols in col_blocks:
            probs_low = (exp_t[at, cols] * inverse[:, cols]).astype(BF16)
            prob_t[at, cols] = probs_low
            attn_t[:, cols] += contract(values, probs_low, 0, 0)
        return carry

    lax.fori_loop(0, blocks, attn_pass, 0)
    gate_rows = jnp.sum(cot_t[...] * attn_t[...], axis=0, keepdims=True)
    delta = jnp.tanh(jnp.full((1, rows), gate[0], F32)) * gate_rows
    gate_ref[...] = jnp.broadcast_to(jnp.sum(gate_rows, axis=1, keepdims=True), gate_ref.shape)

    def grad_pass(block, carry):
        at = block_rows(block)
        keys, values = kv_rows[at, :head_dim], kv_rows[at, head_dim:]
        for cols in col_blocks:
            probs = exp_t[at, cols] * inverse[:, cols]
            dprob = contract(values, dattn_rows[cols, :], 1, 1)
            dscore = (probs * (dprob - delta[:, cols])).astype(BF16)
            dscore_t[:, cols] = dscore
            dquery_t[:, cols] += contract(keys, dscore, 0, 0)
        dkeys = contract(dscore_t[...], query_rows[...], 1, 0) * scale
        dvalues = contract(prob_t[at, :], dattn_rows[...], 1, 0)
        dkv_rows[at, :head_dim] = dkeys.astype(BF16)
        dkv_rows[at, head_dim:] = dvalues.astype(BF16)
        return carry

    lax.fori_loop(0, blocks, grad_pass, 0)

    for slot in range(slots):
        for part in range(parts):
            row = starts[slot] * tile_tok + part * CHUNK
            grads = dkv_rows[pl.ds(pl.multiple_of(row, CHUNK), CHUNK), :]
            live = part * CHUNK < live_tiles[slot] * tile_tok
            dkv_ref[part, slot * CHUNK : (slot + 1) * CHUNK, :] = jnp.where(
                live, grads, jnp.zeros_like(grads)
            )

def sum_kernel(docs, counts, partial_ref, gate_ref, out_ref):
    group = lax.axis_index("dp")
    parts = partial_ref.shape[0]
    half = out_ref.shape[2]
    sent = out_ref.shape[1] - CHUNK
    img_dev = sent // (2 * CHUNK)
    out_ref[:, :sent, :] = jnp.zeros((parts, sent, half), BF16)
    for slot in range(docs.shape[0]):
        at = slice(slot * CHUNK, (slot + 1) * CHUNK)
        total = partial_ref[0, at, :].astype(F32)
        for part in range(1, parts):
            total = total + partial_ref[part, at, :].astype(F32)
        live, owner, place = slot_place(docs, counts, group, slot, parts * img_dev, img_dev)
        rows = pl.multiple_of(place * CHUNK, CHUNK)

        @pl.when(live)
        def _():
            out_ref[owner, pl.ds(rows, CHUNK), :] = total[:, :half].astype(BF16)
            out_ref[owner, pl.ds(rows + sent // 2, CHUNK), :] = total[:, half:].astype(BF16)

    term = jnp.broadcast_to(gate_ref[0:1, :], (CHUNK, half))
    high = term.astype(BF16).astype(F32)
    middle = (term - high).astype(BF16).astype(F32)
    low = term - high - middle
    index = lax.broadcasted_iota(jnp.int32, term.shape, 0)
    split = jnp.where(index == 0, high, jnp.where(index == 1, middle, low)).astype(BF16)
    for part in range(parts):
        out_ref[part, sent:, :] = split


def unpack_kernel(norm_factor, gate, owned_ref, grads_ref, gate_ref):
    parts = owned_ref.shape[0]
    img_dev = grads_ref.shape[0]
    half = owned_ref.shape[2]
    sent = owned_ref.shape[1] - CHUNK
    for part in range(parts):
        to = slice(part * CHUNK, (part + 1) * CHUNK)
        for img in range(img_dev):
            row = img * CHUNK
            grads_ref[img, to, :half] = owned_ref[part, row : row + CHUNK, :].astype(F32)
            row = row + sent // 2
            grads_ref[img, to, half:] = owned_ref[part, row : row + CHUNK, :].astype(F32)
    total = owned_ref[0, sent:, :].astype(F32)
    for part in range(1, parts):
        total = total + owned_ref[part, sent:, :].astype(F32)
    total = total[0:1, :] + total[1:2, :] + total[2:3, :]
    tanh_gate = jnp.tanh(jnp.full(total.shape, gate[0], F32))
    gate_ref[...] = jnp.broadcast_to(
        (1.0 - tanh_gate * tanh_gate) * total * norm_factor, gate_ref.shape
    )


def sum_over(x, axis):
    size = lax.axis_size(axis)

    def moved(step):
        return lax.ppermute(x, axis, [(i, i ^ step) for i in range(size)])

    step = 1
    while step < size:
        if 2 * step < size:
            x = (x + moved(step)) + (moved(2 * step) + moved(3 * step))
            step *= 4
        else:
            x = x + moved(step)
            step *= 2
    return x


def small(**kwargs):
    return pltpu.CompilerParams(vmem_limit_bytes=6 * 1024 * 1024, **kwargs)


def per_device(queries, grad_out, image_kv, image_tiles, doc_images, doc_counts, gate):
    _, tok, width = queries.shape
    img_dev, img_tok, kv_width = image_kv.shape
    head_dim = kv_width // 2
    rows = tok * (width // head_dim)
    slots = doc_images.shape[1]
    parts = lax.axis_size("seq")
    keys = slots * img_tok
    sent = slots * CHUNK
    docs = doc_images.T

    chunks = pl.pallas_call(
        pack_kernel,
        out_shape=jax.ShapeDtypeStruct((parts, img_dev * CHUNK, kv_width), BF16),
        in_specs=[pl.BlockSpec(memory_space=pl.ANY)],
        out_specs=VMEM(),
        scratch_shapes=[pltpu.SemaphoreType.DMA((img_dev,))],
        compiler_params=small(),
        name="pack_chunks",
    )(image_kv.reshape(img_dev, parts, CHUNK, kv_width))
    chunks = lax.all_to_all(chunks, "seq", 0, 0)
    cited = pl.pallas_call(
        select_kernel,
        out_shape=jax.ShapeDtypeStruct((parts, sent, kv_width), BF16),
        in_specs=[SMEM(), SMEM(), VMEM()],
        out_specs=VMEM(),
        compiler_params=small(),
        name="select_cited",
    )(docs, doc_counts, chunks)
    kv_cited = lax.all_to_all(cited, "seq", 0, 0)

    query_rows, dattn_rows, cot_t = pl.pallas_call(
        prepare_kernel,
        out_shape=(
            jax.ShapeDtypeStruct((rows, head_dim), BF16),
            jax.ShapeDtypeStruct((rows, head_dim), BF16),
            jax.ShapeDtypeStruct((head_dim, rows), F32),
        ),
        in_specs=[SMEM(), VMEM(), VMEM()],
        out_specs=(VMEM(), VMEM(), VMEM()),
        compiler_params=small(),
        name="prepare_rows",
    )(gate, queries[0], grad_out[0])
    attn_t, dquery_t, partial, gate_sum = pl.pallas_call(
        attention_kernel,
        out_shape=(
            jax.ShapeDtypeStruct((head_dim, rows), F32),
            jax.ShapeDtypeStruct((head_dim, rows), F32),
            jax.ShapeDtypeStruct((parts, sent, kv_width), BF16),
            jax.ShapeDtypeStruct((8, 128), F32),
        ),
        in_specs=[SMEM()] * 4 + [VMEM()] * 4,
        out_specs=(VMEM(), VMEM(), VMEM(), VMEM()),
        scratch_shapes=[
            pltpu.VMEM((keys, kv_width), BF16),
            pltpu.VMEM((keys, rows), F32),
            pltpu.VMEM((keys, rows), BF16),
            pltpu.VMEM((KEY_BLOCK, rows), BF16),
            pltpu.VMEM((keys, kv_width), BF16),
            pltpu.VMEM((8, rows), F32),
            pltpu.VMEM((8, rows), F32),
        ],
        compiler_params=pltpu.CompilerParams(vmem_limit_bytes=40 * 1024 * 1024),
        name="attention",
    )(docs, doc_counts, image_tiles, gate, kv_cited, query_rows, dattn_rows, cot_t)

    partial = lax.all_to_all(partial, "seq", 0, 0)
    gated, dquery = pl.pallas_call(
        finish_kernel,
        out_shape=(
            jax.ShapeDtypeStruct((tok, width), BF16),
            jax.ShapeDtypeStruct((tok, width), BF16),
        ),
        in_specs=[SMEM(), VMEM(), VMEM()],
        out_specs=(VMEM(), VMEM()),
        compiler_params=small(),
        name="finish_rows",
    )(gate, attn_t, dquery_t)
    gate_sum = sum_over(gate_sum, "dp")
    summed = pl.pallas_call(
        sum_kernel,
        out_shape=jax.ShapeDtypeStruct((parts, 2 * img_dev * CHUNK + CHUNK, head_dim), BF16),
        in_specs=[SMEM(), SMEM(), VMEM(), VMEM()],
        out_specs=VMEM(),
        compiler_params=small(),
        name="sum_partials",
    )(docs, doc_counts, partial, gate_sum)
    owned = lax.all_to_all(summed, "seq", 0, 0)
    norm_factor = float(lax.axis_size("dp") * tok * parts * width) ** (-0.5)
    grad_image_kv, grad_gate = pl.pallas_call(
        functools.partial(unpack_kernel, norm_factor),
        out_shape=(
            jax.ShapeDtypeStruct((img_dev, img_tok, kv_width), F32),
            jax.ShapeDtypeStruct((8, 128), F32),
        ),
        in_specs=[SMEM(), VMEM()],
        out_specs=(VMEM(), VMEM()),
        compiler_params=small(),
        name="unpack_grads",
    )(gate, owned)
    return gated[None], dquery[None], grad_image_kv, grad_gate[0, :1]


def solution(mesh):
    return jax.shard_map(
        per_device,
        mesh=mesh,
        in_specs=(
            P("dp", "seq", None),
            P("dp", "seq", None),
            P(("dp", "seq"), None, None),
            P(),
            P(),
            P(),
            P(),
        ),
        out_specs=(P("dp", "seq", None), P("dp", "seq", None), P(("dp", "seq"), None, None), P()),
        check_vma=False,
    )
```

time: 95.4 us -> 89.8 us (0.941)
  local copies, waits for them, and re-layouts: 5.61 us -> 2.22 us
  blocking collectives: 15.4 us -> 18.3 us
  waiting for transfers between devices: 30.5 us -> 28.2 us
  between operations: 3.22 us -> 1.39 us
    all_to_all x1, waiting for transfers between devices: 10.8 us -> 0.01 us  [per_device(): partial = lax.all_to_all(partial, 'seq', 0, 0)]
    all_to_all x1, waiting for transfers between devices: 0.01 us -> 9.32 us  [per_device(): owned = lax.all_to_all(summed, 'seq', 0, 0)]
    all_to_all x1, starting transfers between devices: 7.17 us -> 3.62 us  [per_device(): partial = lax.all_to_all(partial, 'seq', 0, 0)]
    all_to_all x1, starting transfers between devices: 3.85 us -> 7.11 us  [per_device(): owned = lax.all_to_all(summed, 'seq', 0, 0)]
    all_to_all x1, blocking collectives: 15.4 us -> 18.3 us  [per_device(): chunks = lax.all_to_all(chunks, 'seq', 0, 0)]
    reshape x1 -> x0, local copies, waits for them, and re-layouts: 1.89 us -> none  [per_device(): image_kv.reshape(img_dev, parts, CHUNK, kv_width).transpose(1, 0, 2, 3)]
    convert_element_type x1 -> x0, local copies, waits for them, and re-layouts: 1.07 us -> none  [per_device(): grad_image_kv = owned.reshape(parts, img_dev, CHUNK, kv_width).transpose(...]
    ppermute x4 -> x6, waiting for transfers between devices: 7.33 us -> 6.63 us  [moved(): return lax.ppermute(x, axis, [(i, i ^ step) for i in range(size)])]
  transfers between devices with their start and end apart: 7 -> 9, of which waited for: 6 -> 4; matrix products, arithmetic and copies ran while one was open for 1% -> 0% of each run, Pallas kernels for 0% -> 1%
where the time goes in v2:
time: 89.8 us; the launch traced here: 88.5 us
  starting transfers between devices  28.7 us (32%)
  waiting for transfers between devices  28.2 us (31%)
  blocking collectives  18.3 us (20%)
  Pallas kernels  9.68 us (11%)
  local copies, waits for them, and re-layouts  2.22 us (2%)
  between operations  1.39 us (2%)
    all_to_all x1, blocking collectives, per_device(): chunks = lax.all_to_all(chunks, 'seq', 0, 0)  18.3 us
    ppermute x6, starting transfers between devices, moved(): return lax.ppermute(x, axis, [(i, i ^ step) for i in range(size)])  14.2 us
    all_to_all x1, waiting for transfers between devices, per_device(): kv_cited = lax.all_to_all(cited, 'seq', 0, 0)  12.2 us
    all_to_all x1, waiting for transfers between devices, per_device(): owned = lax.all_to_all(summed, 'seq', 0, 0)  9.32 us
    all_to_all x1, starting transfers between devices, per_device(): owned = lax.all_to_all(summed, 'seq', 0, 0)  7.11 us
    ppermute x6, waiting for transfers between devices, moved(): return lax.ppermute(x, axis, [(i, i ^ step) for i in range(size)])  6.63 us
    pallas_call x1, Pallas kernels, per_device(): pl.pallas_call(attention_kernel, out_shape=(jax.ShapeDtypeStruct((head_di...  4.09 us
    all_to_all x1, starting transfers between devices, per_device(): kv_cited = lax.all_to_all(cited, 'seq', 0, 0)  3.75 us
  transfers between devices with their start and end apart: 9, of which 4 were waited for; matrix products, arithmetic and copies ran while one was open for 0% of the time, Pallas kernels for 1%

profile of v2, /device:TPU:32, one launch (start us, length us, event | category | flops | bytes accessed | tf_op | source)
XLA Modules:
  0.0 88.5 jit_solution(11831666845317035529)
XLA Ops:
  0.6 1.0 %copy-done = bf16[4,256,256]{2,1,0:T(8,128)(2,1)S(1)} copy-done((bf16[4,256,256]{2,1,0:T(8,128)(2,1)S(1)}, bf16[4,256,256]{2,1,0:T(8,128)(2,1)}, u32[]{:S(2)}) %copy-start) | copy-done | bytes 524312
  1.7 0.1 pack_chunks.1
  1.8 18.3 %all_to_all.20.chunks_ref = bf16[16,64,256]{2,1,0:T(8,128)(2,1)S(1)} all-to-all(bf16[16,64,256]{2,1,0:T(8,128)(2,1)S(1)} %pack_chunks.1), channel_id=1, replica_groups=mesh['dp'=16,'seq'=16] {'seq'}, dimensions={0} | all-to-all | bytes 1048576 | tf_op jit(solution)/shard_map/all_to_all | solution.py:280
  20.1 0.7 copy-done.4
  20.8 1.6 %select_cited.1 = bf16[16,96,256]{2,1,0:T(8,128)(2,1)} custom-call(s32[6,16]{1,0:T(8,128)S(1)} %bitcast.10, s32[16]{0:T(128)S(1)} %copy-done.4, bf16[16,64,256]{2,1,0:T(8,128)(2,1)S(1)} %all_to_all.20.chunks_ref), custom_call_target="tpu_custom_call" | custom-call | tf_op jit(solution)/shard_map/select_cited/pallas_call | solution.py:281
  22.4 3.7 %all-to-all-start.1 = ((bf16[16,96,256]{2,1,0:T(8,128)(2,1)}), bf16[16,96,256]{2,1,0:T(8,128)(2,1)S(1)}, u32[]{:S(2)}, u32[]{:S(2)}) async-start(bf16[16,96,256]{2,1,0:T(8,128)(2,1)} %select_cited.1), calls=%async_computation.1 | async-start | bytes 1572864 | tf_op jit(solution)/shard_map/all_to_all | solution.py:289
  26.8 0.1 prepare_rows.1
  26.9 12.2 %all-to-all-done.1.kv_ref = bf16[16,96,256]{2,1,0:T(8,128)(2,1)S(1)} async-done(((bf16[16,96,256]{2,1,0:T(8,128)(2,1)}), bf16[16,96,256]{2,1,0:T(8,128)(2,1)S(1)}, u32[]{:S(2)}, u32[]{:S(2)}) %all-to-all-start.1) | async-done | bytes 786464 | tf_op jit(solution)/shard_map/all_to_all | solution.py:289
  39.2 4.1 %attention.1 = (f32[128,1024]{1,0:T(8,128)S(1)}, f32[128,1024]{1,0:T(8,128)S(1)}, bf16[16,96,256]{2,1,0:T(8,128)(2,1)}, f32[8,128]{1,0:T(8,128)S(1)}) custom-call(s32[6,16]{1,0:T(8,128)S(1)} %bitcast.11, s32[16]{0:T(128)S(1)} %copy-done.4, s32[1024]{0:T(1024)S(1)} %copy-done.5, f32[1]{0:T(128)S(6)} %copy.11.gate, ...), custom_call_target="tpu_custom_call" | custom-call | tf_op jit(solution)/shard_map/attention/pallas_call | solution.py:303
  43.3 3.6 %all-to-all-start.2 = ((bf16[16,96,256]{2,1,0:T(8,128)(2,1)}), bf16[16,96,256]{2,1,0:T(8,128)(2,1)S(1)}, u32[]{:S(2)}, u32[]{:S(2)}) async-start(bf16[16,96,256]{2,1,0:T(8,128)(2,1)} %get-tuple-element.22), calls=%async_computation.2 | async-start | bytes 1572864 | tf_op jit(solution)/shard_map/all_to_all | solution.py:326
  46.9 0.1 collective-permute-start.2
  47.0 6.3 %collective-permute-start.1 = (f32[8,128]{1,0:T(8,128)S(1)}, f32[8,128]{1,0:T(8,128)S(1)}, u32[]{:S(2)}, u32[]{:S(2)}) collective-permute-start(f32[8,128]{1,0:T(8,128)S(1)} %get-tuple-element.23), channel_id=1, source_target_pairs={{0,32},{16,48},{32,0},{48,16},{64,96},{80,112},{96,64},{112,80},{1... | collective-permute-start | bytes 12296 | tf_op jit(solution)/shard_map/ppermute | solution.py:243
  53.3 0.0 collective-permute-start
  53.3 1.6 %collective-permute-done.1 = f32[8,128]{1,0:T(8,128)S(1)} collective-permute-done((f32[8,128]{1,0:T(8,128)S(1)}, f32[8,128]{1,0:T(8,128)S(1)}, u32[]{:S(2)}, u32[]{:S(2)}) %collective-permute-start.1) | collective-permute-done | bytes 4128 | tf_op jit(solution)/shard_map/ppermute | solution.py:243
  54.9 5.4 %collective-permute-start.5 = (f32[8,128]{1,0:T(8,128)S(1)}, f32[8,128]{1,0:T(8,128)S(1)}, u32[]{:S(2)}, u32[]{:S(2)}) collective-permute-start(f32[8,128]{1,0:T(8,128)S(1)} %add_add_fusion.1), channel_id=1, source_target_pairs={{0,192},{16,208},{32,224},{48,240},{64,128},{80,144},{96,160},{112... | collective-permute-start | bytes 12296 | tf_op jit(solution)/shard_map/ppermute | solution.py:243
  60.2 1.0 %collective-permute-start.4 = (f32[8,128]{1,0:T(8,128)S(1)}, f32[8,128]{1,0:T(8,128)S(1)}, u32[]{:S(2)}, u32[]{:S(2)}) collective-permute-start(f32[8,128]{1,0:T(8,128)S(1)} %add_add_fusion.1), channel_id=1, source_target_pairs={{0,128},{16,144},{32,160},{48,176},{64,192},{80,208},{96,224},{112... | collective-permute-start | bytes 12296 | tf_op jit(solution)/shard_map/ppermute | solution.py:243
  61.3 1.5 %collective-permute-start.3 = (f32[8,128]{1,0:T(8,128)S(1)}, f32[8,128]{1,0:T(8,128)S(1)}, u32[]{:S(2)}, u32[]{:S(2)}) collective-permute-start(f32[8,128]{1,0:T(8,128)S(1)} %add_add_fusion.1), channel_id=1, source_target_pairs={{0,64},{16,80},{32,96},{48,112},{64,0},{80,16},{96,32},{112,48},{1... | collective-permute-start | bytes 12296 | tf_op jit(solution)/shard_map/ppermute | solution.py:243
  62.7 5.0 %collective-permute-done.4 = f32[8,128]{1,0:T(8,128)S(1)} collective-permute-done((f32[8,128]{1,0:T(8,128)S(1)}, f32[8,128]{1,0:T(8,128)S(1)}, u32[]{:S(2)}, u32[]{:S(2)}) %collective-permute-start.4) | collective-permute-done | bytes 4128 | tf_op jit(solution)/shard_map/ppermute | solution.py:243
  67.8 1.6 %sum_partials.1 = bf16[16,144,128]{2,1,0:T(8,128)(2,1)} custom-call(s32[6,16]{1,0:T(8,128)S(1)} %bitcast.12, s32[16]{0:T(128)S(1)} %copy-done.4, bf16[16,96,256]{2,1,0:T(8,128)(2,1)S(1)} %all-to-all-done.2.partial_ref, f32[8,128]{1,0:T(8,128)S(1)} %add_add_fusion.gate_ref), custom_call_target="tpu_custom_call" | custom-call | tf_op jit(solution)/shard_map/sum_partials/pallas_call | solution.py:339
  69.4 7.1 %all-to-all-start.3 = ((bf16[16,144,128]{2,1,0:T(8,128)(2,1)}), bf16[16,144,128]{2,1,0:T(8,128)(2,1)S(1)}, u32[]{:S(2)}, u32[]{:S(2)}) async-start(bf16[16,144,128]{2,1,0:T(8,128)(2,1)} %sum_partials.1), calls=%async_computation.3 | async-start | bytes 1179648 | tf_op jit(solution)/shard_map/all_to_all | solution.py:347
  76.5 1.1 %finish_rows.1 = (bf16[128,1024]{1,0:T(8,128)(2,1)}, bf16[128,1024]{1,0:T(8,128)(2,1)}) custom-call(f32[1]{0:T(128)S(6)} %copy.11.gate, f32[128,1024]{1,0:T(8,128)S(1)} %get-tuple-element.18.attn_t, f32[128,1024]{1,0:T(8,128)S(1)} %get-tuple-element.19.dquery_t), custom_call_target="tpu_custom_call" | custom-call | tf_op jit(solution)/shard_map/finish_rows/pallas_call | solution.py:327
  77.6 9.3 %all-to-all-done.3.owned_ref = bf16[16,144,128]{2,1,0:T(8,128)(2,1)S(1)} async-done(((bf16[16,144,128]{2,1,0:T(8,128)(2,1)}), bf16[16,144,128]{2,1,0:T(8,128)(2,1)S(1)}, u32[]{:S(2)}, u32[]{:S(2)}) %all-to-all-start.3) | async-done | bytes 589856 | tf_op jit(solution)/shard_map/all_to_all | solution.py:347
  86.9 1.0 %unpack_grads.1 = (f32[4,256,256]{2,1,0:T(8,128)}, f32[8,128]{1,0:T(8,128)S(1)}) custom-call(f32[1]{0:T(128)S(6)} %copy.11.gate, bf16[16,144,128]{2,1,0:T(8,128)(2,1)S(1)} %all-to-all-done.3.owned_ref), custom_call_target="tpu_custom_call" | custom-call | tf_op jit(solution)/shard_map/unpack_grads/pallas_call | solution.py:349
  88.0 0.5 slice.3
  (17 shorter events, 0.0 us)
Async XLA Ops:
  0.6 1.0 %copy-start = (bf16[4,256,256]{2,1,0:T(8,128)(2,1)S(1)}, bf16[4,256,256]{2,1,0:T(8,128)(2,1)}, u32[]{:S(2)}) copy-start(bf16[4,256,256]{2,1,0:T(8,128)(2,1)} %param.9) | copy-start | bytes 1572868
  1.8 18.3 %copy-start.3 = (s32[16,6]{0,1:T(8,128)S(1)}, s32[16,6]{0,1:T(8,128)}, u32[]{:S(2)}) copy-start(s32[16,6]{0,1:T(8,128)} %param.11) | copy-start | bytes 1156
  20.1 0.7 copy-start.4
  22.4 4.4 %copy-start.1 = (bf16[1,128,1024]{2,1,0:T(8,128)(2,1)S(1)}, bf16[1,128,1024]{2,1,0:T(8,128)(2,1)}, u32[]{:S(2)}) copy-start(bf16[1,128,1024]{2,1,0:T(8,128)(2,1)} %param.7) | copy-start | bytes 786436
  22.4 4.4 %copy-start.2 = (bf16[1,128,1024]{2,1,0:T(8,128)(2,1)S(1)}, bf16[1,128,1024]{2,1,0:T(8,128)(2,1)}, u32[]{:S(2)}) copy-start(bf16[1,128,1024]{2,1,0:T(8,128)(2,1)} %param.8) | copy-start | bytes 786436
  22.4 16.8 %all-to-all-start.1 = ((bf16[16,96,256]{2,1,0:T(8,128)(2,1)}), bf16[16,96,256]{2,1,0:T(8,128)(2,1)S(1)}, u32[]{:S(2)}, u32[]{:S(2)}) async-start(bf16[16,96,256]{2,1,0:T(8,128)(2,1)} %select_cited.1), calls=%async_computation.1 | async-start | bytes 1572864 | tf_op jit(solution)/shard_map/all_to_all | solution.py:289
  26.9 12.3 %copy-start.5 = (s32[1024]{0:T(1024)S(1)}, s32[1024]{0:T(1024)}, u32[]{:S(2)}) copy-start(s32[1024]{0:T(1024)} %tiles.1) | copy-start | bytes 12292
  43.3 24.5 %all-to-all-start.2 = ((bf16[16,96,256]{2,1,0:T(8,128)(2,1)}), bf16[16,96,256]{2,1,0:T(8,128)(2,1)S(1)}, u32[]{:S(2)}, u32[]{:S(2)}) async-start(bf16[16,96,256]{2,1,0:T(8,128)(2,1)} %get-tuple-element.22), calls=%async_computation.2 | async-start | bytes 1572864 | tf_op jit(solution)/shard_map/all_to_all | solution.py:326
  46.9 6.4 %collective-permute-start.2 = (f32[8,128]{1,0:T(8,128)S(1)}, f32[8,128]{1,0:T(8,128)S(1)}, u32[]{:S(2)}, u32[]{:S(2)}) collective-permute-start(f32[8,128]{1,0:T(8,128)S(1)} %get-tuple-element.23), channel_id=1, source_target_pairs={{0,48},{16,32},{32,16},{48,0},{64,112},{80,96},{96,80},{112,64},{1... | collective-permute-start | bytes 12296 | tf_op jit(solution)/shard_map/ppermute | solution.py:243
  47.0 7.9 %collective-permute-start.1 = (f32[8,128]{1,0:T(8,128)S(1)}, f32[8,128]{1,0:T(8,128)S(1)}, u32[]{:S(2)}, u32[]{:S(2)}) collective-permute-start(f32[8,128]{1,0:T(8,128)S(1)} %get-tuple-element.23), channel_id=1, source_target_pairs={{0,32},{16,48},{32,0},{48,16},{64,96},{80,112},{96,64},{112,80},{1... | collective-permute-start | bytes 12296 | tf_op jit(solution)/shard_map/ppermute | solution.py:243
  53.3 1.6 %collective-permute-start = (f32[8,128]{1,0:T(8,128)S(1)}, f32[8,128]{1,0:T(8,128)S(1)}, u32[]{:S(2)}, u32[]{:S(2)}) collective-permute-start(f32[8,128]{1,0:T(8,128)S(1)} %get-tuple-element.23), channel_id=1, source_target_pairs={{0,16},{16,0},{32,48},{48,32},{64,80},{80,64},{96,112},{112,96},{1... | collective-permute-start | bytes 12296 | tf_op jit(solution)/shard_map/ppermute | solution.py:243
  54.9 7.8 %collective-permute-start.5 = (f32[8,128]{1,0:T(8,128)S(1)}, f32[8,128]{1,0:T(8,128)S(1)}, u32[]{:S(2)}, u32[]{:S(2)}) collective-permute-start(f32[8,128]{1,0:T(8,128)S(1)} %add_add_fusion.1), channel_id=1, source_target_pairs={{0,192},{16,208},{32,224},{48,240},{64,128},{80,144},{96,160},{112... | collective-permute-start | bytes 12296 | tf_op jit(solution)/shard_map/ppermute | solution.py:243
  60.2 7.5 %collective-permute-start.4 = (f32[8,128]{1,0:T(8,128)S(1)}, f32[8,128]{1,0:T(8,128)S(1)}, u32[]{:S(2)}, u32[]{:S(2)}) collective-permute-start(f32[8,128]{1,0:T(8,128)S(1)} %add_add_fusion.1), channel_id=1, source_target_pairs={{0,128},{16,144},{32,160},{48,176},{64,192},{80,208},{96,224},{112... | collective-permute-start | bytes 12296 | tf_op jit(solution)/shard_map/ppermute | solution.py:243
  61.3 6.5 %collective-permute-start.3 = (f32[8,128]{1,0:T(8,128)S(1)}, f32[8,128]{1,0:T(8,128)S(1)}, u32[]{:S(2)}, u32[]{:S(2)}) collective-permute-start(f32[8,128]{1,0:T(8,128)S(1)} %add_add_fusion.1), channel_id=1, source_target_pairs={{0,64},{16,80},{32,96},{48,112},{64,0},{80,16},{96,32},{112,48},{1... | collective-permute-start | bytes 12296 | tf_op jit(solution)/shard_map/ppermute | solution.py:243
  69.4 17.6 %all-to-all-start.3 = ((bf16[16,144,128]{2,1,0:T(8,128)(2,1)}), bf16[16,144,128]{2,1,0:T(8,128)(2,1)S(1)}, u32[]{:S(2)}, u32[]{:S(2)}) async-start(bf16[16,144,128]{2,1,0:T(8,128)(2,1)} %sum_partials.1), calls=%async_computation.3 | async-start | bytes 1179648 | tf_op jit(solution)/shard_map/all_to_all | solution.py:347

commit v3 on v2

v3 whole, which is shorter than its diff:
```python
import functools

import jax
import jax.numpy as jnp
from jax import lax
from jax.experimental import pallas as pl
from jax.experimental.pallas import tpu as pltpu
from jax.sharding import PartitionSpec as P

TILES = 4
CHUNK = 16
KEY_BLOCK = 256
ROW_BLOCK = 256
F32 = jnp.float32
BF16 = jnp.bfloat16

SMEM = functools.partial(pl.BlockSpec, memory_space=pltpu.SMEM)
VMEM = functools.partial(pl.BlockSpec, memory_space=pltpu.VMEM)


def contract(a, b, dim_a, dim_b):
    return lax.dot_general(a, b, (((dim_a,), (dim_b,)), ((), ())), preferred_element_type=F32)


def place_in_group():
    side = lax.axis_size("seq") // TILES
    me = lax.axis_index("seq")
    return lax.axis_index("dp"), lax.div(me, side), lax.rem(me, side)


def slot_place(docs, counts, slot, img_dev):
    group, column, row = place_in_group()
    devices = lax.axis_size("seq")
    side = devices // TILES
    live = slot < counts[group]
    local = jnp.where(live, docs[slot, group] - group * devices * img_dev, 0)
    owner = lax.div(local, img_dev)
    column_step = lax.bitwise_xor(lax.div(owner, side), column)
    row_step = lax.bitwise_xor(lax.rem(owner, side), row)
    return live, column_step, row_step, lax.rem(local, img_dev)


def pick(step, values):
    chosen = values[0]
    for index in range(1, len(values)):
        chosen = jnp.where(step == index, values[index], chosen)
    return chosen


def pack_kernel(image_ref, *refs):
    out_refs, sems = refs[:-1], refs[-1]
    _, column, _ = place_in_group()
    img_dev, _, tile_tok, _ = image_ref.shape
    copies = []
    for step, out_ref in enumerate(out_refs):
        tile = lax.bitwise_xor(column, step)
        for img in range(img_dev):
            copies.append(
                pltpu.make_async_copy(
                    image_ref.at[img, tile],
                    out_ref.at[img * tile_tok : (img + 1) * tile_tok, :],
                    sems.at[step, img],
                )
            )
    for copy in copies:
        copy.start()
    for copy in copies:
        copy.wait()


def select_kernel(img_dev, docs, counts, *refs):
    in_refs, out_ref = refs[:-1], refs[-1]
    tile_tok = in_refs[0].shape[0] // img_dev
    for slot in range(docs.shape[0]):
        _, column_step, _, place = slot_place(docs, counts, slot, img_dev)
        at = pl.ds(pl.multiple_of(place * tile_tok, tile_tok), tile_tok)
        out_ref[slot * tile_tok : (slot + 1) * tile_tok, :] = pick(
            column_step, [ref[at, :] for ref in in_refs]
        )


def merge_kernel(img_dev, docs, counts, *refs):
    in_refs, out_ref = refs[:-1], refs[-1]
    slots = docs.shape[0]
    tile_tok = out_ref.shape[0] // slots
    for slot in range(slots):
        _, _, row_step, _ = slot_place(docs, counts, slot, img_dev)
        at = slice(slot * tile_tok, (slot + 1) * tile_tok)
        out_ref[at, :] = pick(row_step, [ref[at, :] for ref in in_refs])


def prepare_kernel(gate, query_ref, cot_ref, query_rows, dattn_rows, cot_t):
    tok = query_ref.shape[0]
    head_dim = query_rows.shape[1]
    tanh_gate = jnp.tanh(jnp.full((1, head_dim), gate[0], F32))
    for head in range(query_ref.shape[1] // head_dim):
        cols = slice(head * head_dim, (head + 1) * head_dim)
        at = slice(head * tok, (head + 1) * tok)
        query_rows[at, :] = query_ref[:, cols]
        cot = cot_ref[:, cols].astype(F32)
        dattn_rows[at, :] = (tanh_gate * cot).astype(BF16)
        cot_t[:, at] = cot.T


def finish_kernel(gate, attn_t, dquery_t, gated_ref, dquery_ref):
    tok = gated_ref.shape[0]
    head_dim = attn_t.shape[0]
    tanh_gate = jnp.tanh(jnp.full((1, head_dim), gate[0], F32))
    for head in range(gated_ref.shape[1] // head_dim):
        cols = slice(head * head_dim, (head + 1) * head_dim)
        at = slice(head * tok, (head + 1) * tok)
        gated_ref[:, cols] = (attn_t[:, at].T * tanh_gate).astype(BF16)
        dquery_ref[:, cols] = (dquery_t[:, at].T * head_dim ** (-0.5)).astype(BF16)


def attention_kernel(docs, counts, tiles, gate, *refs):
    kv_refs, (query_rows, dattn_rows, cot_t, attn_t, dquery_t) = refs[:TILES], refs[TILES:][:5]
    dkv_refs, gate_ref = refs[TILES + 5 :][:TILES], refs[2 * TILES + 5]
    kv_rows, exp_t, prob_t, dscore_t, dkv_rows, top_part, total_part = refs[2 * TILES + 6 :]
    group, column, _ = place_in_group()
    slots = docs.shape[0]
    rows, head_dim = query_rows.shape
    scale = head_dim ** (-0.5)
    tile_tok = kv_refs[0].shape[0] // slots
    col_blocks = [slice(c, c + ROW_BLOCK) for c in range(0, rows, ROW_BLOCK)]

    kv_rows[...] = jnp.zeros_like(kv_rows)
    places = []
    start = jnp.int32(0)
    for slot in range(slots):
        live = slot < counts[group]
        count = jnp.where(live, tiles[jnp.where(live, docs[slot, group], 0)], 0)
        for step in range(TILES):
            tile = lax.bitwise_xor(column, step)
            at = pl.ds(pl.multiple_of((start + tile) * tile_tok, tile_tok), tile_tok)
            places.append((slot, step, at, tile < count))
            kv_rows[at, :] = kv_refs[step][slot * tile_tok : (slot + 1) * tile_tok, :]
        start = start + count
    live_keys = start * tile_tok
    blocks = lax.div(live_keys + (KEY_BLOCK - 1), KEY_BLOCK)

    top_part[...] = jnp.full_like(top_part, -jnp.inf)
    total_part[...] = jnp.zeros_like(total_part)
    attn_t[...] = jnp.zeros_like(attn_t)
    dquery_t[...] = jnp.zeros_like(dquery_t)

    def block_rows(block):
        return pl.ds(pl.multiple_of(block * KEY_BLOCK, KEY_BLOCK), KEY_BLOCK)

    def fold(x, op):
        return op(x.reshape(KEY_BLOCK // 8, 8, x.shape[1]), axis=0)

    def score_pass(block, carry):
        at = block_rows(block)
        keys = kv_rows[at, :head_dim]
        key_index = lax.broadcasted_iota(jnp.int32, (KEY_BLOCK, ROW_BLOCK), 0)
        live = key_index < live_keys - block * KEY_BLOCK
        for cols in col_blocks:
            scores = contract(keys, query_rows[cols, :], 1, 1) * scale
            scores = jnp.where(live, scores, -jnp.inf)
            exp_t[at, cols] = scores
            top_part[:, cols] = jnp.maximum(top_part[:, cols], fold(scores, jnp.max))
        return carry

    lax.fori_loop(0, blocks, score_pass, 0)
    top = jnp.max(top_part[...], axis=0, keepdims=True)

    def exp_pass(block, carry):
        at = block_rows(block)
        for cols in col_blocks:
            raised = jnp.exp(exp_t[at, cols] - top[:, cols])
            exp_t[at, cols] = raised
            total_part[:, cols] += fold(raised, jnp.sum)
        return carry

    lax.fori_loop(0, blocks, exp_pass, 0)
    inverse = 1.0 / jnp.sum(total_part[...], axis=0, keepdims=True)

    def attn_pass(block, carry):
        at = block_rows(block)
        values = kv_rows[at, head_dim:]
        for cols in col_blocks:
            probs_low = (exp_t[at, cols] * inverse[:, cols]).astype(BF16)
            prob_t[at, cols] = probs_low
            attn_t[:, cols] += contract(values, probs_low, 0, 0)
        return carry

    lax.fori_loop(0, blocks, attn_pass, 0)
    gate_rows = jnp.sum(cot_t[...] * attn_t[...], axis=0, keepdims=True)
    delta = jnp.tanh(jnp.full((1, rows), gate[0], F32)) * gate_rows
    gate_ref[...] = jnp.broadcast_to(jnp.sum(gate_rows, axis=1, keepdims=True), gate_ref.shape)

    def grad_pass(block, carry):
        at = block_rows(block)
        keys, values = kv_rows[at, :head_dim], kv_rows[at, head_dim:]
        for cols in col_blocks:
            probs = exp_t[at, cols] * inverse[:, cols]
            dprob = contract(values, dattn_rows[cols, :], 1, 1)
            dscore = (probs * (dprob - delta[:, cols])).astype(BF16)
            dscore_t[:, cols] = dscore
            dquery_t[:, cols] += contract(keys, dscore, 0, 0)
        dkeys = contract(dscore_t[...], query_rows[...], 1, 0) * scale
        dvalues = contract(prob_t[at, :], dattn_rows[...], 1, 0)
        dkv_rows[at, :head_dim] = dkeys.astype(BF16)
        dkv_rows[at, head_dim:] = dvalues.astype(BF16)
        return carry

    lax.fori_loop(0, blocks, grad_pass, 0)

    for slot, step, at, live in places:
        grads = dkv_rows[at, :]
        dkv_refs[step][slot * tile_tok : (slot + 1) * tile_tok, :] = jnp.where(
            live, grads, jnp.zeros_like(grads)
        )


def split_term(term):
    term = jnp.broadcast_to(term, (CHUNK, term.shape[1]))
    high = term.astype(BF16).astype(F32)
    middle = (term - high).astype(BF16).astype(F32)
    low = term - high - middle
    index = lax.broadcasted_iota(jnp.int32, term.shape, 0)
    return jnp.where(index == 0, high, jnp.where(index == 1, middle, low)).astype(BF16)


def pair_sum(values):
    while len(values) > 1:
        values = [a + b for a, b in zip(values[::2], values[1::2], strict=True)]
    return values[0]


def term_sum(in_refs, first):
    terms = []
    for ref in in_refs:
        rows = ref[first : first + CHUNK, :].astype(F32)
        terms.append(rows[0:1, :] + rows[1:2, :] + rows[2:3, :])
    return pair_sum(terms)


def sum_kernel(gate_ref, *refs):
    in_refs, out_ref = refs[:-1], refs[-1]
    sent = in_refs[0].shape[0]
    for first in range(0, sent, 64):
        at = slice(first, first + 64)
        out_ref[at, :] = pair_sum([ref[at, :].astype(F32) for ref in in_refs]).astype(BF16)
    width = gate_ref.shape[1]
    split = split_term(gate_ref[0:1, :])
    for first in range(0, out_ref.shape[1], width):
        out_ref[sent:, first : first + width] = split


def route_kernel(img_dev, docs, counts, *refs):
    in_refs, out_refs = refs[:TILES], refs[TILES:]
    slots = docs.shape[0]
    sent = in_refs[0].shape[0] - CHUNK
    tile_tok = sent // slots
    split = split_term(term_sum(in_refs, sent))
    for out_ref in out_refs:
        out_ref[: img_dev * tile_tok, :] = jnp.zeros((img_dev * tile_tok, out_ref.shape[1]), BF16)
        out_ref[img_dev * tile_tok :, :] = split
    for slot in range(slots):
        at = slice(slot * tile_tok, (slot + 1) * tile_tok)
        total = pair_sum([ref[at, :].astype(F32) for ref in in_refs]).astype(BF16)
        live, column_step, row_step, place = slot_place(docs, counts, slot, img_dev)
        to = pl.ds(pl.multiple_of(place * tile_tok, tile_tok), tile_tok)
        for step, out_ref in enumerate(out_refs):

            @pl.when(live & (row_step == 0) & (column_step == step))
            def _(out_ref=out_ref):
                out_ref[to, :] = total


def unpack_kernel(norm_factor, gate, *refs):
    in_refs, (grads_ref, gate_ref) = refs[:-2], refs[-2:]
    _, column, _ = place_in_group()
    img_dev, img_tok, _ = grads_ref.shape
    tile_tok = img_tok // TILES
    for step, ref in enumerate(in_refs):
        tile = lax.bitwise_xor(column, step)
        to = pl.ds(pl.multiple_of(tile * tile_tok, tile_tok), tile_tok)
        for img in range(img_dev):
            grads_ref[img, to, :] = ref[img * tile_tok : (img + 1) * tile_tok, :].astype(F32)
    total = term_sum(in_refs, img_dev * tile_tok)
    tanh_gate = jnp.tanh(jnp.full(total.shape, gate[0], F32))
    gate_ref[0] = ((1.0 - tanh_gate * tanh_gate) * total * norm_factor)[0, 0]


def sum_over(x, axis):
    size = lax.axis_size(axis)

    def moved(step):
        return lax.ppermute(x, axis, [(i, i ^ step) for i in range(size)])

    step = 1
    while step < size:
        if 2 * step < size:
            x = (x + moved(step)) + (moved(2 * step) + moved(3 * step))
            step *= 4
        else:
            x = x + moved(step)
            step *= 2
    return x


def swap(arrays, unit):
    size = lax.axis_size("seq")
    return [arrays[0]] + [
        lax.ppermute(arrays[step], "seq", [(i, i ^ (step * unit)) for i in range(size)])
        for step in range(1, len(arrays))
    ]


def call(kernel, name, outs, smem, vmem, **kwargs):
    return pl.pallas_call(
        kernel,
        out_shape=outs,
        in_specs=[SMEM()] * len(smem) + [VMEM()] * len(vmem),
        out_specs=jax.tree.map(lambda _: VMEM(), outs),
        compiler_params=pltpu.CompilerParams(vmem_limit_bytes=6 * 1024 * 1024),
        name=name,
        **kwargs,
    )(*smem, *vmem)


def per_device(queries, grad_out, image_kv, image_tiles, doc_images, doc_counts, gate):
    _, tok, width = queries.shape
    img_dev, img_tok, kv_width = image_kv.shape
    head_dim = kv_width // 2
    rows = tok * (width // head_dim)
    slots = doc_images.shape[1]
    devices = lax.axis_size("seq")
    side = devices // TILES
    keys = slots * img_tok
    tile_tok = img_tok // TILES
    sent = slots * tile_tok
    docs = doc_images.T
    place = (docs, doc_counts)

    def low(*shape):
        return jax.ShapeDtypeStruct(shape, BF16)

    def full(*shape):
        return jax.ShapeDtypeStruct(shape, F32)

    own = pl.pallas_call(
        pack_kernel,
        out_shape=(low(img_dev * tile_tok, kv_width),) * TILES,
        in_specs=[pl.BlockSpec(memory_space=pl.ANY)],
        out_specs=(VMEM(),) * TILES,
        scratch_shapes=[pltpu.SemaphoreType.DMA((TILES, img_dev))],
        compiler_params=pltpu.CompilerParams(vmem_limit_bytes=6 * 1024 * 1024),
        name="pack_tiles",
    )(image_kv.reshape(img_dev, TILES, tile_tok, kv_width))
    mine = swap(own, side)
    cited = call(
        functools.partial(select_kernel, img_dev), "select_cited", low(sent, kv_width), place, mine
    )
    cited = call(
        functools.partial(merge_kernel, img_dev),
        "merge_cited",
        low(sent, kv_width),
        place,
        swap([cited] * side, 1),
    )
    kv_tiles = swap([cited] * TILES, side)

    prepared = call(
        prepare_kernel,
        "prepare_rows",
        (low(rows, head_dim), low(rows, head_dim), full(head_dim, rows)),
        (gate,),
        (queries[0], grad_out[0]),
    )
    attn_t, dquery_t, *partial, gate_sum = pl.pallas_call(
        attention_kernel,
        out_shape=(
            full(head_dim, rows),
            full(head_dim, rows),
            *[low(sent, kv_width)] * TILES,
            full(8, 128),
        ),
        in_specs=[SMEM()] * 4 + [VMEM()] * (TILES + 3),
        out_specs=(VMEM(),) * (TILES + 3),
        scratch_shapes=[
            pltpu.VMEM((keys, kv_width), BF16),
            pltpu.VMEM((keys, rows), F32),
            pltpu.VMEM((keys, rows), BF16),
            pltpu.VMEM((KEY_BLOCK, rows), BF16),
            pltpu.VMEM((keys, kv_width), BF16),
            pltpu.VMEM((8, rows), F32),
            pltpu.VMEM((8, rows), F32),
        ],
        compiler_params=pltpu.CompilerParams(vmem_limit_bytes=40 * 1024 * 1024),
        name="attention",
    )(docs, doc_counts, image_tiles, gate, *kv_tiles, *prepared)

    partial = swap(partial, side)
    gate_sum = sum_over(gate_sum, "dp")
    summed = call(sum_kernel, "sum_column", low(sent + CHUNK, kv_width), (), (gate_sum, *partial))
    gated, dquery = call(
        finish_kernel, "finish_rows", (low(tok, width),) * 2, (gate,), (attn_t, dquery_t)
    )
    routed = call(
        functools.partial(route_kernel, img_dev),
        "sum_row_and_route",
        (low(img_dev * tile_tok + CHUNK, kv_width),) * TILES,
        place,
        swap([summed] * side, 1),
    )
    norm_factor = float(lax.axis_size("dp") * tok * devices * width) ** (-0.5)
    grad_image_kv, grad_gate = pl.pallas_call(
        functools.partial(unpack_kernel, norm_factor),
        out_shape=(full(img_dev, img_tok, kv_width), full(1)),
        in_specs=[SMEM()] + [VMEM()] * TILES,
        out_specs=(VMEM(), SMEM()),
        compiler_params=pltpu.CompilerParams(vmem_limit_bytes=6 * 1024 * 1024),
        name="unpack_grads",
    )(gate, *swap(routed, side))
    return gated[None], dquery[None], grad_image_kv, grad_gate


def solution(mesh):
    return jax.shard_map(
        per_device,
        mesh=mesh,
        in_specs=(
            P("dp", "seq", None),
            P("dp", "seq", None),
            P(("dp", "seq"), None, None),
            P(),
            P(),
            P(),
            P(),
        ),
        out_specs=(P("dp", "seq", None), P("dp", "seq", None), P(("dp", "seq"), None, None), P()),
        check_vma=False,
    )
```

time: 89.8 us -> 101 us (1.12)
  blocking collectives: 18.3 us -> 0 us
  waiting for transfers between devices: 28.2 us -> 46.2 us
  starting transfers between devices: 28.7 us -> 41.8 us
  Pallas kernels: 9.68 us -> 8.66 us
    ppermute x0 -> x18, waiting for transfers between devices: none -> 44.6 us  [swap(): lax.ppermute(arrays[step], 'seq', [(i, i ^ step * unit) for i in range(si...]
    ppermute x0 -> x18, starting transfers between devices: none -> 26.8 us  [swap(): lax.ppermute(arrays[step], 'seq', [(i, i ^ step * unit) for i in range(si...]
    all_to_all x3 -> x0, waiting for transfers between devices: 21.6 us -> none  [the longest x1 12.2 us: per_device(): kv_cited = lax.all_to_all(cited, 'seq', 0, 0)]
    all_to_all x1 -> x0, blocking collectives: 18.3 us -> none  [per_device(): chunks = lax.all_to_all(chunks, 'seq', 0, 0)]
    all_to_all x3 -> x0, starting transfers between devices: 14.5 us -> none  [the longest x1 7.11 us: per_device(): owned = lax.all_to_all(summed, 'seq', 0, 0)]
    ppermute x6, waiting for transfers between devices: 6.63 us -> 1.58 us  [moved(): return lax.ppermute(x, axis, [(i, i ^ step) for i in range(size)])]
    pallas_call x6 -> x8, Pallas kernels: 8.64 us -> 7.61 us  [the longest x6 3.6 us: call(): pl.pallas_call(kernel, out_shape=outs, in_specs=[SMEM()] * len(smem) + [V...]
  transfers between devices with their start and end apart: 9 -> 24, of which waited for: 4 -> 15; matrix products, arithmetic and copies ran while one was open for 0% -> 0% of each run, Pallas kernels for 1% -> 1%
where the time goes in v3:
time: 101 us; the launch traced here: 100 us
  waiting for transfers between devices  46.2 us (46%)
  starting transfers between devices  41.8 us (41%)
  Pallas kernels  8.66 us (9%)
  local copies, waits for them, and re-layouts  1.71 us (2%)
  between operations  1.59 us (2%)
    ppermute x18, waiting for transfers between devices, swap(): lax.ppermute(arrays[step], 'seq', [(i, i ^ step * unit) for i in range(si...  44.6 us
    ppermute x18, starting transfers between devices, swap(): lax.ppermute(arrays[step], 'seq', [(i, i ^ step * unit) for i in range(si...  26.8 us
    ppermute x6, starting transfers between devices, moved(): return lax.ppermute(x, axis, [(i, i ^ step) for i in range(size)])  15 us
    pallas_call x6, Pallas kernels, call(): pl.pallas_call(kernel, out_shape=outs, in_specs=[SMEM()] * len(smem) + [V...  3.6 us
    pallas_call x1, Pallas kernels, per_device(): pl.pallas_call(attention_kernel, out_shape=(full(head_dim, rows), full(he...  3.2 us
  transfers between devices with their start and end apart: 24, of which 15 were waited for; matrix products, arithmetic and copies ran while one was open for 0% of the time, Pallas kernels for 1%

profile of v3, /device:TPU:32, one launch (start us, length us, event | category | flops | bytes accessed | tf_op | source)
XLA Modules:
  0.0 100.0 jit_solution(477979889128049774)
XLA Ops:
  2.5 1.6 %collective-permute-start = (bf16[256,256]{1,0:T(8,128)(2,1)S(1)}, bf16[256,256]{1,0:T(8,128)(2,1)S(1)}, u32[]{:S(2)}, u32[]{:S(2)}) collective-permute-start(bf16[256,256]{1,0:T(8,128)(2,1)S(1)} %get-tuple-element.27), channel_id=1, source_target_pairs={{0,4},{1,5},{2,6},{3,7},{4,0},{5,1},{6,2},{7,3},{8,12},{9,13},{10,... | collective-permute-start | bytes 393224 | tf_op jit(solution)/shard_map/ppermute | solution.py:308
  4.1 2.7 %collective-permute-start.1 = (bf16[256,256]{1,0:T(8,128)(2,1)S(1)}, bf16[256,256]{1,0:T(8,128)(2,1)S(1)}, u32[]{:S(2)}, u32[]{:S(2)}) collective-permute-start(bf16[256,256]{1,0:T(8,128)(2,1)S(1)} %get-tuple-element.28), channel_id=1, source_target_pairs={{0,8},{1,9},{2,10},{3,11},{4,12},{5,13},{6,14},{7,15},{8,0},{9,1},... | collective-permute-start | bytes 393224 | tf_op jit(solution)/shard_map/ppermute | solution.py:308
  8.5 4.4 %collective-permute-done.1.refs_2_ = bf16[256,256]{1,0:T(8,128)(2,1)S(1)} collective-permute-done((bf16[256,256]{1,0:T(8,128)(2,1)S(1)}, bf16[256,256]{1,0:T(8,128)(2,1)S(1)}, u32[]{:S(2)}, u32[]{:S(2)}) %collective-permute-start.1) | collective-permute-done | bytes 131104 | tf_op jit(solution)/shard_map/ppermute | solution.py:308
  12.9 2.1 %collective-permute-done.2.refs_3_ = bf16[256,256]{1,0:T(8,128)(2,1)S(1)} collective-permute-done((bf16[256,256]{1,0:T(8,128)(2,1)S(1)}, bf16[256,256]{1,0:T(8,128)(2,1)S(1)}, u32[]{:S(2)}, u32[]{:S(2)}) %collective-permute-start.2) | collective-permute-done | bytes 131104 | tf_op jit(solution)/shard_map/ppermute | solution.py:308
  16.4 3.1 %collective-permute-start.5 = (bf16[384,256]{1,0:T(8,128)(2,1)S(1)}, bf16[384,256]{1,0:T(8,128)(2,1)S(1)}, u32[]{:S(2)}, u32[]{:S(2)}) collective-permute-start(bf16[384,256]{1,0:T(8,128)(2,1)S(1)} %select_cited.1.refs_0_), channel_id=1, source_target_pairs={{0,3},{1,2},{2,1},{3,0},{4,7},{5,6},{6,5},{7,4},{8,11},{9,10},{10,... | collective-permute-start | bytes 589832 | tf_op jit(solution)/shard_map/ppermute | solution.py:308
  20.6 6.8 %collective-permute-done.5.refs_3_ = bf16[384,256]{1,0:T(8,128)(2,1)S(1)} collective-permute-done((bf16[384,256]{1,0:T(8,128)(2,1)S(1)}, bf16[384,256]{1,0:T(8,128)(2,1)S(1)}, u32[]{:S(2)}, u32[]{:S(2)}) %collective-permute-start.5) | collective-permute-done | bytes 196640 | tf_op jit(solution)/shard_map/ppermute | solution.py:308
  31.1 2.6 %collective-permute-start.6 = (bf16[384,256]{1,0:T(8,128)(2,1)S(1)}, bf16[384,256]{1,0:T(8,128)(2,1)S(1)}, u32[]{:S(2)}, u32[]{:S(2)}) collective-permute-start(bf16[384,256]{1,0:T(8,128)(2,1)S(1)} %merge_cited.1.refs_0_), channel_id=1, source_target_pairs={{0,4},{1,5},{2,6},{3,7},{4,0},{5,1},{6,2},{7,3},{8,12},{9,13},{10,... | collective-permute-start | bytes 589832 | tf_op jit(solution)/shard_map/ppermute | solution.py:308
  34.5 5.6 %collective-permute-done.8.refs_3_ = bf16[384,256]{1,0:T(8,128)(2,1)S(1)} collective-permute-done((bf16[384,256]{1,0:T(8,128)(2,1)S(1)}, bf16[384,256]{1,0:T(8,128)(2,1)S(1)}, u32[]{:S(2)}, u32[]{:S(2)}) %collective-permute-start.8) | collective-permute-done | bytes 196640 | tf_op jit(solution)/shard_map/ppermute | solution.py:308
  40.7 3.2 %attention.1 = (f32[128,1024]{1,0:T(8,128)S(1)}, f32[128,1024]{1,0:T(8,128)S(1)}, bf16[384,256]{1,0:T(8,128)(2,1)S(1)}, bf16[384,256]{1,0:T(8,128)(2,1)S(1)}, bf...) custom-call(s32[6,16]{1,0:T(8,128)S(1)} %bitcast.11, s32[16]{0:T(128)S(1)} %copy-done.4, ...), custom_call_target="tpu_custom_call" | custom-call | tf_op jit(solution)/shard_map/attention/pallas_call | solution.py:374
  44.0 8.3 %collective-permute-start.10 = (f32[8,128]{1,0:T(8,128)S(1)}, f32[8,128]{1,0:T(8,128)S(1)}, u32[]{:S(2)}, u32[]{:S(2)}) collective-permute-start(f32[8,128]{1,0:T(8,128)S(1)} %get-tuple-element.37), channel_id=1, source_target_pairs={{0,32},{16,48},{32,0},{48,16},{64,96},{80,112},{96,64},{112,80},{1... | collective-permute-start | bytes 12296 | tf_op jit(solution)/shard_map/ppermute | solution.py:292
  52.4 1.6 %collective-permute-done.10 = f32[8,128]{1,0:T(8,128)S(1)} collective-permute-done((f32[8,128]{1,0:T(8,128)S(1)}, f32[8,128]{1,0:T(8,128)S(1)}, u32[]{:S(2)}, u32[]{:S(2)}) %collective-permute-start.10) | collective-permute-done | bytes 4128 | tf_op jit(solution)/shard_map/ppermute | solution.py:292
  54.0 2.3 %collective-permute-start.14 = (f32[8,128]{1,0:T(8,128)S(1)}, f32[8,128]{1,0:T(8,128)S(1)}, u32[]{:S(2)}, u32[]{:S(2)}) collective-permute-start(f32[8,128]{1,0:T(8,128)S(1)} %add_add_fusion.1), channel_id=1, source_target_pairs={{0,192},{16,208},{32,224},{48,240},{64,128},{80,144},{96,160},{112... | collective-permute-start | bytes 12296 | tf_op jit(solution)/shard_map/ppermute | solution.py:292
  56.7 3.9 %collective-permute-start.12 = (f32[8,128]{1,0:T(8,128)S(1)}, f32[8,128]{1,0:T(8,128)S(1)}, u32[]{:S(2)}, u32[]{:S(2)}) collective-permute-start(f32[8,128]{1,0:T(8,128)S(1)} %add_add_fusion.1), channel_id=1, source_target_pairs={{0,64},{16,80},{32,96},{48,112},{64,0},{80,16},{96,32},{112,48},{1... | collective-permute-start | bytes 12296 | tf_op jit(solution)/shard_map/ppermute | solution.py:292
  60.5 2.8 %collective-permute-start.16 = (bf16[384,256]{1,0:T(8,128)(2,1)S(1)}, bf16[384,256]{1,0:T(8,128)(2,1)S(1)}, u32[]{:S(2)}, u32[]{:S(2)}) collective-permute-start(bf16[384,256]{1,0:T(8,128)(2,1)S(1)} %get-tuple-element.40), channel_id=1, source_target_pairs={{0,8},{1,9},{2,10},{3,11},{4,12},{5,13},{6,14},{7,15},{8,0},{9,1},... | collective-permute-start | bytes 589832 | tf_op jit(solution)/shard_map/ppermute | solution.py:308
  63.3 1.9 %collective-permute-start.17 = (bf16[384,256]{1,0:T(8,128)(2,1)S(1)}, bf16[384,256]{1,0:T(8,128)(2,1)S(1)}, u32[]{:S(2)}, u32[]{:S(2)}) collective-permute-start(bf16[384,256]{1,0:T(8,128)(2,1)S(1)} %get-tuple-element.41), channel_id=1, source_target_pairs={{0,12},{1,13},{2,14},{3,15},{4,8},{5,9},{6,10},{7,11},{8,4},{9,5},... | collective-permute-start | bytes 589832 | tf_op jit(solution)/shard_map/ppermute | solution.py:308
  65.3 3.0 %collective-permute-done.15.refs_1_ = bf16[384,256]{1,0:T(8,128)(2,1)S(1)} collective-permute-done((bf16[384,256]{1,0:T(8,128)(2,1)S(1)}, bf16[384,256]{1,0:T(8,128)(2,1)S(1)}, u32[]{:S(2)}, u32[]{:S(2)}) %collective-permute-start.15) | collective-permute-done | bytes 196640 | tf_op jit(solution)/shard_map/ppermute | solution.py:308
  68.3 4.2 %collective-permute-done.16.refs_2_ = bf16[384,256]{1,0:T(8,128)(2,1)S(1)} collective-permute-done((bf16[384,256]{1,0:T(8,128)(2,1)S(1)}, bf16[384,256]{1,0:T(8,128)(2,1)S(1)}, u32[]{:S(2)}, u32[]{:S(2)}) %collective-permute-start.16) | collective-permute-done | bytes 196640 | tf_op jit(solution)/shard_map/ppermute | solution.py:308
  72.5 2.6 %collective-permute-done.17.refs_3_ = bf16[384,256]{1,0:T(8,128)(2,1)S(1)} collective-permute-done((bf16[384,256]{1,0:T(8,128)(2,1)S(1)}, bf16[384,256]{1,0:T(8,128)(2,1)S(1)}, u32[]{:S(2)}, u32[]{:S(2)}) %collective-permute-start.17) | collective-permute-done | bytes 196640 | tf_op jit(solution)/shard_map/ppermute | solution.py:308
  75.2 3.2 %collective-permute-start.20 = (bf16[400,256]{1,0:T(8,128)(2,1)S(1)}, bf16[400,256]{1,0:T(8,128)(2,1)S(1)}, u32[]{:S(2)}, u32[]{:S(2)}) collective-permute-start(bf16[400,256]{1,0:T(8,128)(2,1)S(1)} %sum_column.1.refs_0_), channel_id=1, source_target_pairs={{0,3},{1,2},{2,1},{3,0},{4,7},{5,6},{6,5},{7,4},{8,11},{9,10},{10,... | collective-permute-start | bytes 614408 | tf_op jit(solution)/shard_map/ppermute | solution.py:308
  79.4 6.9 %collective-permute-done.20.refs_3_ = bf16[400,256]{1,0:T(8,128)(2,1)S(1)} collective-permute-done((bf16[400,256]{1,0:T(8,128)(2,1)S(1)}, bf16[400,256]{1,0:T(8,128)(2,1)S(1)}, u32[]{:S(2)}, u32[]{:S(2)}) %collective-permute-start.20) | collective-permute-done | bytes 204832 | tf_op jit(solution)/shard_map/ppermute | solution.py:308
  86.3 1.6 %collective-permute-done.19.refs_2_ = bf16[400,256]{1,0:T(8,128)(2,1)S(1)} collective-permute-done((bf16[400,256]{1,0:T(8,128)(2,1)S(1)}, bf16[400,256]{1,0:T(8,128)(2,1)S(1)}, u32[]{:S(2)}, u32[]{:S(2)}) %collective-permute-start.19) | collective-permute-done | bytes 204832 | tf_op jit(solution)/shard_map/ppermute | solution.py:308
  88.8 3.7 %collective-permute-start.22 = (bf16[272,256]{1,0:T(8,128)(2,1)S(1)}, bf16[272,256]{1,0:T(8,128)(2,1)S(1)}, u32[]{:S(2)}, u32[]{:S(2)}) collective-permute-start(bf16[272,256]{1,0:T(8,128)(2,1)S(1)} %get-tuple-element.44), channel_id=1, source_target_pairs={{0,8},{1,9},{2,10},{3,11},{4,12},{5,13},{6,14},{7,15},{8,0},{9,1},... | collective-permute-start | bytes 417800 | tf_op jit(solution)/shard_map/ppermute | solution.py:308
  94.6 2.4 %collective-permute-done.22.refs_2_ = bf16[272,256]{1,0:T(8,128)(2,1)S(1)} collective-permute-done((bf16[272,256]{1,0:T(8,128)(2,1)S(1)}, bf16[272,256]{1,0:T(8,128)(2,1)S(1)}, u32[]{:S(2)}, u32[]{:S(2)}) %collective-permute-start.22) | collective-permute-done | bytes 139296 | tf_op jit(solution)/shard_map/ppermute | solution.py:308
  97.1 1.7 %collective-permute-done.23.refs_3_ = bf16[272,256]{1,0:T(8,128)(2,1)S(1)} collective-permute-done((bf16[272,256]{1,0:T(8,128)(2,1)S(1)}, bf16[272,256]{1,0:T(8,128)(2,1)S(1)}, u32[]{:S(2)}, u32[]{:S(2)}) %collective-permute-start.23) | collective-permute-done | bytes 139296 | tf_op jit(solution)/shard_map/ppermute | solution.py:308
  (47 shorter events, 16.3 us)
Async XLA Ops:
  2.5 6.0 %collective-permute-start = (bf16[256,256]{1,0:T(8,128)(2,1)S(1)}, bf16[256,256]{1,0:T(8,128)(2,1)S(1)}, u32[]{:S(2)}, u32[]{:S(2)}) collective-permute-start(bf16[256,256]{1,0:T(8,128)(2,1)S(1)} %get-tuple-element.27), channel_id=1, source_target_pairs={{0,4},{1,5},{2,6},{3,7},{4,0},{5,1},{6,2},{7,3},{8,12},{9,13},{10,... | collective-permute-start | bytes 393224 | tf_op jit(solution)/shard_map/ppermute | solution.py:308
  4.1 8.9 %collective-permute-start.1 = (bf16[256,256]{1,0:T(8,128)(2,1)S(1)}, bf16[256,256]{1,0:T(8,128)(2,1)S(1)}, u32[]{:S(2)}, u32[]{:S(2)}) collective-permute-start(bf16[256,256]{1,0:T(8,128)(2,1)S(1)} %get-tuple-element.28), channel_id=1, source_target_pairs={{0,8},{1,9},{2,10},{3,11},{4,12},{5,13},{6,14},{7,15},{8,0},{9,1},... | collective-permute-start | bytes 393224 | tf_op jit(solution)/shard_map/ppermute | solution.py:308
  6.8 8.2 %collective-permute-start.2 = (bf16[256,256]{1,0:T(8,128)(2,1)S(1)}, bf16[256,256]{1,0:T(8,128)(2,1)S(1)}, u32[]{:S(2)}, u32[]{:S(2)}) collective-permute-start(bf16[256,256]{1,0:T(8,128)(2,1)S(1)} %get-tuple-element.29), channel_id=1, source_target_pairs={{0,12},{1,13},{2,14},{3,15},{4,8},{5,9},{6,10},{7,11},{8,4},{9,5},... | collective-permute-start | bytes 393224 | tf_op jit(solution)/shard_map/ppermute | solution.py:308
  16.4 10.9 %collective-permute-start.5 = (bf16[384,256]{1,0:T(8,128)(2,1)S(1)}, bf16[384,256]{1,0:T(8,128)(2,1)S(1)}, u32[]{:S(2)}, u32[]{:S(2)}) collective-permute-start(bf16[384,256]{1,0:T(8,128)(2,1)S(1)} %select_cited.1.refs_0_), channel_id=1, source_target_pairs={{0,3},{1,2},{2,1},{3,0},{4,7},{5,6},{6,5},{7,4},{8,11},{9,10},{10,... | collective-permute-start | bytes 589832 | tf_op jit(solution)/shard_map/ppermute | solution.py:308
  19.5 9.3 %collective-permute-start.4 = (bf16[384,256]{1,0:T(8,128)(2,1)S(1)}, bf16[384,256]{1,0:T(8,128)(2,1)S(1)}, u32[]{:S(2)}, u32[]{:S(2)}) collective-permute-start(bf16[384,256]{1,0:T(8,128)(2,1)S(1)} %select_cited.1.refs_0_), channel_id=1, source_target_pairs={{0,2},{1,3},{2,0},{3,1},{4,6},{5,7},{6,4},{7,5},{8,10},{9,11},{10,... | collective-permute-start | bytes 589832 | tf_op jit(solution)/shard_map/ppermute | solution.py:308
  20.1 8.7 %collective-permute-start.3 = (bf16[384,256]{1,0:T(8,128)(2,1)S(1)}, bf16[384,256]{1,0:T(8,128)(2,1)S(1)}, u32[]{:S(2)}, u32[]{:S(2)}) collective-permute-start(bf16[384,256]{1,0:T(8,128)(2,1)S(1)} %select_cited.1.refs_0_), channel_id=1, source_target_pairs={{0,1},{1,0},{2,3},{3,2},{4,5},{5,4},{6,7},{7,6},{8,9},{9,8},{10,11... | collective-permute-start | bytes 589832 | tf_op jit(solution)/shard_map/ppermute | solution.py:308
  29.5 10.6 %collective-permute-start.8 = (bf16[384,256]{1,0:T(8,128)(2,1)S(1)}, bf16[384,256]{1,0:T(8,128)(2,1)S(1)}, u32[]{:S(2)}, u32[]{:S(2)}) collective-permute-start(bf16[384,256]{1,0:T(8,128)(2,1)S(1)} %merge_cited.1.refs_0_), channel_id=1, source_target_pairs={{0,12},{1,13},{2,14},{3,15},{4,8},{5,9},{6,10},{7,11},{8,4},{9,5},... | collective-permute-start | bytes 589832 | tf_op jit(solution)/shard_map/ppermute | solution.py:308
  30.5 9.6 %collective-permute-start.7 = (bf16[384,256]{1,0:T(8,128)(2,1)S(1)}, bf16[384,256]{1,0:T(8,128)(2,1)S(1)}, u32[]{:S(2)}, u32[]{:S(2)}) collective-permute-start(bf16[384,256]{1,0:T(8,128)(2,1)S(1)} %merge_cited.1.refs_0_), channel_id=1, source_target_pairs={{0,8},{1,9},{2,10},{3,11},{4,12},{5,13},{6,14},{7,15},{8,0},{9,1},... | collective-permute-start | bytes 589832 | tf_op jit(solution)/shard_map/ppermute | solution.py:308
  31.1 9.6 %collective-permute-start.6 = (bf16[384,256]{1,0:T(8,128)(2,1)S(1)}, bf16[384,256]{1,0:T(8,128)(2,1)S(1)}, u32[]{:S(2)}, u32[]{:S(2)}) collective-permute-start(bf16[384,256]{1,0:T(8,128)(2,1)S(1)} %merge_cited.1.refs_0_), channel_id=1, source_target_pairs={{0,4},{1,5},{2,6},{3,7},{4,0},{5,1},{6,2},{7,3},{8,12},{9,13},{10,... | collective-permute-start | bytes 589832 | tf_op jit(solution)/shard_map/ppermute | solution.py:308
  43.9 8.5 %collective-permute-start.11 = (f32[8,128]{1,0:T(8,128)S(1)}, f32[8,128]{1,0:T(8,128)S(1)}, u32[]{:S(2)}, u32[]{:S(2)}) collective-permute-start(f32[8,128]{1,0:T(8,128)S(1)} %get-tuple-element.37), channel_id=1, source_target_pairs={{0,48},{16,32},{32,16},{48,0},{64,112},{80,96},{96,80},{112,64},{1... | collective-permute-start | bytes 12296 | tf_op jit(solution)/shard_map/ppermute | solution.py:292
  44.0 9.9 %collective-permute-start.10 = (f32[8,128]{1,0:T(8,128)S(1)}, f32[8,128]{1,0:T(8,128)S(1)}, u32[]{:S(2)}, u32[]{:S(2)}) collective-permute-start(f32[8,128]{1,0:T(8,128)S(1)} %get-tuple-element.37), channel_id=1, source_target_pairs={{0,32},{16,48},{32,0},{48,16},{64,96},{80,112},{96,64},{112,80},{1... | collective-permute-start | bytes 12296 | tf_op jit(solution)/shard_map/ppermute | solution.py:292
  52.4 1.6 %collective-permute-start.9 = (f32[8,128]{1,0:T(8,128)S(1)}, f32[8,128]{1,0:T(8,128)S(1)}, u32[]{:S(2)}, u32[]{:S(2)}) collective-permute-start(f32[8,128]{1,0:T(8,128)S(1)} %get-tuple-element.37), channel_id=1, source_target_pairs={{0,16},{16,0},{32,48},{48,32},{64,80},{80,64},{96,112},{112,96},{1... | collective-permute-start | bytes 12296 | tf_op jit(solution)/shard_map/ppermute | solution.py:292
  54.0 9.4 %collective-permute-start.14 = (f32[8,128]{1,0:T(8,128)S(1)}, f32[8,128]{1,0:T(8,128)S(1)}, u32[]{:S(2)}, u32[]{:S(2)}) collective-permute-start(f32[8,128]{1,0:T(8,128)S(1)} %add_add_fusion.1), channel_id=1, source_target_pairs={{0,192},{16,208},{32,224},{48,240},{64,128},{80,144},{96,160},{112... | collective-permute-start | bytes 12296 | tf_op jit(solution)/shard_map/ppermute | solution.py:292
  56.3 9.0 %collective-permute-start.13 = (f32[8,128]{1,0:T(8,128)S(1)}, f32[8,128]{1,0:T(8,128)S(1)}, u32[]{:S(2)}, u32[]{:S(2)}) collective-permute-start(f32[8,128]{1,0:T(8,128)S(1)} %add_add_fusion.1), channel_id=1, source_target_pairs={{0,128},{16,144},{32,160},{48,176},{64,192},{80,208},{96,224},{112... | collective-permute-start | bytes 12296 | tf_op jit(solution)/shard_map/ppermute | solution.py:292
  56.7 8.6 %collective-permute-start.12 = (f32[8,128]{1,0:T(8,128)S(1)}, f32[8,128]{1,0:T(8,128)S(1)}, u32[]{:S(2)}, u32[]{:S(2)}) collective-permute-start(f32[8,128]{1,0:T(8,128)S(1)} %add_add_fusion.1), channel_id=1, source_target_pairs={{0,64},{16,80},{32,96},{48,112},{64,0},{80,16},{96,32},{112,48},{1... | collective-permute-start | bytes 12296 | tf_op jit(solution)/shard_map/ppermute | solution.py:292
  60.5 7.8 %collective-permute-start.15 = (bf16[384,256]{1,0:T(8,128)(2,1)S(1)}, bf16[384,256]{1,0:T(8,128)(2,1)S(1)}, u32[]{:S(2)}, u32[]{:S(2)}) collective-permute-start(bf16[384,256]{1,0:T(8,128)(2,1)S(1)} %get-tuple-element.39), channel_id=1, source_target_pairs={{0,4},{1,5},{2,6},{3,7},{4,0},{5,1},{6,2},{7,3},{8,12},{9,13},{10,... | collective-permute-start | bytes 589832 | tf_op jit(solution)/shard_map/ppermute | solution.py:308
  60.5 11.9 %collective-permute-start.16 = (bf16[384,256]{1,0:T(8,128)(2,1)S(1)}, bf16[384,256]{1,0:T(8,128)(2,1)S(1)}, u32[]{:S(2)}, u32[]{:S(2)}) collective-permute-start(bf16[384,256]{1,0:T(8,128)(2,1)S(1)} %get-tuple-element.40), channel_id=1, source_target_pairs={{0,8},{1,9},{2,10},{3,11},{4,12},{5,13},{6,14},{7,15},{8,0},{9,1},... | collective-permute-start | bytes 589832 | tf_op jit(solution)/shard_map/ppermute | solution.py:308
  63.3 11.7 %collective-permute-start.17 = (bf16[384,256]{1,0:T(8,128)(2,1)S(1)}, bf16[384,256]{1,0:T(8,128)(2,1)S(1)}, u32[]{:S(2)}, u32[]{:S(2)}) collective-permute-start(bf16[384,256]{1,0:T(8,128)(2,1)S(1)} %get-tuple-element.41), channel_id=1, source_target_pairs={{0,12},{1,13},{2,14},{3,15},{4,8},{5,9},{6,10},{7,11},{8,4},{9,5},... | collective-permute-start | bytes 589832 | tf_op jit(solution)/shard_map/ppermute | solution.py:308
  75.2 11.1 %collective-permute-start.20 = (bf16[400,256]{1,0:T(8,128)(2,1)S(1)}, bf16[400,256]{1,0:T(8,128)(2,1)S(1)}, u32[]{:S(2)}, u32[]{:S(2)}) collective-permute-start(bf16[400,256]{1,0:T(8,128)(2,1)S(1)} %sum_column.1.refs_0_), channel_id=1, source_target_pairs={{0,3},{1,2},{2,1},{3,0},{4,7},{5,6},{6,5},{7,4},{8,11},{9,10},{10,... | collective-permute-start | bytes 614408 | tf_op jit(solution)/shard_map/ppermute | solution.py:308
  78.4 9.4 %collective-permute-start.19 = (bf16[400,256]{1,0:T(8,128)(2,1)S(1)}, bf16[400,256]{1,0:T(8,128)(2,1)S(1)}, u32[]{:S(2)}, u32[]{:S(2)}) collective-permute-start(bf16[400,256]{1,0:T(8,128)(2,1)S(1)} %sum_column.1.refs_0_), channel_id=1, source_target_pairs={{0,2},{1,3},{2,0},{3,1},{4,6},{5,7},{6,4},{7,5},{8,10},{9,11},{10,... | collective-permute-start | bytes 614408 | tf_op jit(solution)/shard_map/ppermute | solution.py:308
  78.5 9.4 %collective-permute-start.18 = (bf16[400,256]{1,0:T(8,128)(2,1)S(1)}, bf16[400,256]{1,0:T(8,128)(2,1)S(1)}, u32[]{:S(2)}, u32[]{:S(2)}) collective-permute-start(bf16[400,256]{1,0:T(8,128)(2,1)S(1)} %sum_column.1.refs_0_), channel_id=1, source_target_pairs={{0,1},{1,0},{2,3},{3,2},{4,5},{5,4},{6,7},{7,6},{8,9},{9,8},{10,11... | collective-permute-start | bytes 614408 | tf_op jit(solution)/shard_map/ppermute | solution.py:308
  88.7 5.9 %collective-permute-start.21 = (bf16[272,256]{1,0:T(8,128)(2,1)S(1)}, bf16[272,256]{1,0:T(8,128)(2,1)S(1)}, u32[]{:S(2)}, u32[]{:S(2)}) collective-permute-start(bf16[272,256]{1,0:T(8,128)(2,1)S(1)} %get-tuple-element.43), channel_id=1, source_target_pairs={{0,4},{1,5},{2,6},{3,7},{4,0},{5,1},{6,2},{7,3},{8,12},{9,13},{10,... | collective-permute-start | bytes 417800 | tf_op jit(solution)/shard_map/ppermute | solution.py:308
  88.8 8.3 %collective-permute-start.22 = (bf16[272,256]{1,0:T(8,128)(2,1)S(1)}, bf16[272,256]{1,0:T(8,128)(2,1)S(1)}, u32[]{:S(2)}, u32[]{:S(2)}) collective-permute-start(bf16[272,256]{1,0:T(8,128)(2,1)S(1)} %get-tuple-element.44), channel_id=1, source_target_pairs={{0,8},{1,9},{2,10},{3,11},{4,12},{5,13},{6,14},{7,15},{8,0},{9,1},... | collective-permute-start | bytes 417800 | tf_op jit(solution)/shard_map/ppermute | solution.py:308
  92.5 6.3 %collective-permute-start.23 = (bf16[272,256]{1,0:T(8,128)(2,1)S(1)}, bf16[272,256]{1,0:T(8,128)(2,1)S(1)}, u32[]{:S(2)}, u32[]{:S(2)}) collective-permute-start(bf16[272,256]{1,0:T(8,128)(2,1)S(1)} %get-tuple-element.45), channel_id=1, source_target_pairs={{0,12},{1,13},{2,14},{3,15},{4,8},{5,9},{6,10},{7,11},{8,4},{9,5},... | collective-permute-start | bytes 417800 | tf_op jit(solution)/shard_map/ppermute | solution.py:308
  (6 other events, 56.4 us)

commit v4 on v2

v4 whole, which is shorter than its diff:
```python
import functools

import jax
import jax.numpy as jnp
from jax import lax
from jax.experimental import pallas as pl
from jax.experimental.pallas import tpu as pltpu
from jax.sharding import PartitionSpec as P

TILES = 4
CHUNK = 16
KEY_BLOCK = 256
ROW_BLOCK = 256
F32 = jnp.float32
BF16 = jnp.bfloat16

SMEM = functools.partial(pl.BlockSpec, memory_space=pltpu.SMEM)
VMEM = functools.partial(pl.BlockSpec, memory_space=pltpu.VMEM)


def contract(a, b, dim_a, dim_b):
    return lax.dot_general(a, b, (((dim_a,), (dim_b,)), ((), ())), preferred_element_type=F32)


class Slot:
    pass


def plan(docs, counts, tiles, img_dev):
    group = lax.axis_index("dp")
    group_img = lax.axis_size("seq") * img_dev
    slots = []
    start = jnp.int32(0)
    for index in range(docs.shape[0]):
        slot = Slot()
        slot.live = index < counts[group]
        image = jnp.where(slot.live, docs[index, group], group * group_img)
        slot.owner = lax.div(image - group * group_img, img_dev)
        slot.place = lax.rem(image - group * group_img, img_dev)
        slot.start, slot.count = start, jnp.where(slot.live, tiles[image], 0)
        slot.rank = jnp.int32(0)
        for other in slots:
            slot.rank = slot.rank + jnp.where(other.owner == slot.owner, 1, 0)
        start = start + slot.count
        slots.append(slot)
    return slots, start


def position(slot, img_dev, room):
    return slot.place if room == img_dev else slot.rank


def own_image(slots, me, place):
    cited, start, rank = jnp.bool_(False), jnp.int32(0), jnp.int32(0)
    for slot in slots:
        here = slot.live & (slot.owner == me) & (slot.place == place)
        cited = cited | here
        start = jnp.where(here, slot.start, start)
        rank = jnp.where(here, slot.rank, rank)
    return cited, start, rank


def tile_of(residue, start):
    return lax.bitwise_and(residue - start, TILES - 1)


def chunk_rows(index):
    return pl.ds(pl.multiple_of(index * CHUNK, CHUNK), CHUNK)


def pack_kernel(docs, counts, tiles, image_ref, out_ref):
    img_dev, img_tok, _ = image_ref.shape
    quarters = img_tok // TILES // CHUNK
    slots, _ = plan(docs, counts, tiles, img_dev)
    for img in range(img_dev):
        _, start, _ = own_image(slots, lax.axis_index("seq"), img)
        for residue in range(TILES):
            tile = tile_of(residue, start)
            for quarter in range(quarters):
                out_ref[residue * quarters + quarter, img * CHUNK : (img + 1) * CHUNK, :] = (
                    image_ref[img, chunk_rows(tile * quarters + quarter), :]
                )


def held_chunks(slots, quarters):
    residue = lax.div(lax.axis_index("seq"), quarters)
    for slot in slots:
        tile = tile_of(residue, slot.start)
        yield slot, tile < slot.count, lax.div(slot.start + tile, TILES)


def select_kernel(docs, counts, tiles, chunks_ref, out_ref, held):
    parts = chunks_ref.shape[0]
    img_dev = chunks_ref.shape[1] // CHUNK
    slots, _ = plan(docs, counts, tiles, img_dev)
    held[...] = jnp.zeros_like(held)
    for slot, here, number in held_chunks(slots, parts // TILES):

        @pl.when(here)
        def _(slot=slot, number=number):
            held[chunk_rows(number), :] = chunks_ref[slot.owner, chunk_rows(slot.place), :]

    for part in range(parts):
        out_ref[part] = held[...]


def prepare_kernel(gate, query_ref, cot_ref, query_rows, dattn_rows, cot_t):
    tok = query_ref.shape[0]
    head_dim = query_rows.shape[1]
    tanh_gate = jnp.tanh(jnp.full((1, head_dim), gate[0], F32))
    for head in range(query_ref.shape[1] // head_dim):
        cols = slice(head * head_dim, (head + 1) * head_dim)
        at = slice(head * tok, (head + 1) * tok)
        query_rows[at, :] = query_ref[:, cols]
        cot = cot_ref[:, cols].astype(F32)
        dattn_rows[at, :] = (tanh_gate * cot).astype(BF16)
        cot_t[:, at] = cot.T


def finish_kernel(gate, attn_t, dquery_t, gated_ref, dquery_ref):
    tok = gated_ref.shape[0]
    head_dim = attn_t.shape[0]
    tanh_gate = jnp.tanh(jnp.full((1, head_dim), gate[0], F32))
    for head in range(gated_ref.shape[1] // head_dim):
        cols = slice(head * head_dim, (head + 1) * head_dim)
        at = slice(head * tok, (head + 1) * tok)
        gated_ref[:, cols] = (attn_t[:, at].T * tanh_gate).astype(BF16)
        dquery_ref[:, cols] = (dquery_t[:, at].T * head_dim ** (-0.5)).astype(BF16)


def attention_kernel(
    img_dev, docs, counts, tiles, gate,
    kv_ref, query_rows, dattn_rows, cot_t,
    attn_t, dquery_t, dkv_ref, gate_ref,
    kv_rows, exp_t, prob_t, dscore_t, dkv_rows, top_part, total_part,
):
    parts = kv_ref.shape[0]
    rows, head_dim = query_rows.shape
    scale = head_dim ** (-0.5)
    tile_tok = parts * CHUNK // TILES
    col_blocks = [slice(c, c + ROW_BLOCK) for c in range(0, rows, ROW_BLOCK)]
    chunks = kv_ref.shape[1] // CHUNK
    places = [
        (part, slice(n * CHUNK, (n + 1) * CHUNK), n, slice(row, row + CHUNK))
        for n in range(chunks)
        for part in range(parts)
        for row in [n * KEY_BLOCK + part * CHUNK]
    ]
    for part, at, _, row in places:
        kv_rows[row, :] = kv_ref[part, at, :]
    _, live_tiles = plan(docs, counts, tiles, img_dev)
    live_keys = live_tiles * tile_tok
    blocks = lax.div(live_keys + (KEY_BLOCK - 1), KEY_BLOCK)
    top_part[...] = jnp.full_like(top_part, -jnp.inf)
    total_part[...] = jnp.zeros_like(total_part)
    attn_t[...] = jnp.zeros_like(attn_t)
    dquery_t[...] = jnp.zeros_like(dquery_t)

    def block_rows(block):
        return pl.ds(pl.multiple_of(block * KEY_BLOCK, KEY_BLOCK), KEY_BLOCK)

    def fold(x, op):
        return op(x.reshape(KEY_BLOCK // 8, 8, x.shape[1]), axis=0)

    def score_pass(block, carry):
        at = block_rows(block)
        keys = kv_rows[at, :head_dim]
        key_index = lax.broadcasted_iota(jnp.int32, (KEY_BLOCK, ROW_BLOCK), 0)
        live = key_index < live_keys - block * KEY_BLOCK
        for cols in col_blocks:
            scores = contract(keys, query_rows[cols, :], 1, 1) * scale
            scores = jnp.where(live, scores, -jnp.inf)
            exp_t[at, cols] = scores
            top_part[:, cols] = jnp.maximum(top_part[:, cols], fold(scores, jnp.max))
        return carry

    lax.fori_loop(0, blocks, score_pass, 0)
    top = jnp.max(top_part[...], axis=0, keepdims=True)

    def exp_pass(block, carry):
        at = block_rows(block)
        for cols in col_blocks:
            raised = jnp.exp(exp_t[at, cols] - top[:, cols])
            exp_t[at, cols] = raised
            total_part[:, cols] += fold(raised, jnp.sum)
        return carry

    lax.fori_loop(0, blocks, exp_pass, 0)
    inverse = 1.0 / jnp.sum(total_part[...], axis=0, keepdims=True)

    def attn_pass(block, carry):
        at = block_rows(block)
        values = kv_rows[at, head_dim:]
        for cols in col_blocks:
            probs_low = (exp_t[at, cols] * inverse[:, cols]).astype(BF16)
            prob_t[at, cols] = probs_low
        attn_t[...] += contract(values, prob_t[at, :], 0, 0)
        return carry

    lax.fori_loop(0, blocks, attn_pass, 0)
    gate_rows = jnp.sum(cot_t[...] * attn_t[...], axis=0, keepdims=True)
    delta = jnp.tanh(jnp.full((1, rows), gate[0], F32)) * gate_rows
    gate_ref[...] = jnp.broadcast_to(jnp.sum(gate_rows, axis=1, keepdims=True), gate_ref.shape)

    def grad_pass(block, carry):
        at = block_rows(block)
        keys, values = kv_rows[at, :head_dim], kv_rows[at, head_dim:]
        for cols in col_blocks:
            probs = exp_t[at, cols] * inverse[:, cols]
            dprob = contract(values, dattn_rows[cols, :], 1, 1)
            dscore = (probs * (dprob - delta[:, cols])).astype(BF16)
            dscore_t[:, cols] = dscore
        dquery_t[...] += contract(keys, dscore_t[...], 0, 0)
        dkeys = contract(dscore_t[...], query_rows[...], 1, 0) * scale
        dvalues = contract(prob_t[at, :], dattn_rows[...], 1, 0)
        dkv_rows[at, :head_dim] = dkeys.astype(BF16)
        dkv_rows[at, head_dim:] = dvalues.astype(BF16)
        return carry

    lax.fori_loop(0, blocks, grad_pass, 0)

    for part, at, n, row in places:
        grads = dkv_rows[row, :]
        dkv_ref[part, at, :] = jnp.where(n < blocks, grads, jnp.zeros_like(grads))


def sum_kernel(img_dev, docs, counts, tiles, partial_ref, gate_ref, out_ref, sums):
    parts = partial_ref.shape[0]
    half = out_ref.shape[2]
    sent = out_ref.shape[1] - CHUNK
    room = sent // (2 * CHUNK)
    for number in range(partial_ref.shape[1] // CHUNK):
        at = slice(number * CHUNK, (number + 1) * CHUNK)
        total = partial_ref[0, at, :].astype(F32)
        for part in range(1, parts):
            total = total + partial_ref[part, at, :].astype(F32)
        sums[at, :] = total.astype(BF16)
    out_ref[:, :sent, :] = jnp.zeros((parts, sent, half), BF16)
    slots, _ = plan(docs, counts, tiles, img_dev)
    for slot, here, number in held_chunks(slots, parts // TILES):

        @pl.when(here)
        def _(slot=slot, number=number):
            place = position(slot, img_dev, room)
            out_ref[slot.owner, chunk_rows(place), :] = sums[chunk_rows(number), :half]
            out_ref[slot.owner, chunk_rows(place + room), :] = sums[chunk_rows(number), half:]

    term = jnp.broadcast_to(gate_ref[0:1, :], (CHUNK, half))
    high = term.astype(BF16).astype(F32)
    middle = (term - high).astype(BF16).astype(F32)
    low = term - high - middle
    index = lax.broadcasted_iota(jnp.int32, term.shape, 0)
    split = jnp.where(index == 0, high, jnp.where(index == 1, middle, low)).astype(BF16)
    for part in range(parts):
        out_ref[part, sent:, :] = split


def unpack_kernel(norm_factor, docs, counts, tiles, gate, owned_ref, grads_ref, gate_ref):
    parts = owned_ref.shape[0]
    img_dev = grads_ref.shape[0]
    half = owned_ref.shape[2]
    sent = owned_ref.shape[1] - CHUNK
    room = sent // (2 * CHUNK)
    quarters = parts // TILES
    slots, _ = plan(docs, counts, tiles, img_dev)
    for img in range(img_dev):
        cited, start, rank = own_image(slots, lax.axis_index("seq"), img)
        place = jnp.int32(img) if room == img_dev else rank
        for part in range(parts):
            tile = tile_of(part // quarters, start)
            to = chunk_rows(tile * quarters + part % quarters)
            for cols, row in ((slice(0, half), place), (slice(half, 2 * half), place + room)):
                grads = owned_ref[part, chunk_rows(row), :].astype(F32)
                grads_ref[img, to, cols] = jnp.where(cited, grads, jnp.zeros_like(grads))
    total = owned_ref[0, sent:, :].astype(F32)
    for part in range(1, parts):
        total = total + owned_ref[part, sent:, :].astype(F32)
    total = total[0:1, :] + total[1:2, :] + total[2:3, :]
    tanh_gate = jnp.tanh(jnp.full(total.shape, gate[0], F32))
    gate_ref[0] = ((1.0 - tanh_gate * tanh_gate) * total * norm_factor)[0, 0]


def sum_over(x, axis):
    size = lax.axis_size(axis)

    def moved(step):
        return lax.ppermute(x, axis, [(i, i ^ step) for i in range(size)])

    step = 1
    while step < size:
        if 2 * step < size:
            x = (x + moved(step)) + (moved(2 * step) + moved(3 * step))
            step *= 4
        else:
            x = x + moved(step)
            step *= 2
    return x


def call(kernel, name, outs, smem, vmem, scratch=(), vmem_mib=6, out_specs=None):
    return pl.pallas_call(
        kernel,
        out_shape=outs,
        in_specs=[SMEM()] * len(smem) + [VMEM()] * len(vmem),
        out_specs=out_specs or jax.tree.map(lambda _: VMEM(), outs),
        scratch_shapes=list(scratch),
        compiler_params=pltpu.CompilerParams(vmem_limit_bytes=vmem_mib * 1024 * 1024),
        name=name,
    )(*smem, *vmem)


def low(*shape):
    return jax.ShapeDtypeStruct(shape, BF16)


def full(*shape):
    return jax.ShapeDtypeStruct(shape, F32)


def after_scatter(blocks, room, img_dev, queries, grad_out, chunks, gate, *lists):
    tok, width = queries.shape
    parts, _, kv_width = chunks.shape
    head_dim = kv_width // 2
    rows = tok * (width // head_dim)
    keys = blocks * KEY_BLOCK
    sent = blocks * CHUNK

    cited = call(
        select_kernel,
        "select_cited",
        low(parts, sent, kv_width),
        lists,
        (chunks,),
        [pltpu.VMEM((sent, kv_width), BF16)],
    )
    kv_cited = lax.all_to_all(cited, "seq", 0, 0)
    prepared = call(
        prepare_kernel,
        "prepare_rows",
        (low(rows, head_dim), low(rows, head_dim), full(head_dim, rows)),
        (gate,),
        (queries, grad_out),
    )
    attn_t, dquery_t, partial, gate_sum = call(
        functools.partial(attention_kernel, img_dev),
        "attention",
        (
            full(head_dim, rows),
            full(head_dim, rows),
            low(parts, sent, kv_width),
            full(8, 128),
        ),
        (*lists, gate),
        (kv_cited, *prepared),
        [
            pltpu.VMEM((keys, kv_width), BF16),
            pltpu.VMEM((keys, rows), F32),
            pltpu.VMEM((keys, rows), BF16),
            pltpu.VMEM((KEY_BLOCK, rows), BF16),
            pltpu.VMEM((keys, kv_width), BF16),
            pltpu.VMEM((8, rows), F32),
            pltpu.VMEM((8, rows), F32),
        ],
        vmem_mib=40,
    )
    partial = lax.all_to_all(partial, "seq", 0, 0)
    gated, dquery = call(
        finish_kernel, "finish_rows", (low(tok, width),) * 2, (gate,), (attn_t, dquery_t)
    )
    gate_sum = sum_over(gate_sum, "dp")
    summed = call(
        functools.partial(sum_kernel, img_dev),
        "sum_partials",
        low(parts, (2 * room + 1) * CHUNK, head_dim),
        lists,
        (partial, gate_sum),
        [pltpu.VMEM((sent, kv_width), BF16)],
    )
    owned = lax.all_to_all(summed, "seq", 0, 0)
    norm_factor = float(lax.axis_size("dp") * tok * parts * width) ** (-0.5)
    grads, grad_gate = call(
        functools.partial(unpack_kernel, norm_factor),
        "unpack_grads",
        (full(img_dev, parts * CHUNK, kv_width), full(1)),
        (*lists, gate),
        (owned,),
        out_specs=(VMEM(), SMEM()),
    )
    return gated, dquery, grads, grad_gate


def per_device(queries, grad_out, image_kv, image_tiles, doc_images, doc_counts, gate):
    img_dev, img_tok, kv_width = image_kv.shape
    parts = lax.axis_size("seq")
    slots = doc_images.shape[1]
    lists = (doc_images.T, doc_counts, image_tiles)
    chunks = call(
        pack_kernel,
        "pack_chunks",
        low(parts, img_dev * CHUNK, kv_width),
        lists,
        (image_kv,),
    )
    chunks = lax.all_to_all(chunks, "seq", 0, 0)
    gated, dquery, grads, grad_gate = after_scatter(
        slots, img_dev, img_dev, queries[0], grad_out[0], chunks, gate, *lists
    )
    return gated[None], dquery[None], grads, grad_gate


def solution(mesh):
    return jax.shard_map(
        per_device,
        mesh=mesh,
        in_specs=(
            P("dp", "seq", None),
            P("dp", "seq", None),
            P(("dp", "seq"), None, None),
            P(),
            P(),
            P(),
            P(),
        ),
        out_specs=(P("dp", "seq", None), P("dp", "seq", None), P(("dp", "seq"), None, None), P()),
        check_vma=False,
    )
```

time: 89.8 us -> 89.8 us (level)
  starting transfers between devices: 28.7 us -> 24.6 us
  Pallas kernels: 9.68 us -> 12.1 us
    ppermute x6, starting transfers between devices: 14.2 us -> 10.2 us  [moved(): return lax.ppermute(x, axis, [(i, i ^ step) for i in range(size)])]
    pallas_call x7, Pallas kernels: 9.68 us -> 12.1 us  [call(): pl.pallas_call(kernel, out_shape=outs, in_specs=[SMEM()] * len(smem) + [V...]
    unnamed x12 -> x16, local copies, waits for them, and re-layouts: 1.71 us -> 3.08 us
    all_to_all x3, waiting for transfers between devices: 21.6 us -> 22.9 us  [the longest x1 12.2 us: after_scatter(): kv_cited = lax.all_to_all(cited, 'seq', 0, 0)]
  transfers between devices with their start and end apart: 9 -> 9, of which waited for: 4 -> 5; matrix products, arithmetic and copies ran while one was open for 0% -> 0% of each run, Pallas kernels for 1% -> 1%
where the time goes in v4:
time: 89.8 us; the launch traced here: 88.6 us
  waiting for transfers between devices  29 us (32%)
  starting transfers between devices  24.6 us (27%)
  blocking collectives  18.3 us (20%)
  Pallas kernels  12.1 us (13%)
  local copies, waits for them, and re-layouts  3.08 us (3%)
  between operations  1.39 us (2%)
    all_to_all x1, blocking collectives, per_device(): chunks = lax.all_to_all(chunks, 'seq', 0, 0)  18.3 us
    all_to_all x1, waiting for transfers between devices, after_scatter(): kv_cited = lax.all_to_all(cited, 'seq', 0, 0)  12.2 us
    pallas_call x7, Pallas kernels, call(): pl.pallas_call(kernel, out_shape=outs, in_specs=[SMEM()] * len(smem) + [V...  12.1 us
    all_to_all x1, waiting for transfers between devices, after_scatter(): owned = lax.all_to_all(summed, 'seq', 0, 0)  10.7 us
    ppermute x6, starting transfers between devices, moved(): return lax.ppermute(x, axis, [(i, i ^ step) for i in range(size)])  10.2 us
    all_to_all x1, starting transfers between devices, after_scatter(): owned = lax.all_to_all(summed, 'seq', 0, 0)  7.11 us
    ppermute x6, waiting for transfers between devices, moved(): return lax.ppermute(x, axis, [(i, i ^ step) for i in range(size)])  6.07 us
    all_to_all x1, starting transfers between devices, after_scatter(): kv_cited = lax.all_to_all(cited, 'seq', 0, 0)  3.75 us
  transfers between devices with their start and end apart: 9, of which 5 were waited for; matrix products, arithmetic and copies ran while one was open for 0% of the time, Pallas kernels for 1%

profile of v4, /device:TPU:32, one launch (start us, length us, event | category | flops | bytes accessed | tf_op | source)
XLA Modules:
  0.0 88.6 jit_solution(16702469544362357966)
XLA Ops:
  0.6 0.6 copy-done.7
  1.3 1.0 %copy-done = bf16[4,256,256]{2,1,0:T(8,128)(2,1)S(1)} copy-done((bf16[4,256,256]{2,1,0:T(8,128)(2,1)S(1)}, bf16[4,256,256]{2,1,0:T(8,128)(2,1)}, u32[]{:S(2)}) %copy-start) | copy-done | bytes 524312
  2.3 0.7 copy-done.3
  3.0 0.7 copy-done.5
  3.7 0.8 pack_chunks.1
  4.5 18.3 %all_to_all.20.chunks_ref = bf16[16,64,256]{2,1,0:T(8,128)(2,1)S(1)} all-to-all(bf16[16,64,256]{2,1,0:T(8,128)(2,1)S(1)} %pack_chunks.1), channel_id=1, replica_groups=mesh['dp'=16,'seq'=16] {'seq'}, dimensions={0} | all-to-all | bytes 1048576 | tf_op jit(solution)/shard_map/all_to_all | solution.py:404
  22.8 1.7 %select_cited.1 = bf16[16,96,256]{2,1,0:T(8,128)(2,1)} custom-call(s32[6,16]{1,0:T(8,128)S(1)} %bitcast.8, s32[16]{0:T(128)S(1)} %copy-done.7, s32[1024]{0:T(1024)S(1)} %copy-done.5, bf16[16,64,256]{2,1,0:T(8,128)(2,1)S(1)} %all_to_all.20.chunks_ref), custom_call_target="tpu_custom_call" | custom-call | tf_op jit(solution)/shard_map/select_cited/pallas_call | solution.py:301
  24.5 3.7 %all-to-all-start.1 = ((bf16[16,96,256]{2,1,0:T(8,128)(2,1)}), bf16[16,96,256]{2,1,0:T(8,128)(2,1)S(1)}, u32[]{:S(2)}, u32[]{:S(2)}) async-start(bf16[16,96,256]{2,1,0:T(8,128)(2,1)} %select_cited.1), calls=%async_computation.1 | async-start | bytes 1572864 | tf_op jit(solution)/shard_map/all_to_all | solution.py:336
  29.0 0.1 prepare_rows.1
  29.1 12.2 %all-to-all-done.1.kv_ref = bf16[16,96,256]{2,1,0:T(8,128)(2,1)S(1)} async-done(((bf16[16,96,256]{2,1,0:T(8,128)(2,1)}), bf16[16,96,256]{2,1,0:T(8,128)(2,1)S(1)}, u32[]{:S(2)}, u32[]{:S(2)}) %all-to-all-start.1) | async-done | bytes 786464 | tf_op jit(solution)/shard_map/all_to_all | solution.py:336
  41.4 4.8 %attention.1 = (f32[128,1024]{1,0:T(8,128)S(1)}, f32[128,1024]{1,0:T(8,128)S(1)}, bf16[16,96,256]{2,1,0:T(8,128)(2,1)}, f32[8,128]{1,0:T(8,128)S(1)}) custom-call(s32[6,16]{1,0:T(8,128)S(1)} %bitcast.9, s32[16]{0:T(128)S(1)} %copy-done.7, s32[1024]{0:T(1024)S(1)} %copy-done.6, f32[1]{0:T(128)S(6)} %copy.11.gate, ...), custom_call_target="tpu_custom_call" | custom-call | tf_op jit(solution)/shard_map/attention/pallas_call | solution.py:301
  46.2 3.6 %all-to-all-start.2 = ((bf16[16,96,256]{2,1,0:T(8,128)(2,1)}), bf16[16,96,256]{2,1,0:T(8,128)(2,1)S(1)}, u32[]{:S(2)}, u32[]{:S(2)}) async-start(bf16[16,96,256]{2,1,0:T(8,128)(2,1)} %get-tuple-element.22), calls=%async_computation.2 | async-start | bytes 1572864 | tf_op jit(solution)/shard_map/all_to_all | solution.py:366
  49.8 0.1 collective-permute-start.2
  49.9 3.1 %collective-permute-start.1 = (f32[8,128]{1,0:T(8,128)S(1)}, f32[8,128]{1,0:T(8,128)S(1)}, u32[]{:S(2)}, u32[]{:S(2)}) collective-permute-start(f32[8,128]{1,0:T(8,128)S(1)} %get-tuple-element.23), channel_id=1, source_target_pairs={{0,32},{16,48},{32,0},{48,16},{64,96},{80,112},{96,64},{112,80},{1... | collective-permute-start | bytes 12296 | tf_op jit(solution)/shard_map/ppermute | solution.py:287
  53.1 1.6 %collective-permute-done.1 = f32[8,128]{1,0:T(8,128)S(1)} collective-permute-done((f32[8,128]{1,0:T(8,128)S(1)}, f32[8,128]{1,0:T(8,128)S(1)}, u32[]{:S(2)}, u32[]{:S(2)}) %collective-permute-start.1) | collective-permute-done | bytes 4128 | tf_op jit(solution)/shard_map/ppermute | solution.py:287
  54.7 3.0 %collective-permute-start.5 = (f32[8,128]{1,0:T(8,128)S(1)}, f32[8,128]{1,0:T(8,128)S(1)}, u32[]{:S(2)}, u32[]{:S(2)}) collective-permute-start(f32[8,128]{1,0:T(8,128)S(1)} %add_add_fusion.1), channel_id=1, source_target_pairs={{0,192},{16,208},{32,224},{48,240},{64,128},{80,144},{96,160},{112... | collective-permute-start | bytes 12296 | tf_op jit(solution)/shard_map/ppermute | solution.py:287
  57.6 3.9 %collective-permute-start.4 = (f32[8,128]{1,0:T(8,128)S(1)}, f32[8,128]{1,0:T(8,128)S(1)}, u32[]{:S(2)}, u32[]{:S(2)}) collective-permute-start(f32[8,128]{1,0:T(8,128)S(1)} %add_add_fusion.1), channel_id=1, source_target_pairs={{0,128},{16,144},{32,160},{48,176},{64,192},{80,208},{96,224},{112... | collective-permute-start | bytes 12296 | tf_op jit(solution)/shard_map/ppermute | solution.py:287
  61.6 3.6 %collective-permute-done.4 = f32[8,128]{1,0:T(8,128)S(1)} collective-permute-done((f32[8,128]{1,0:T(8,128)S(1)}, f32[8,128]{1,0:T(8,128)S(1)}, u32[]{:S(2)}, u32[]{:S(2)}) %collective-permute-start.4) | collective-permute-done | bytes 4128 | tf_op jit(solution)/shard_map/ppermute | solution.py:287
  65.2 0.9 %collective-permute-done.3 = f32[8,128]{1,0:T(8,128)S(1)} collective-permute-done((f32[8,128]{1,0:T(8,128)S(1)}, f32[8,128]{1,0:T(8,128)S(1)}, u32[]{:S(2)}, u32[]{:S(2)}) %collective-permute-start.3) | collective-permute-done | bytes 4128 | tf_op jit(solution)/shard_map/ppermute | solution.py:287
  66.1 1.7 %sum_partials.1 = bf16[16,144,128]{2,1,0:T(8,128)(2,1)} custom-call(s32[6,16]{1,0:T(8,128)S(1)} %bitcast.10, s32[16]{0:T(128)S(1)} %copy-done.7, s32[1024]{0:T(1024)S(1)} %copy-done.6, bf16[16,96,256]{2,1,0:T(8,128)(2,1)S(1)} %all-to-all-done.2.partial_ref, f32[8,128]{1,0:T(8,128)S(1)} %add_add_fusion.gate_ref), custom_call_target="tpu_custom_call" | custom-call | tf_op jit(solution)/shard_map/sum_partials/pallas_call | solution.py:301
  67.8 7.1 %all-to-all-start.3 = ((bf16[16,144,128]{2,1,0:T(8,128)(2,1)}), bf16[16,144,128]{2,1,0:T(8,128)(2,1)S(1)}, u32[]{:S(2)}, u32[]{:S(2)}) async-start(bf16[16,144,128]{2,1,0:T(8,128)(2,1)} %sum_partials.1), calls=%async_computation.3 | async-start | bytes 1179648 | tf_op jit(solution)/shard_map/all_to_all | solution.py:379
  74.9 1.1 %finish_rows.1 = (bf16[128,1024]{1,0:T(8,128)(2,1)}, bf16[128,1024]{1,0:T(8,128)(2,1)}) custom-call(f32[1]{0:T(128)S(6)} %copy.11.gate, f32[128,1024]{1,0:T(8,128)S(1)} %get-tuple-element.18.attn_t, f32[128,1024]{1,0:T(8,128)S(1)} %get-tuple-element.19.dquery_t), custom_call_target="tpu_custom_call" | custom-call | tf_op jit(solution)/shard_map/finish_rows/pallas_call | solution.py:301
  76.0 10.7 %all-to-all-done.3.owned_ref = bf16[16,144,128]{2,1,0:T(8,128)(2,1)S(1)} async-done(((bf16[16,144,128]{2,1,0:T(8,128)(2,1)}), bf16[16,144,128]{2,1,0:T(8,128)(2,1)S(1)}, u32[]{:S(2)}, u32[]{:S(2)}) %all-to-all-start.3) | async-done | bytes 589856 | tf_op jit(solution)/shard_map/all_to_all | solution.py:379
  86.7 1.8 %unpack_grads.1 = (f32[4,256,256]{2,1,0:T(8,128)}, f32[1]{0:T(128)}) custom-call(s32[6,16]{1,0:T(8,128)S(1)} %bitcast.11, s32[16]{0:T(128)S(1)} %copy-done.7, s32[1024]{0:T(1024)S(1)} %copy-done.6, f32[1]{0:T(128)S(6)} %copy.11.gate, bf16[16,144,128]{2,1,0:T(8,128)(2,1)S(1)} %all-to-all-done.3.owned_ref), custom_call_target="tpu_custom_call" | custom-call | tf_op jit(solution)/shard_map/unpack_grads/pallas_call | solution.py:301
  (20 shorter events, 0.1 us)
Async XLA Ops:
  0.6 0.7 copy-start.7
  1.3 1.0 %copy-start = (bf16[4,256,256]{2,1,0:T(8,128)(2,1)S(1)}, bf16[4,256,256]{2,1,0:T(8,128)(2,1)}, u32[]{:S(2)}) copy-start(bf16[4,256,256]{2,1,0:T(8,128)(2,1)} %image_ref.1) | copy-start | bytes 1572868
  2.3 0.7 copy-start.3
  3.0 0.7 copy-start.5
  24.5 4.4 %copy-start.1 = (bf16[1,128,1024]{2,1,0:T(8,128)(2,1)S(1)}, bf16[1,128,1024]{2,1,0:T(8,128)(2,1)}, u32[]{:S(2)}) copy-start(bf16[1,128,1024]{2,1,0:T(8,128)(2,1)} %param.7) | copy-start | bytes 786436
  24.5 4.4 %copy-start.2 = (bf16[1,128,1024]{2,1,0:T(8,128)(2,1)S(1)}, bf16[1,128,1024]{2,1,0:T(8,128)(2,1)}, u32[]{:S(2)}) copy-start(bf16[1,128,1024]{2,1,0:T(8,128)(2,1)} %param.8) | copy-start | bytes 786436
  24.5 16.8 %all-to-all-start.1 = ((bf16[16,96,256]{2,1,0:T(8,128)(2,1)}), bf16[16,96,256]{2,1,0:T(8,128)(2,1)S(1)}, u32[]{:S(2)}, u32[]{:S(2)}) async-start(bf16[16,96,256]{2,1,0:T(8,128)(2,1)} %select_cited.1), calls=%async_computation.1 | async-start | bytes 1572864 | tf_op jit(solution)/shard_map/all_to_all | solution.py:336
  29.0 12.4 %copy-start.6 = (s32[1024]{0:T(1024)S(1)}, s32[1024]{0:T(1024)}, u32[]{:S(2)}) copy-start(s32[1024]{0:T(1024)} %tiles.9) | copy-start | bytes 12292
  29.1 12.2 %copy-start.4 = (s32[16,6]{0,1:T(8,128)S(1)}, s32[16,6]{0,1:T(8,128)}, u32[]{:S(2)}) copy-start(s32[16,6]{0,1:T(8,128)} %param.11) | copy-start | bytes 1156
  46.2 19.9 %all-to-all-start.2 = ((bf16[16,96,256]{2,1,0:T(8,128)(2,1)}), bf16[16,96,256]{2,1,0:T(8,128)(2,1)S(1)}, u32[]{:S(2)}, u32[]{:S(2)}) async-start(bf16[16,96,256]{2,1,0:T(8,128)(2,1)} %get-tuple-element.22), calls=%async_computation.2 | async-start | bytes 1572864 | tf_op jit(solution)/shard_map/all_to_all | solution.py:366
  49.8 3.3 %collective-permute-start.2 = (f32[8,128]{1,0:T(8,128)S(1)}, f32[8,128]{1,0:T(8,128)S(1)}, u32[]{:S(2)}, u32[]{:S(2)}) collective-permute-start(f32[8,128]{1,0:T(8,128)S(1)} %get-tuple-element.23), channel_id=1, source_target_pairs={{0,48},{16,32},{32,16},{48,0},{64,112},{80,96},{96,80},{112,64},{1... | collective-permute-start | bytes 12296 | tf_op jit(solution)/shard_map/ppermute | solution.py:287
  49.9 4.7 %collective-permute-start.1 = (f32[8,128]{1,0:T(8,128)S(1)}, f32[8,128]{1,0:T(8,128)S(1)}, u32[]{:S(2)}, u32[]{:S(2)}) collective-permute-start(f32[8,128]{1,0:T(8,128)S(1)} %get-tuple-element.23), channel_id=1, source_target_pairs={{0,32},{16,48},{32,0},{48,16},{64,96},{80,112},{96,64},{112,80},{1... | collective-permute-start | bytes 12296 | tf_op jit(solution)/shard_map/ppermute | solution.py:287
  53.1 1.6 %collective-permute-start = (f32[8,128]{1,0:T(8,128)S(1)}, f32[8,128]{1,0:T(8,128)S(1)}, u32[]{:S(2)}, u32[]{:S(2)}) collective-permute-start(f32[8,128]{1,0:T(8,128)S(1)} %get-tuple-element.23), channel_id=1, source_target_pairs={{0,16},{16,0},{32,48},{48,32},{64,80},{80,64},{96,112},{112,96},{1... | collective-permute-start | bytes 12296 | tf_op jit(solution)/shard_map/ppermute | solution.py:287
  54.7 6.9 %collective-permute-start.5 = (f32[8,128]{1,0:T(8,128)S(1)}, f32[8,128]{1,0:T(8,128)S(1)}, u32[]{:S(2)}, u32[]{:S(2)}) collective-permute-start(f32[8,128]{1,0:T(8,128)S(1)} %add_add_fusion.1), channel_id=1, source_target_pairs={{0,192},{16,208},{32,224},{48,240},{64,128},{80,144},{96,160},{112... | collective-permute-start | bytes 12296 | tf_op jit(solution)/shard_map/ppermute | solution.py:287
  57.6 7.5 %collective-permute-start.4 = (f32[8,128]{1,0:T(8,128)S(1)}, f32[8,128]{1,0:T(8,128)S(1)}, u32[]{:S(2)}, u32[]{:S(2)}) collective-permute-start(f32[8,128]{1,0:T(8,128)S(1)} %add_add_fusion.1), channel_id=1, source_target_pairs={{0,128},{16,144},{32,160},{48,176},{64,192},{80,208},{96,224},{112... | collective-permute-start | bytes 12296 | tf_op jit(solution)/shard_map/ppermute | solution.py:287
  61.6 4.5 %collective-permute-start.3 = (f32[8,128]{1,0:T(8,128)S(1)}, f32[8,128]{1,0:T(8,128)S(1)}, u32[]{:S(2)}, u32[]{:S(2)}) collective-permute-start(f32[8,128]{1,0:T(8,128)S(1)} %add_add_fusion.1), channel_id=1, source_target_pairs={{0,64},{16,80},{32,96},{48,112},{64,0},{80,16},{96,32},{112,48},{1... | collective-permute-start | bytes 12296 | tf_op jit(solution)/shard_map/ppermute | solution.py:287
  67.8 18.9 %all-to-all-start.3 = ((bf16[16,144,128]{2,1,0:T(8,128)(2,1)}), bf16[16,144,128]{2,1,0:T(8,128)(2,1)S(1)}, u32[]{:S(2)}, u32[]{:S(2)}) async-start(bf16[16,144,128]{2,1,0:T(8,128)(2,1)} %sum_partials.1), calls=%async_computation.3 | async-start | bytes 1179648 | tf_op jit(solution)/shard_map/all_to_all | solution.py:379

commit v5 on v4

--- a/solution.py
+++ b/solution.py
@@ -26,24 +26,42 @@
     pass
 
 
-def plan(docs, counts, tiles, img_dev):
+FIELDS = ("live", "owner", "place", "start", "count", "rank")
+STRIDE = 8
+
+
+def write_plan(docs, counts, tiles, img_dev, plan_ref):
     group = lax.axis_index("dp")
     group_img = lax.axis_size("seq") * img_dev
     slots = []
     start = jnp.int32(0)
     for index in range(docs.shape[0]):
         slot = Slot()
-        slot.live = index < counts[group]
-        image = jnp.where(slot.live, docs[index, group], group * group_img)
+        live = index < counts[group]
+        slot.live = jnp.where(live, 1, 0)
+        image = jnp.where(live, docs[index, group], group * group_img)
         slot.owner = lax.div(image - group * group_img, img_dev)
         slot.place = lax.rem(image - group * group_img, img_dev)
-        slot.start, slot.count = start, jnp.where(slot.live, tiles[image], 0)
+        slot.start, slot.count = start, jnp.where(live, tiles[image], 0)
         slot.rank = jnp.int32(0)
         for other in slots:
             slot.rank = slot.rank + jnp.where(other.owner == slot.owner, 1, 0)
         start = start + slot.count
         slots.append(slot)
-    return slots, start
+        for field, name in enumerate(FIELDS):
+            plan_ref[field * STRIDE + index] = getattr(slot, name)
+    plan_ref[len(FIELDS) * STRIDE] = start
+    return slots
+
+
+def read_plan(plan_ref, count):
+    slots = []
+    for index in range(count):
+        slot = Slot()
+        for field, name in enumerate(FIELDS):
+            setattr(slot, name, plan_ref[field * STRIDE + index])
+        slots.append(slot)
+    return slots
 
 
 def position(slot, img_dev, room):
@@ -51,13 +69,13 @@
 
 
 def own_image(slots, me, place):
-    cited, start, rank = jnp.bool_(False), jnp.int32(0), jnp.int32(0)
+    cited, start, rank = jnp.int32(0), jnp.int32(0), jnp.int32(0)
     for slot in slots:
-        here = slot.live & (slot.owner == me) & (slot.place == place)
-        cited = cited | here
+        here = (slot.live == 1) & (slot.owner == me) & (slot.place == place)
+        cited = jnp.where(here, 1, cited)
         start = jnp.where(here, slot.start, start)
         rank = jnp.where(here, slot.rank, rank)
-    return cited, start, rank
+    return cited == 1, start, rank
 
 
 def tile_of(residue, start):
@@ -68,18 +86,31 @@
     return pl.ds(pl.multiple_of(index * CHUNK, CHUNK), CHUNK)
 
 
-def pack_kernel(docs, counts, tiles, image_ref, out_ref):
-    img_dev, img_tok, _ = image_ref.shape
+def pack_kernel(
+    docs_hbm, counts_hbm, tiles_hbm, image_hbm, out_ref, plan_ref, docs, counts, tiles, image, sems
+):
+    copies = [
+        pltpu.make_async_copy(source, target, sems.at[index])
+        for index, (source, target) in enumerate(
+            ((docs_hbm, docs), (counts_hbm, counts), (tiles_hbm, tiles), (image_hbm, image))
+        )
+    ]
+    for copy in copies:
+        copy.start()
+    for copy in copies[:3]:
+        copy.wait()
+    img_dev, img_tok, _ = image.shape
     quarters = img_tok // TILES // CHUNK
-    slots, _ = plan(docs, counts, tiles, img_dev)
+    slots = write_plan(docs, counts, tiles, img_dev, plan_ref)
+    copies[3].wait()
     for img in range(img_dev):
         _, start, _ = own_image(slots, lax.axis_index("seq"), img)
         for residue in range(TILES):
             tile = tile_of(residue, start)
             for quarter in range(quarters):
-                out_ref[residue * quarters + quarter, img * CHUNK : (img + 1) * CHUNK, :] = (
-                    image_ref[img, chunk_rows(tile * quarters + quarter), :]
-                )
+                out_ref[residue * quarters + quarter, img * CHUNK : (img + 1) * CHUNK, :] = image[
+                    img, chunk_rows(tile * quarters + quarter), :
+                ]
 
 
 def held_chunks(slots, quarters):
@@ -89,10 +120,9 @@
         yield slot, tile < slot.count, lax.div(slot.start + tile, TILES)
 
 
-def select_kernel(docs, counts, tiles, chunks_ref, out_ref, held):
+def select_kernel(slot_count, plan, chunks_ref, out_ref, held):
     parts = chunks_ref.shape[0]
-    img_dev = chunks_ref.shape[1] // CHUNK
-    slots, _ = plan(docs, counts, tiles, img_dev)
+    slots = read_plan(plan, slot_count)
     held[...] = jnp.zeros_like(held)
     for slot, here, number in held_chunks(slots, parts // TILES):
 
@@ -129,7 +159,7 @@
 
 
 def attention_kernel(
-    img_dev, docs, counts, tiles, gate,
+    plan, gate,
     kv_ref, query_rows, dattn_rows, cot_t,
     attn_t, dquery_t, dkv_ref, gate_ref,
     kv_rows, exp_t, prob_t, dscore_t, dkv_rows, top_part, total_part,
@@ -148,8 +178,7 @@
     ]
     for part, at, _, row in places:
         kv_rows[row, :] = kv_ref[part, at, :]
-    _, live_tiles = plan(docs, counts, tiles, img_dev)
-    live_keys = live_tiles * tile_tok
+    live_keys = plan[len(FIELDS) * STRIDE] * tile_tok
     blocks = lax.div(live_keys + (KEY_BLOCK - 1), KEY_BLOCK)
     top_part[...] = jnp.full_like(top_part, -jnp.inf)
     total_part[...] = jnp.zeros_like(total_part)
@@ -224,7 +253,7 @@
         dkv_ref[part, at, :] = jnp.where(n < blocks, grads, jnp.zeros_like(grads))
 
 
-def sum_kernel(img_dev, docs, counts, tiles, partial_ref, gate_ref, out_ref, sums):
+def sum_kernel(slot_count, img_dev, plan, partial_ref, gate_ref, out_ref, sums):
     parts = partial_ref.shape[0]
     half = out_ref.shape[2]
     sent = out_ref.shape[1] - CHUNK
@@ -236,7 +265,7 @@
             total = total + partial_ref[part, at, :].astype(F32)
         sums[at, :] = total.astype(BF16)
     out_ref[:, :sent, :] = jnp.zeros((parts, sent, half), BF16)
-    slots, _ = plan(docs, counts, tiles, img_dev)
+    slots = read_plan(plan, slot_count)
     for slot, here, number in held_chunks(slots, parts // TILES):
 
         @pl.when(here)
@@ -255,14 +284,14 @@
         out_ref[part, sent:, :] = split
 
 
-def unpack_kernel(norm_factor, docs, counts, tiles, gate, owned_ref, grads_ref, gate_ref):
+def unpack_kernel(slot_count, norm_factor, plan, gate, owned_ref, grads_ref, gate_ref):
     parts = owned_ref.shape[0]
     img_dev = grads_ref.shape[0]
     half = owned_ref.shape[2]
     sent = owned_ref.shape[1] - CHUNK
     room = sent // (2 * CHUNK)
     quarters = parts // TILES
-    slots, _ = plan(docs, counts, tiles, img_dev)
+    slots = read_plan(plan, slot_count)
     for img in range(img_dev):
         cited, start, rank = own_image(slots, lax.axis_index("seq"), img)
         place = jnp.int32(img) if room == img_dev else rank
@@ -271,7 +300,9 @@
             to = chunk_rows(tile * quarters + part % quarters)
             for cols, row in ((slice(0, half), place), (slice(half, 2 * half), place + room)):
                 grads = owned_ref[part, chunk_rows(row), :].astype(F32)
-                grads_ref[img, to, cols] = jnp.where(cited, grads, jnp.zeros_like(grads))
+                if room < img_dev:
+                    grads = jnp.where(cited, grads, jnp.zeros_like(grads))
+                grads_ref[img, to, cols] = grads
     total = owned_ref[0, sent:, :].astype(F32)
     for part in range(1, parts):
         total = total + owned_ref[part, sent:, :].astype(F32)
@@ -317,7 +348,7 @@
     return jax.ShapeDtypeStruct(shape, F32)
 
 
-def after_scatter(blocks, room, img_dev, queries, grad_out, chunks, gate, *lists):
+def after_scatter(slots, blocks, room, img_dev, queries, grad_out, chunks, gate, plan):
     tok, width = queries.shape
     parts, _, kv_width = chunks.shape
     head_dim = kv_width // 2
@@ -326,10 +357,10 @@
     sent = blocks * CHUNK
 
     cited = call(
-        select_kernel,
+        functools.partial(select_kernel, slots),
         "select_cited",
         low(parts, sent, kv_width),
-        lists,
+        (plan,),
         (chunks,),
         [pltpu.VMEM((sent, kv_width), BF16)],
     )
@@ -342,7 +373,7 @@
         (queries, grad_out),
     )
     attn_t, dquery_t, partial, gate_sum = call(
-        functools.partial(attention_kernel, img_dev),
+        attention_kernel,
         "attention",
         (
             full(head_dim, rows),
@@ -350,7 +381,7 @@
             low(parts, sent, kv_width),
             full(8, 128),
         ),
-        (*lists, gate),
+        (plan, gate),
         (kv_cited, *prepared),
         [
             pltpu.VMEM((keys, kv_width), BF16),
@@ -369,20 +400,20 @@
     )
     gate_sum = sum_over(gate_sum, "dp")
     summed = call(
-        functools.partial(sum_kernel, img_dev),
+        functools.partial(sum_kernel, slots, img_dev),
         "sum_partials",
         low(parts, (2 * room + 1) * CHUNK, head_dim),
-        lists,
+        (plan,),
         (partial, gate_sum),
         [pltpu.VMEM((sent, kv_width), BF16)],
     )
     owned = lax.all_to_all(summed, "seq", 0, 0)
     norm_factor = float(lax.axis_size("dp") * tok * parts * width) ** (-0.5)
     grads, grad_gate = call(
-        functools.partial(unpack_kernel, norm_factor),
+        functools.partial(unpack_kernel, slots, norm_factor),
         "unpack_grads",
         (full(img_dev, parts * CHUNK, kv_width), full(1)),
-        (*lists, gate),
+        (plan, gate),
         (owned,),
         out_specs=(VMEM(), SMEM()),
     )
@@ -393,17 +424,27 @@
     img_dev, img_tok, kv_width = image_kv.shape
     parts = lax.axis_size("seq")
     slots = doc_images.shape[1]
-    lists = (doc_images.T, doc_counts, image_tiles)
-    chunks = call(
+    chunks, plan = pl.pallas_call(
         pack_kernel,
-        "pack_chunks",
-        low(parts, img_dev * CHUNK, kv_width),
-        lists,
-        (image_kv,),
-    )
+        out_shape=(
+            low(parts, img_dev * CHUNK, kv_width),
+            jax.ShapeDtypeStruct(((len(FIELDS) + 1) * STRIDE,), jnp.int32),
+        ),
+        in_specs=[pl.BlockSpec(memory_space=pltpu.HBM)] * 4,
+        out_specs=(VMEM(), SMEM()),
+        scratch_shapes=[
+            pltpu.SMEM((slots, doc_counts.shape[0]), jnp.int32),
+            pltpu.SMEM(doc_counts.shape, jnp.int32),
+            pltpu.SMEM(image_tiles.shape, jnp.int32),
+            pltpu.VMEM(image_kv.shape, BF16),
+            pltpu.SemaphoreType.DMA((4,)),
+        ],
+        compiler_params=pltpu.CompilerParams(vmem_limit_bytes=60 * 1024 * 1024),
+        name="pack_chunks",
+    )(doc_images.T, doc_counts, image_tiles, image_kv)
     chunks = lax.all_to_all(chunks, "seq", 0, 0)
     gated, dquery, grads, grad_gate = after_scatter(
-        slots, img_dev, img_dev, queries[0], grad_out[0], chunks, gate, *lists
+        slots, slots, img_dev, img_dev, queries[0], grad_out[0], chunks, gate, plan
     )
     return gated[None], dquery[None], grads, grad_gate
 

time: 89.8 us -> 88.9 us (0.990)
  local copies, waits for them, and re-layouts: 3.08 us -> 0.66 us
  starting transfers between devices: 24.6 us -> 26.3 us
  Pallas kernels: 12.1 us -> 11.2 us
    pallas_call x7 -> x6, Pallas kernels: 12.1 us -> 9.26 us  [call(): pl.pallas_call(kernel, out_shape=outs, in_specs=[SMEM()] * len(smem) + [V...]
    unnamed x16 -> x6, local copies, waits for them, and re-layouts: 3.08 us -> 0.66 us
    pallas_call x0 -> x1, Pallas kernels: none -> 1.96 us  [per_device(): pl.pallas_call(pack_kernel, out_shape=(low(parts, img_dev * CHUNK, kv_wid...]
    ppermute x6, starting transfers between devices: 10.2 us -> 11.8 us  [moved(): return lax.ppermute(x, axis, [(i, i ^ step) for i in range(size)])]
where the time goes in v5:
time: 88.9 us; the launch traced here: 88 us
  waiting for transfers between devices  29.8 us (34%)
  starting transfers between devices  26.3 us (30%)
  blocking collectives  18.5 us (21%)
  Pallas kernels  11.2 us (13%)
  between operations  1.37 us (2%)
    all_to_all x1, blocking collectives, per_device(): chunks = lax.all_to_all(chunks, 'seq', 0, 0)  18.5 us
    all_to_all x1, waiting for transfers between devices, after_scatter(): kv_cited = lax.all_to_all(cited, 'seq', 0, 0)  12.3 us
    ppermute x6, starting transfers between devices, moved(): return lax.ppermute(x, axis, [(i, i ^ step) for i in range(size)])  11.8 us
    all_to_all x1, waiting for transfers between devices, after_scatter(): owned = lax.all_to_all(summed, 'seq', 0, 0)  10.7 us
    pallas_call x6, Pallas kernels, call(): pl.pallas_call(kernel, out_shape=outs, in_specs=[SMEM()] * len(smem) + [V...  9.26 us
    all_to_all x1, starting transfers between devices, after_scatter(): owned = lax.all_to_all(summed, 'seq', 0, 0)  7.11 us
    ppermute x6, waiting for transfers between devices, moved(): return lax.ppermute(x, axis, [(i, i ^ step) for i in range(size)])  6.9 us
    all_to_all x1, starting transfers between devices, after_scatter(): kv_cited = lax.all_to_all(cited, 'seq', 0, 0)  3.75 us
  transfers between devices with their start and end apart: 9, of which 5 were waited for; matrix products, arithmetic and copies ran while one was open for 0% of the time, Pallas kernels for 1%

profile of v5, /device:TPU:32, one launch (start us, length us, event | category | flops | bytes accessed | tf_op | source)
XLA Modules:
  0.0 88.0 jit_solution(15880613309342896784)
XLA Ops:
  0.6 2.0 %pack_chunks.1 = (bf16[16,64,256]{2,1,0:T(8,128)(2,1)}, s32[56]{0:T(128)}) custom-call(s32[6,16]{1,0:T(8,128)} %bitcast.7, s32[16]{0:T(128)} %counts_hbm.1, s32[1024]{0:T(1024)} %tiles_hbm.1, bf16[4,256,256]{2,1,0:T(8,128)(2,1)} %image_hbm.1), custom_call_target="tpu_custom_call" | custom-call | tf_op jit(solution)/shard_map/pack_chunks/pallas_call | solution.py:427
  2.6 18.5 %all_to_all.20.chunks_ref = bf16[16,64,256]{2,1,0:T(8,128)(2,1)S(1)} all-to-all(bf16[16,64,256]{2,1,0:T(8,128)(2,1)} %get-tuple-element.18), channel_id=1, replica_groups=mesh['dp'=16,'seq'=16] {'seq'}, dimensions={0} | all-to-all | bytes 1048576 | tf_op jit(solution)/shard_map/all_to_all | solution.py:445
  21.1 0.7 copy-done.2
  21.8 1.5 %select_cited.1 = bf16[16,96,256]{2,1,0:T(8,128)(2,1)} custom-call(s32[56]{0:T(128)S(1)} %copy-done.2, bf16[16,64,256]{2,1,0:T(8,128)(2,1)S(1)} %all_to_all.20.chunks_ref), custom_call_target="tpu_custom_call" | custom-call | tf_op jit(solution)/shard_map/select_cited/pallas_call | solution.py:332
  23.3 3.7 %all-to-all-start.1 = ((bf16[16,96,256]{2,1,0:T(8,128)(2,1)}), bf16[16,96,256]{2,1,0:T(8,128)(2,1)S(1)}, u32[]{:S(2)}, u32[]{:S(2)}) async-start(bf16[16,96,256]{2,1,0:T(8,128)(2,1)} %select_cited.1), calls=%async_computation.1 | async-start | bytes 1572864 | tf_op jit(solution)/shard_map/all_to_all | solution.py:367
  27.8 0.1 prepare_rows.1
  27.9 12.3 %all-to-all-done.1.kv_ref = bf16[16,96,256]{2,1,0:T(8,128)(2,1)S(1)} async-done(((bf16[16,96,256]{2,1,0:T(8,128)(2,1)}), bf16[16,96,256]{2,1,0:T(8,128)(2,1)S(1)}, u32[]{:S(2)}, u32[]{:S(2)}) %all-to-all-start.1) | async-done | bytes 786464 | tf_op jit(solution)/shard_map/all_to_all | solution.py:367
  40.2 3.2 %attention.1 = (f32[128,1024]{1,0:T(8,128)S(1)}, f32[128,1024]{1,0:T(8,128)S(1)}, bf16[16,96,256]{2,1,0:T(8,128)(2,1)}, f32[8,128]{1,0:T(8,128)S(1)}) custom-call(s32[56]{0:T(128)S(1)} %copy-done.2, f32[1]{0:T(128)S(6)} %copy.11.gate, bf16[16,96,256]{2,1,0:T(8,128)(2,1)S(1)} %all-to-all-done.1.kv_ref, bf16[1024,128]{1,0:T(8,128)(2,1)S(1)} %get-tuple-element.19.query_rows, ...), custom_call_target="tpu_custom_call" | custom-call | tf_op jit(solution)/shard_map/attention/pallas_call | solution.py:332
  43.4 3.6 %all-to-all-start.2 = ((bf16[16,96,256]{2,1,0:T(8,128)(2,1)}), bf16[16,96,256]{2,1,0:T(8,128)(2,1)S(1)}, u32[]{:S(2)}, u32[]{:S(2)}) async-start(bf16[16,96,256]{2,1,0:T(8,128)(2,1)} %get-tuple-element.26), calls=%async_computation.2 | async-start | bytes 1572864 | tf_op jit(solution)/shard_map/all_to_all | solution.py:397
  47.0 0.1 collective-permute-start.2
  47.1 1.7 %collective-permute-start.1 = (f32[8,128]{1,0:T(8,128)S(1)}, f32[8,128]{1,0:T(8,128)S(1)}, u32[]{:S(2)}, u32[]{:S(2)}) collective-permute-start(f32[8,128]{1,0:T(8,128)S(1)} %get-tuple-element.27), channel_id=1, source_target_pairs={{0,32},{16,48},{32,0},{48,16},{64,96},{80,112},{96,64},{112,80},{1... | collective-permute-start | bytes 12296 | tf_op jit(solution)/shard_map/ppermute | solution.py:318
  48.8 0.2 collective-permute-start
  49.0 1.2 %collective-permute-done.2 = f32[8,128]{1,0:T(8,128)S(1)} collective-permute-done((f32[8,128]{1,0:T(8,128)S(1)}, f32[8,128]{1,0:T(8,128)S(1)}, u32[]{:S(2)}, u32[]{:S(2)}) %collective-permute-start.2) | collective-permute-done | bytes 4128 | tf_op jit(solution)/shard_map/ppermute | solution.py:318
  50.1 0.7 collective-permute-done.1
  50.8 7.4 %collective-permute-start.5 = (f32[8,128]{1,0:T(8,128)S(1)}, f32[8,128]{1,0:T(8,128)S(1)}, u32[]{:S(2)}, u32[]{:S(2)}) collective-permute-start(f32[8,128]{1,0:T(8,128)S(1)} %add_add_fusion.1), channel_id=1, source_target_pairs={{0,192},{16,208},{32,224},{48,240},{64,128},{80,144},{96,160},{112... | collective-permute-start | bytes 12296 | tf_op jit(solution)/shard_map/ppermute | solution.py:318
  58.3 0.5 collective-permute-start.4
  58.8 1.9 %collective-permute-start.3 = (f32[8,128]{1,0:T(8,128)S(1)}, f32[8,128]{1,0:T(8,128)S(1)}, u32[]{:S(2)}, u32[]{:S(2)}) collective-permute-start(f32[8,128]{1,0:T(8,128)S(1)} %add_add_fusion.1), channel_id=1, source_target_pairs={{0,64},{16,80},{32,96},{48,112},{64,0},{80,16},{96,32},{112,48},{1... | collective-permute-start | bytes 12296 | tf_op jit(solution)/shard_map/ppermute | solution.py:318
  60.7 0.0 collective-permute-done.5
  60.7 5.0 %collective-permute-done.4 = f32[8,128]{1,0:T(8,128)S(1)} collective-permute-done((f32[8,128]{1,0:T(8,128)S(1)}, f32[8,128]{1,0:T(8,128)S(1)}, u32[]{:S(2)}, u32[]{:S(2)}) %collective-permute-start.4) | collective-permute-done | bytes 4128 | tf_op jit(solution)/shard_map/ppermute | solution.py:318
  65.8 1.6 %sum_partials.1 = bf16[16,144,128]{2,1,0:T(8,128)(2,1)} custom-call(s32[56]{0:T(128)S(1)} %copy-done.2, bf16[16,96,256]{2,1,0:T(8,128)(2,1)S(1)} %all-to-all-done.2.partial_ref, f32[8,128]{1,0:T(8,128)S(1)} %add_add_fusion.gate_ref), custom_call_target="tpu_custom_call" | custom-call | tf_op jit(solution)/shard_map/sum_partials/pallas_call | solution.py:332
  67.4 7.1 %all-to-all-start.3 = ((bf16[16,144,128]{2,1,0:T(8,128)(2,1)}), bf16[16,144,128]{2,1,0:T(8,128)(2,1)S(1)}, u32[]{:S(2)}, u32[]{:S(2)}) async-start(bf16[16,144,128]{2,1,0:T(8,128)(2,1)} %sum_partials.1), calls=%async_computation.3 | async-start | bytes 1179648 | tf_op jit(solution)/shard_map/all_to_all | solution.py:410
  74.5 1.1 %finish_rows.1 = (bf16[128,1024]{1,0:T(8,128)(2,1)}, bf16[128,1024]{1,0:T(8,128)(2,1)}) custom-call(f32[1]{0:T(128)S(6)} %copy.11.gate, f32[128,1024]{1,0:T(8,128)S(1)} %get-tuple-element.22.attn_t, f32[128,1024]{1,0:T(8,128)S(1)} %get-tuple-element.23.dquery_t), custom_call_target="tpu_custom_call" | custom-call | tf_op jit(solution)/shard_map/finish_rows/pallas_call | solution.py:332
  75.6 10.7 %all-to-all-done.3.owned_ref = bf16[16,144,128]{2,1,0:T(8,128)(2,1)S(1)} async-done(((bf16[16,144,128]{2,1,0:T(8,128)(2,1)}), bf16[16,144,128]{2,1,0:T(8,128)(2,1)S(1)}, u32[]{:S(2)}, u32[]{:S(2)}) %all-to-all-start.3) | async-done | bytes 589856 | tf_op jit(solution)/shard_map/all_to_all | solution.py:410
  86.3 1.7 %unpack_grads.1 = (f32[4,256,256]{2,1,0:T(8,128)}, f32[1]{0:T(128)}) custom-call(s32[56]{0:T(128)S(1)} %copy-done.2, f32[1]{0:T(128)S(6)} %copy.11.gate, bf16[16,144,128]{2,1,0:T(8,128)(2,1)S(1)} %all-to-all-done.3.owned_ref), custom_call_target="tpu_custom_call" | custom-call | tf_op jit(solution)/shard_map/unpack_grads/pallas_call | solution.py:332
  (10 shorter events, 0.0 us)
Async XLA Ops:
  21.1 0.7 copy-start.2
  23.3 4.4 %copy-start = (bf16[1,128,1024]{2,1,0:T(8,128)(2,1)S(1)}, bf16[1,128,1024]{2,1,0:T(8,128)(2,1)}, u32[]{:S(2)}) copy-start(bf16[1,128,1024]{2,1,0:T(8,128)(2,1)} %param.7) | copy-start | bytes 786436
  23.3 4.4 %copy-start.1 = (bf16[1,128,1024]{2,1,0:T(8,128)(2,1)S(1)}, bf16[1,128,1024]{2,1,0:T(8,128)(2,1)}, u32[]{:S(2)}) copy-start(bf16[1,128,1024]{2,1,0:T(8,128)(2,1)} %param.8) | copy-start | bytes 786436
  23.3 16.8 %all-to-all-start.1 = ((bf16[16,96,256]{2,1,0:T(8,128)(2,1)}), bf16[16,96,256]{2,1,0:T(8,128)(2,1)S(1)}, u32[]{:S(2)}, u32[]{:S(2)}) async-start(bf16[16,96,256]{2,1,0:T(8,128)(2,1)} %select_cited.1), calls=%async_computation.1 | async-start | bytes 1572864 | tf_op jit(solution)/shard_map/all_to_all | solution.py:367
  43.4 22.4 %all-to-all-start.2 = ((bf16[16,96,256]{2,1,0:T(8,128)(2,1)}), bf16[16,96,256]{2,1,0:T(8,128)(2,1)S(1)}, u32[]{:S(2)}, u32[]{:S(2)}) async-start(bf16[16,96,256]{2,1,0:T(8,128)(2,1)} %get-tuple-element.26), calls=%async_computation.2 | async-start | bytes 1572864 | tf_op jit(solution)/shard_map/all_to_all | solution.py:397
  47.0 3.1 %collective-permute-start.2 = (f32[8,128]{1,0:T(8,128)S(1)}, f32[8,128]{1,0:T(8,128)S(1)}, u32[]{:S(2)}, u32[]{:S(2)}) collective-permute-start(f32[8,128]{1,0:T(8,128)S(1)} %get-tuple-element.27), channel_id=1, source_target_pairs={{0,48},{16,32},{32,16},{48,0},{64,112},{80,96},{96,80},{112,64},{1... | collective-permute-start | bytes 12296 | tf_op jit(solution)/shard_map/ppermute | solution.py:318
  47.1 3.7 %collective-permute-start.1 = (f32[8,128]{1,0:T(8,128)S(1)}, f32[8,128]{1,0:T(8,128)S(1)}, u32[]{:S(2)}, u32[]{:S(2)}) collective-permute-start(f32[8,128]{1,0:T(8,128)S(1)} %get-tuple-element.27), channel_id=1, source_target_pairs={{0,32},{16,48},{32,0},{48,16},{64,96},{80,112},{96,64},{112,80},{1... | collective-permute-start | bytes 12296 | tf_op jit(solution)/shard_map/ppermute | solution.py:318
  48.8 2.0 %collective-permute-start = (f32[8,128]{1,0:T(8,128)S(1)}, f32[8,128]{1,0:T(8,128)S(1)}, u32[]{:S(2)}, u32[]{:S(2)}) collective-permute-start(f32[8,128]{1,0:T(8,128)S(1)} %get-tuple-element.27), channel_id=1, source_target_pairs={{0,16},{16,0},{32,48},{48,32},{64,80},{80,64},{96,112},{112,96},{1... | collective-permute-start | bytes 12296 | tf_op jit(solution)/shard_map/ppermute | solution.py:318
  50.8 9.9 %collective-permute-start.5 = (f32[8,128]{1,0:T(8,128)S(1)}, f32[8,128]{1,0:T(8,128)S(1)}, u32[]{:S(2)}, u32[]{:S(2)}) collective-permute-start(f32[8,128]{1,0:T(8,128)S(1)} %add_add_fusion.1), channel_id=1, source_target_pairs={{0,192},{16,208},{32,224},{48,240},{64,128},{80,144},{96,160},{112... | collective-permute-start | bytes 12296 | tf_op jit(solution)/shard_map/ppermute | solution.py:318
  58.3 7.5 %collective-permute-start.4 = (f32[8,128]{1,0:T(8,128)S(1)}, f32[8,128]{1,0:T(8,128)S(1)}, u32[]{:S(2)}, u32[]{:S(2)}) collective-permute-start(f32[8,128]{1,0:T(8,128)S(1)} %add_add_fusion.1), channel_id=1, source_target_pairs={{0,128},{16,144},{32,160},{48,176},{64,192},{80,208},{96,224},{112... | collective-permute-start | bytes 12296 | tf_op jit(solution)/shard_map/ppermute | solution.py:318
  58.8 7.0 %collective-permute-start.3 = (f32[8,128]{1,0:T(8,128)S(1)}, f32[8,128]{1,0:T(8,128)S(1)}, u32[]{:S(2)}, u32[]{:S(2)}) collective-permute-start(f32[8,128]{1,0:T(8,128)S(1)} %add_add_fusion.1), channel_id=1, source_target_pairs={{0,64},{16,80},{32,96},{48,112},{64,0},{80,16},{96,32},{112,48},{1... | collective-permute-start | bytes 12296 | tf_op jit(solution)/shard_map/ppermute | solution.py:318
  67.4 18.9 %all-to-all-start.3 = ((bf16[16,144,128]{2,1,0:T(8,128)(2,1)}), bf16[16,144,128]{2,1,0:T(8,128)(2,1)S(1)}, u32[]{:S(2)}, u32[]{:S(2)}) async-start(bf16[16,144,128]{2,1,0:T(8,128)(2,1)} %sum_partials.1), calls=%async_computation.3 | async-start | bytes 1179648 | tf_op jit(solution)/shard_map/all_to_all | solution.py:410

commit v6 on v5

--- a/solution.py
+++ b/solution.py
@@ -83,6 +83,8 @@
 
 
 def chunk_rows(index):
+    if isinstance(index, int):
+        return slice(index * CHUNK, (index + 1) * CHUNK)
     return pl.ds(pl.multiple_of(index * CHUNK, CHUNK), CHUNK)
 
 
@@ -134,7 +136,8 @@
         out_ref[part] = held[...]
 
 
-def prepare_kernel(gate, query_ref, cot_ref, query_rows, dattn_rows, cot_t):
+def prepare_kernel(gate, plan, query_ref, cot_ref, query_rows, dattn_rows, cot_t):
+    del plan
     tok = query_ref.shape[0]
     head_dim = query_rows.shape[1]
     tanh_gate = jnp.tanh(jnp.full((1, head_dim), gate[0], F32))
@@ -255,26 +258,25 @@
 
 def sum_kernel(slot_count, img_dev, plan, partial_ref, gate_ref, out_ref, sums):
     parts = partial_ref.shape[0]
-    half = out_ref.shape[2]
+    width = out_ref.shape[2]
     sent = out_ref.shape[1] - CHUNK
-    room = sent // (2 * CHUNK)
+    room = sent // CHUNK
     for number in range(partial_ref.shape[1] // CHUNK):
         at = slice(number * CHUNK, (number + 1) * CHUNK)
         total = partial_ref[0, at, :].astype(F32)
         for part in range(1, parts):
             total = total + partial_ref[part, at, :].astype(F32)
         sums[at, :] = total.astype(BF16)
-    out_ref[:, :sent, :] = jnp.zeros((parts, sent, half), BF16)
+    out_ref[:, :sent, :] = jnp.zeros((parts, sent, width), BF16)
     slots = read_plan(plan, slot_count)
     for slot, here, number in held_chunks(slots, parts // TILES):
 
         @pl.when(here)
         def _(slot=slot, number=number):
             place = position(slot, img_dev, room)
-            out_ref[slot.owner, chunk_rows(place), :] = sums[chunk_rows(number), :half]
-            out_ref[slot.owner, chunk_rows(place + room), :] = sums[chunk_rows(number), half:]
-
-    term = jnp.broadcast_to(gate_ref[0:1, :], (CHUNK, half))
+            out_ref[slot.owner, chunk_rows(place), :] = sums[chunk_rows(number), :]
+
+    term = jnp.broadcast_to(gate_ref[0:1, 0:1], (CHUNK, width))
     high = term.astype(BF16).astype(F32)
     middle = (term - high).astype(BF16).astype(F32)
     low = term - high - middle
@@ -287,22 +289,20 @@
 def unpack_kernel(slot_count, norm_factor, plan, gate, owned_ref, grads_ref, gate_ref):
     parts = owned_ref.shape[0]
     img_dev = grads_ref.shape[0]
-    half = owned_ref.shape[2]
     sent = owned_ref.shape[1] - CHUNK
-    room = sent // (2 * CHUNK)
+    room = sent // CHUNK
     quarters = parts // TILES
     slots = read_plan(plan, slot_count)
     for img in range(img_dev):
         cited, start, rank = own_image(slots, lax.axis_index("seq"), img)
-        place = jnp.int32(img) if room == img_dev else rank
+        place = img if room == img_dev else rank
         for part in range(parts):
             tile = tile_of(part // quarters, start)
             to = chunk_rows(tile * quarters + part % quarters)
-            for cols, row in ((slice(0, half), place), (slice(half, 2 * half), place + room)):
-                grads = owned_ref[part, chunk_rows(row), :].astype(F32)
-                if room < img_dev:
-                    grads = jnp.where(cited, grads, jnp.zeros_like(grads))
-                grads_ref[img, to, cols] = grads
+            grads = owned_ref[part, chunk_rows(place), :].astype(F32)
+            if room < img_dev:
+                grads = jnp.where(cited, grads, jnp.zeros_like(grads))
+            grads_ref[img, to, :] = grads
     total = owned_ref[0, sent:, :].astype(F32)
     for part in range(1, parts):
         total = total + owned_ref[part, sent:, :].astype(F32)
@@ -328,7 +328,7 @@
     return x
 
 
-def call(kernel, name, outs, smem, vmem, scratch=(), vmem_mib=6, out_specs=None):
+def call(kernel, name, outs, smem, vmem, scratch=(), vmem_mib=3, out_specs=None):
     return pl.pallas_call(
         kernel,
         out_shape=outs,
@@ -348,8 +348,7 @@
     return jax.ShapeDtypeStruct(shape, F32)
 
 
-def after_scatter(slots, blocks, room, img_dev, queries, grad_out, chunks, gate, plan):
-    tok, width = queries.shape
+def after_scatter(slots, blocks, room, img_dev, tok, width, prepared, chunks, gate, plan):
     parts, _, kv_width = chunks.shape
     head_dim = kv_width // 2
     rows = tok * (width // head_dim)
@@ -365,13 +364,6 @@
         [pltpu.VMEM((sent, kv_width), BF16)],
     )
     kv_cited = lax.all_to_all(cited, "seq", 0, 0)
-    prepared = call(
-        prepare_kernel,
-        "prepare_rows",
-        (low(rows, head_dim), low(rows, head_dim), full(head_dim, rows)),
-        (gate,),
-        (queries, grad_out),
-    )
     attn_t, dquery_t, partial, gate_sum = call(
         attention_kernel,
         "attention",
@@ -402,7 +394,7 @@
     summed = call(
         functools.partial(sum_kernel, slots, img_dev),
         "sum_partials",
-        low(parts, (2 * room + 1) * CHUNK, head_dim),
+        low(parts, (room + 1) * CHUNK, kv_width),
         (plan,),
         (partial, gate_sum),
         [pltpu.VMEM((sent, kv_width), BF16)],
@@ -421,7 +413,10 @@
 
 
 def per_device(queries, grad_out, image_kv, image_tiles, doc_images, doc_counts, gate):
-    img_dev, img_tok, kv_width = image_kv.shape
+    _, tok, width = queries.shape
+    img_dev, _, kv_width = image_kv.shape
+    head_dim = kv_width // 2
+    rows = tok * (width // head_dim)
     parts = lax.axis_size("seq")
     slots = doc_images.shape[1]
     chunks, plan = pl.pallas_call(
@@ -443,8 +438,16 @@
         name="pack_chunks",
     )(doc_images.T, doc_counts, image_tiles, image_kv)
     chunks = lax.all_to_all(chunks, "seq", 0, 0)
+    prepared = call(
+        prepare_kernel,
+        "prepare_rows",
+        (low(rows, head_dim), low(rows, head_dim), full(head_dim, rows)),
+        (gate, plan),
+        (queries[0], grad_out[0]),
+    )
+    chunks, prepared = lax.optimization_barrier((chunks, prepared))
     gated, dquery, grads, grad_gate = after_scatter(
-        slots, slots, img_dev, img_dev, queries[0], grad_out[0], chunks, gate, plan
+        slots, slots, img_dev, img_dev, tok, width, prepared, chunks, gate, plan
     )
     return gated[None], dquery[None], grads, grad_gate
 

time: 88.9 us -> 85.4 us (0.961)
  waiting for transfers between devices: 29.8 us -> 25.5 us
  Pallas kernels: 11.2 us -> 13.9 us
  blocking collectives: 18.5 us -> 16.2 us
    all_to_all x1, starting transfers between devices: 3.75 us -> 7.18 us  [per_device(): chunks = lax.all_to_all(chunks, 'seq', 0, 0)]
    ppermute x6, starting transfers between devices: 11.8 us -> 8.52 us  [moved(): return lax.ppermute(x, axis, [(i, i ^ step) for i in range(size)])]
    all_to_all x1, waiting for transfers between devices: 12.3 us -> 9.5 us  [per_device(): chunks = lax.all_to_all(chunks, 'seq', 0, 0)]
    pallas_call x6, Pallas kernels: 9.26 us -> 12 us  [call(): pl.pallas_call(kernel, out_shape=outs, in_specs=[SMEM()] * len(smem) + [V...]
    all_to_all x1, blocking collectives: 18.5 us -> 16.2 us  [after_scatter(): kv_cited = lax.all_to_all(cited, 'seq', 0, 0)]
    ppermute x6, waiting for transfers between devices: 6.9 us -> 5.29 us  [moved(): return lax.ppermute(x, axis, [(i, i ^ step) for i in range(size)])]
  transfers between devices with their start and end apart: 9 -> 9, of which waited for: 5 -> 5; matrix products, arithmetic and copies ran while one was open for 0% -> 0% of each run, Pallas kernels for 1% -> 2%
where the time goes in v6:
time: 85.4 us; the launch traced here: 84.1 us
  starting transfers between devices  26.5 us (31%)
  waiting for transfers between devices  25.5 us (30%)
  blocking collectives  16.2 us (19%)
  Pallas kernels  13.9 us (16%)
  between operations  1.4 us (2%)
    all_to_all x1, blocking collectives, after_scatter(): kv_cited = lax.all_to_all(cited, 'seq', 0, 0)  16.2 us
    pallas_call x6, Pallas kernels, call(): pl.pallas_call(kernel, out_shape=outs, in_specs=[SMEM()] * len(smem) + [V...  12 us
    all_to_all x1, waiting for transfers between devices, after_scatter(): owned = lax.all_to_all(summed, 'seq', 0, 0)  10.7 us
    all_to_all x1, waiting for transfers between devices, per_device(): chunks = lax.all_to_all(chunks, 'seq', 0, 0)  9.5 us
    ppermute x6, starting transfers between devices, moved(): return lax.ppermute(x, axis, [(i, i ^ step) for i in range(size)])  8.52 us
    all_to_all x1, starting transfers between devices, per_device(): chunks = lax.all_to_all(chunks, 'seq', 0, 0)  7.18 us
    all_to_all x1, starting transfers between devices, after_scatter(): owned = lax.all_to_all(summed, 'seq', 0, 0)  7.12 us
    ppermute x6, waiting for transfers between devices, moved(): return lax.ppermute(x, axis, [(i, i ^ step) for i in range(size)])  5.29 us
  transfers between devices with their start and end apart: 9, of which 5 were waited for; matrix products, arithmetic and copies ran while one was open for 0% of the time, Pallas kernels for 2%

profile of v6, /device:TPU:32, one launch (start us, length us, event | category | flops | bytes accessed | tf_op | source)
XLA Modules:
  0.0 84.1 jit_solution(6452345245992285226)
XLA Ops:
  0.6 2.0 %pack_chunks.1 = (bf16[16,64,256]{2,1,0:T(8,128)(2,1)}, s32[56]{0:T(128)}) custom-call(s32[6,16]{1,0:T(8,128)} %bitcast.7, s32[16]{0:T(128)} %counts_hbm.1, s32[1024]{0:T(1024)} %tiles_hbm.1, bf16[4,256,256]{2,1,0:T(8,128)(2,1)} %image_hbm.1), custom_call_target="tpu_custom_call" | custom-call | tf_op jit(solution)/shard_map/pack_chunks/pallas_call | solution.py:422
  2.6 0.0 copy-start.1
  2.6 7.2 %all-to-all-start = ((bf16[16,64,256]{2,1,0:T(8,128)(2,1)}), bf16[16,64,256]{2,1,0:T(8,128)(2,1)S(1)}, u32[]{:S(2)}, u32[]{:S(2)}) async-start(bf16[16,64,256]{2,1,0:T(8,128)(2,1)} %get-tuple-element.22), calls=%async_computation | async-start | bytes 1048576 | tf_op jit(solution)/shard_map/all_to_all | solution.py:440
  10.5 0.6 copy-done.2
  11.1 0.7 prepare_rows.1
  11.8 9.5 %all-to-all-done.chunks_ref = bf16[16,64,256]{2,1,0:T(8,128)(2,1)S(1)} async-done(((bf16[16,64,256]{2,1,0:T(8,128)(2,1)}), bf16[16,64,256]{2,1,0:T(8,128)(2,1)S(1)}, u32[]{:S(2)}, u32[]{:S(2)}) %all-to-all-start) | async-done | bytes 524320 | tf_op jit(solution)/shard_map/all_to_all | solution.py:440
  21.3 0.7 select_cited.1
  22.0 16.2 %all_to_all.20.kv_ref = bf16[16,96,256]{2,1,0:T(8,128)(2,1)S(1)} all-to-all(bf16[16,96,256]{2,1,0:T(8,128)(2,1)S(1)} %select_cited.1), channel_id=1, replica_groups=mesh['dp'=16,'seq'=16] {'seq'}, dimensions={0} | all-to-all | bytes 1572864 | tf_op jit(solution)/shard_map/all_to_all | solution.py:366
  38.2 6.2 %attention.1 = (f32[128,1024]{1,0:T(8,128)S(1)}, f32[128,1024]{1,0:T(8,128)S(1)}, bf16[16,96,256]{2,1,0:T(8,128)(2,1)}, f32[8,128]{1,0:T(8,128)S(1)}) custom-call(s32[56]{0:T(128)S(1)} %copy-done.2, f32[1]{0:T(128)S(6)} %copy.11.gate, bf16[16,96,256]{2,1,0:T(8,128)(2,1)S(1)} %all_to_all.20.kv_ref, bf16[1024,128]{1,0:T(8,128)(2,1)S(1)} %get-tuple-element.27.query_rows, ...), custom_call_target="tpu_custom_call" | custom-call | tf_op jit(solution)/shard_map/attention/pallas_call | solution.py:332
  44.4 3.6 %all-to-all-start.2 = ((bf16[16,96,256]{2,1,0:T(8,128)(2,1)}), bf16[16,96,256]{2,1,0:T(8,128)(2,1)S(1)}, u32[]{:S(2)}, u32[]{:S(2)}) async-start(bf16[16,96,256]{2,1,0:T(8,128)(2,1)} %get-tuple-element.34), calls=%async_computation.2 | async-start | bytes 1572864 | tf_op jit(solution)/shard_map/all_to_all | solution.py:389
  48.1 0.1 collective-permute-start.2
  48.2 1.7 %collective-permute-start.1 = (f32[8,128]{1,0:T(8,128)S(1)}, f32[8,128]{1,0:T(8,128)S(1)}, u32[]{:S(2)}, u32[]{:S(2)}) collective-permute-start(f32[8,128]{1,0:T(8,128)S(1)} %get-tuple-element.35), channel_id=1, source_target_pairs={{0,32},{16,48},{32,0},{48,16},{64,96},{80,112},{96,64},{112,80},{1... | collective-permute-start | bytes 12296 | tf_op jit(solution)/shard_map/ppermute | solution.py:318
  49.9 0.2 collective-permute-start
  50.0 1.2 %collective-permute-done.2 = f32[8,128]{1,0:T(8,128)S(1)} collective-permute-done((f32[8,128]{1,0:T(8,128)S(1)}, f32[8,128]{1,0:T(8,128)S(1)}, u32[]{:S(2)}, u32[]{:S(2)}) %collective-permute-start.2) | collective-permute-done | bytes 4128 | tf_op jit(solution)/shard_map/ppermute | solution.py:318
  51.2 0.7 collective-permute-done.1
  51.9 2.5 %collective-permute-start.5 = (f32[8,128]{1,0:T(8,128)S(1)}, f32[8,128]{1,0:T(8,128)S(1)}, u32[]{:S(2)}, u32[]{:S(2)}) collective-permute-start(f32[8,128]{1,0:T(8,128)S(1)} %add_add_fusion.1), channel_id=1, source_target_pairs={{0,192},{16,208},{32,224},{48,240},{64,128},{80,144},{96,160},{112... | collective-permute-start | bytes 12296 | tf_op jit(solution)/shard_map/ppermute | solution.py:318
  54.4 1.5 %collective-permute-start.4 = (f32[8,128]{1,0:T(8,128)S(1)}, f32[8,128]{1,0:T(8,128)S(1)}, u32[]{:S(2)}, u32[]{:S(2)}) collective-permute-start(f32[8,128]{1,0:T(8,128)S(1)} %add_add_fusion.1), channel_id=1, source_target_pairs={{0,128},{16,144},{32,160},{48,176},{64,192},{80,208},{96,224},{112... | collective-permute-start | bytes 12296 | tf_op jit(solution)/shard_map/ppermute | solution.py:318
  55.9 2.6 %collective-permute-start.3 = (f32[8,128]{1,0:T(8,128)S(1)}, f32[8,128]{1,0:T(8,128)S(1)}, u32[]{:S(2)}, u32[]{:S(2)}) collective-permute-start(f32[8,128]{1,0:T(8,128)S(1)} %add_add_fusion.1), channel_id=1, source_target_pairs={{0,64},{16,80},{32,96},{48,112},{64,0},{80,16},{96,32},{112,48},{1... | collective-permute-start | bytes 12296 | tf_op jit(solution)/shard_map/ppermute | solution.py:318
  58.5 3.4 %collective-permute-done.4 = f32[8,128]{1,0:T(8,128)S(1)} collective-permute-done((f32[8,128]{1,0:T(8,128)S(1)}, f32[8,128]{1,0:T(8,128)S(1)}, u32[]{:S(2)}, u32[]{:S(2)}) %collective-permute-start.4) | collective-permute-done | bytes 4128 | tf_op jit(solution)/shard_map/ppermute | solution.py:318
  61.9 1.6 %sum_partials.1 = bf16[16,80,256]{2,1,0:T(8,128)(2,1)} custom-call(s32[56]{0:T(128)S(1)} %copy-done.2, bf16[16,96,256]{2,1,0:T(8,128)(2,1)S(1)} %all-to-all-done.2.partial_ref, f32[8,128]{1,0:T(8,128)S(1)} %add_add_fusion.gate_ref), custom_call_target="tpu_custom_call" | custom-call | tf_op jit(solution)/shard_map/sum_partials/pallas_call | solution.py:332
  63.5 7.1 %all-to-all-start.3 = ((bf16[16,80,256]{2,1,0:T(8,128)(2,1)}), bf16[16,80,256]{2,1,0:T(8,128)(2,1)S(1)}, u32[]{:S(2)}, u32[]{:S(2)}) async-start(bf16[16,80,256]{2,1,0:T(8,128)(2,1)} %sum_partials.1), calls=%async_computation.3 | async-start | bytes 1310720 | tf_op jit(solution)/shard_map/all_to_all | solution.py:402
  70.7 1.1 %finish_rows.1 = (bf16[128,1024]{1,0:T(8,128)(2,1)}, bf16[128,1024]{1,0:T(8,128)(2,1)}) custom-call(f32[1]{0:T(128)S(6)} %copy.11.gate, f32[128,1024]{1,0:T(8,128)S(1)} %get-tuple-element.30.attn_t, f32[128,1024]{1,0:T(8,128)S(1)} %get-tuple-element.31.dquery_t), custom_call_target="tpu_custom_call" | custom-call | tf_op jit(solution)/shard_map/finish_rows/pallas_call | solution.py:332
  71.8 10.7 %all-to-all-done.3.owned_ref = bf16[16,80,256]{2,1,0:T(8,128)(2,1)S(1)} async-done(((bf16[16,80,256]{2,1,0:T(8,128)(2,1)}), bf16[16,80,256]{2,1,0:T(8,128)(2,1)S(1)}, u32[]{:S(2)}, u32[]{:S(2)}) %all-to-all-start.3) | async-done | bytes 655392 | tf_op jit(solution)/shard_map/all_to_all | solution.py:402
  82.5 1.7 %unpack_grads.1 = (f32[4,256,256]{2,1,0:T(8,128)}, f32[1]{0:T(128)}) custom-call(s32[56]{0:T(128)S(1)} %copy-done.2, f32[1]{0:T(128)S(6)} %copy.11.gate, bf16[16,80,256]{2,1,0:T(8,128)(2,1)S(1)} %all-to-all-done.3.owned_ref), custom_call_target="tpu_custom_call" | custom-call | tf_op jit(solution)/shard_map/unpack_grads/pallas_call | solution.py:332
  (10 shorter events, 0.0 us)
Async XLA Ops:
  2.6 7.9 %copy-start = (bf16[1,128,1024]{2,1,0:T(8,128)(2,1)S(1)}, bf16[1,128,1024]{2,1,0:T(8,128)(2,1)}, u32[]{:S(2)}) copy-start(bf16[1,128,1024]{2,1,0:T(8,128)(2,1)} %param.7) | copy-start | bytes 786436
  2.6 7.9 %copy-start.1 = (bf16[1,128,1024]{2,1,0:T(8,128)(2,1)S(1)}, bf16[1,128,1024]{2,1,0:T(8,128)(2,1)}, u32[]{:S(2)}) copy-start(bf16[1,128,1024]{2,1,0:T(8,128)(2,1)} %param.8) | copy-start | bytes 786436
  2.6 18.7 %all-to-all-start = ((bf16[16,64,256]{2,1,0:T(8,128)(2,1)}), bf16[16,64,256]{2,1,0:T(8,128)(2,1)S(1)}, u32[]{:S(2)}, u32[]{:S(2)}) async-start(bf16[16,64,256]{2,1,0:T(8,128)(2,1)} %get-tuple-element.22), calls=%async_computation | async-start | bytes 1048576 | tf_op jit(solution)/shard_map/all_to_all | solution.py:440
  10.5 0.7 copy-start.2
  44.4 17.5 %all-to-all-start.2 = ((bf16[16,96,256]{2,1,0:T(8,128)(2,1)}), bf16[16,96,256]{2,1,0:T(8,128)(2,1)S(1)}, u32[]{:S(2)}, u32[]{:S(2)}) async-start(bf16[16,96,256]{2,1,0:T(8,128)(2,1)} %get-tuple-element.34), calls=%async_computation.2 | async-start | bytes 1572864 | tf_op jit(solution)/shard_map/all_to_all | solution.py:389
  48.1 3.1 %collective-permute-start.2 = (f32[8,128]{1,0:T(8,128)S(1)}, f32[8,128]{1,0:T(8,128)S(1)}, u32[]{:S(2)}, u32[]{:S(2)}) collective-permute-start(f32[8,128]{1,0:T(8,128)S(1)} %get-tuple-element.35), channel_id=1, source_target_pairs={{0,48},{16,32},{32,16},{48,0},{64,112},{80,96},{96,80},{112,64},{1... | collective-permute-start | bytes 12296 | tf_op jit(solution)/shard_map/ppermute | solution.py:318
  48.2 3.7 %collective-permute-start.1 = (f32[8,128]{1,0:T(8,128)S(1)}, f32[8,128]{1,0:T(8,128)S(1)}, u32[]{:S(2)}, u32[]{:S(2)}) collective-permute-start(f32[8,128]{1,0:T(8,128)S(1)} %get-tuple-element.35), channel_id=1, source_target_pairs={{0,32},{16,48},{32,0},{48,16},{64,96},{80,112},{96,64},{112,80},{1... | collective-permute-start | bytes 12296 | tf_op jit(solution)/shard_map/ppermute | solution.py:318
  49.9 2.0 %collective-permute-start = (f32[8,128]{1,0:T(8,128)S(1)}, f32[8,128]{1,0:T(8,128)S(1)}, u32[]{:S(2)}, u32[]{:S(2)}) collective-permute-start(f32[8,128]{1,0:T(8,128)S(1)} %get-tuple-element.35), channel_id=1, source_target_pairs={{0,16},{16,0},{32,48},{48,32},{64,80},{80,64},{96,112},{112,96},{1... | collective-permute-start | bytes 12296 | tf_op jit(solution)/shard_map/ppermute | solution.py:318
  51.9 6.6 %collective-permute-start.5 = (f32[8,128]{1,0:T(8,128)S(1)}, f32[8,128]{1,0:T(8,128)S(1)}, u32[]{:S(2)}, u32[]{:S(2)}) collective-permute-start(f32[8,128]{1,0:T(8,128)S(1)} %add_add_fusion.1), channel_id=1, source_target_pairs={{0,192},{16,208},{32,224},{48,240},{64,128},{80,144},{96,160},{112... | collective-permute-start | bytes 12296 | tf_op jit(solution)/shard_map/ppermute | solution.py:318
  54.4 7.5 %collective-permute-start.4 = (f32[8,128]{1,0:T(8,128)S(1)}, f32[8,128]{1,0:T(8,128)S(1)}, u32[]{:S(2)}, u32[]{:S(2)}) collective-permute-start(f32[8,128]{1,0:T(8,128)S(1)} %add_add_fusion.1), channel_id=1, source_target_pairs={{0,128},{16,144},{32,160},{48,176},{64,192},{80,208},{96,224},{112... | collective-permute-start | bytes 12296 | tf_op jit(solution)/shard_map/ppermute | solution.py:318
  55.9 6.1 %collective-permute-start.3 = (f32[8,128]{1,0:T(8,128)S(1)}, f32[8,128]{1,0:T(8,128)S(1)}, u32[]{:S(2)}, u32[]{:S(2)}) collective-permute-start(f32[8,128]{1,0:T(8,128)S(1)} %add_add_fusion.1), channel_id=1, source_target_pairs={{0,64},{16,80},{32,96},{48,112},{64,0},{80,16},{96,32},{112,48},{1... | collective-permute-start | bytes 12296 | tf_op jit(solution)/shard_map/ppermute | solution.py:318
  63.5 18.9 %all-to-all-start.3 = ((bf16[16,80,256]{2,1,0:T(8,128)(2,1)}), bf16[16,80,256]{2,1,0:T(8,128)(2,1)S(1)}, u32[]{:S(2)}, u32[]{:S(2)}) async-start(bf16[16,80,256]{2,1,0:T(8,128)(2,1)} %sum_partials.1), calls=%async_computation.3 | async-start | bytes 1310720 | tf_op jit(solution)/shard_map/all_to_all | solution.py:402

commit v7 on v6

--- a/solution.py
+++ b/solution.py
@@ -89,30 +89,34 @@
 
 
 def pack_kernel(
-    docs_hbm, counts_hbm, tiles_hbm, image_hbm, out_ref, plan_ref, docs, counts, tiles, image, sems
+    docs_hbm, counts_hbm, tiles_hbm, image_ref, out_ref, plan_ref, docs, counts, tiles, sems, sends
 ):
     copies = [
         pltpu.make_async_copy(source, target, sems.at[index])
         for index, (source, target) in enumerate(
-            ((docs_hbm, docs), (counts_hbm, counts), (tiles_hbm, tiles), (image_hbm, image))
+            ((docs_hbm, docs), (counts_hbm, counts), (tiles_hbm, tiles))
         )
     ]
     for copy in copies:
         copy.start()
-    for copy in copies[:3]:
+    for copy in copies:
         copy.wait()
-    img_dev, img_tok, _ = image.shape
-    quarters = img_tok // TILES // CHUNK
+    img_dev, _, quarters, _, _ = image_ref.shape
     slots = write_plan(docs, counts, tiles, img_dev, plan_ref)
-    copies[3].wait()
+    copies = []
     for img in range(img_dev):
         _, start, _ = own_image(slots, lax.axis_index("seq"), img)
         for residue in range(TILES):
-            tile = tile_of(residue, start)
-            for quarter in range(quarters):
-                out_ref[residue * quarters + quarter, img * CHUNK : (img + 1) * CHUNK, :] = image[
-                    img, chunk_rows(tile * quarters + quarter), :
-                ]
+            to = slice(residue * quarters, (residue + 1) * quarters)
+            copy = pltpu.make_async_copy(
+                image_ref.at[img, tile_of(residue, start)],
+                out_ref.at[to, img * CHUNK : (img + 1) * CHUNK, :],
+                sends.at[img, residue],
+            )
+            copy.start()
+            copies.append(copy)
+    for copy in copies:
+        copy.wait()
 
 
 def held_chunks(slots, quarters):
@@ -258,25 +262,26 @@
 
 def sum_kernel(slot_count, img_dev, plan, partial_ref, gate_ref, out_ref, sums):
     parts = partial_ref.shape[0]
-    width = out_ref.shape[2]
+    half = out_ref.shape[2]
     sent = out_ref.shape[1] - CHUNK
-    room = sent // CHUNK
+    room = sent // (2 * CHUNK)
     for number in range(partial_ref.shape[1] // CHUNK):
         at = slice(number * CHUNK, (number + 1) * CHUNK)
         total = partial_ref[0, at, :].astype(F32)
         for part in range(1, parts):
             total = total + partial_ref[part, at, :].astype(F32)
         sums[at, :] = total.astype(BF16)
-    out_ref[:, :sent, :] = jnp.zeros((parts, sent, width), BF16)
+    out_ref[:, :sent, :] = jnp.zeros((parts, sent, half), BF16)
     slots = read_plan(plan, slot_count)
     for slot, here, number in held_chunks(slots, parts // TILES):
 
         @pl.when(here)
         def _(slot=slot, number=number):
             place = position(slot, img_dev, room)
-            out_ref[slot.owner, chunk_rows(place), :] = sums[chunk_rows(number), :]
-
-    term = jnp.broadcast_to(gate_ref[0:1, 0:1], (CHUNK, width))
+            out_ref[slot.owner, chunk_rows(place), :] = sums[chunk_rows(number), :half]
+            out_ref[slot.owner, chunk_rows(place + room), :] = sums[chunk_rows(number), half:]
+
+    term = jnp.broadcast_to(gate_ref[0:1, :], (CHUNK, half))
     high = term.astype(BF16).astype(F32)
     middle = (term - high).astype(BF16).astype(F32)
     low = term - high - middle
@@ -289,8 +294,9 @@
 def unpack_kernel(slot_count, norm_factor, plan, gate, owned_ref, grads_ref, gate_ref):
     parts = owned_ref.shape[0]
     img_dev = grads_ref.shape[0]
+    half = owned_ref.shape[2]
     sent = owned_ref.shape[1] - CHUNK
-    room = sent // CHUNK
+    room = sent // (2 * CHUNK)
     quarters = parts // TILES
     slots = read_plan(plan, slot_count)
     for img in range(img_dev):
@@ -299,10 +305,11 @@
         for part in range(parts):
             tile = tile_of(part // quarters, start)
             to = chunk_rows(tile * quarters + part % quarters)
-            grads = owned_ref[part, chunk_rows(place), :].astype(F32)
-            if room < img_dev:
-                grads = jnp.where(cited, grads, jnp.zeros_like(grads))
-            grads_ref[img, to, :] = grads
+            for cols, row in ((slice(0, half), place), (slice(half, 2 * half), place + room)):
+                grads = owned_ref[part, chunk_rows(row), :].astype(F32)
+                if room < img_dev:
+                    grads = jnp.where(cited, grads, jnp.zeros_like(grads))
+                grads_ref[img, to, cols] = grads
     total = owned_ref[0, sent:, :].astype(F32)
     for part in range(1, parts):
         total = total + owned_ref[part, sent:, :].astype(F32)
@@ -394,7 +401,7 @@
     summed = call(
         functools.partial(sum_kernel, slots, img_dev),
         "sum_partials",
-        low(parts, (room + 1) * CHUNK, kv_width),
+        low(parts, (2 * room + 1) * CHUNK, head_dim),
         (plan,),
         (partial, gate_sum),
         [pltpu.VMEM((sent, kv_width), BF16)],
@@ -426,17 +433,22 @@
             jax.ShapeDtypeStruct(((len(FIELDS) + 1) * STRIDE,), jnp.int32),
         ),
         in_specs=[pl.BlockSpec(memory_space=pltpu.HBM)] * 4,
-        out_specs=(VMEM(), SMEM()),
+        out_specs=(pl.BlockSpec(memory_space=pltpu.HBM), SMEM()),
         scratch_shapes=[
             pltpu.SMEM((slots, doc_counts.shape[0]), jnp.int32),
             pltpu.SMEM(doc_counts.shape, jnp.int32),
             pltpu.SMEM(image_tiles.shape, jnp.int32),
-            pltpu.VMEM(image_kv.shape, BF16),
-            pltpu.SemaphoreType.DMA((4,)),
+            pltpu.SemaphoreType.DMA((3,)),
+            pltpu.SemaphoreType.DMA((img_dev, TILES)),
         ],
         compiler_params=pltpu.CompilerParams(vmem_limit_bytes=60 * 1024 * 1024),
         name="pack_chunks",
-    )(doc_images.T, doc_counts, image_tiles, image_kv)
+    )(
+        doc_images.T,
+        doc_counts,
+        image_tiles,
+        image_kv.reshape(img_dev, TILES, parts // TILES, CHUNK, kv_width),
+    )
     chunks = lax.all_to_all(chunks, "seq", 0, 0)
     prepared = call(
         prepare_kernel,

time: 85.4 us -> 102 us (1.19)
  Pallas kernels: 13.9 us -> 27.5 us
  starting transfers between devices: 26.5 us -> 29 us
    pallas_call x1, Pallas kernels: 1.96 us -> 18.5 us  [per_device(): pl.pallas_call(pack_kernel, out_shape=(low(parts, img_dev * CHUNK, kv_wid...]
    pallas_call x6, Pallas kernels: 12 us -> 8.95 us  [call(): pl.pallas_call(kernel, out_shape=outs, in_specs=[SMEM()] * len(smem) + [V...]
    ppermute x6, starting transfers between devices: 8.52 us -> 11.3 us  [moved(): return lax.ppermute(x, axis, [(i, i ^ step) for i in range(size)])]
  transfers between devices with their start and end apart: 9 -> 9, of which waited for: 5 -> 4; matrix products, arithmetic and copies ran while one was open for 0% -> 0% of each run, Pallas kernels for 2% -> 2%
where the time goes in v7:
time: 102 us; the launch traced here: 101 us
  starting transfers between devices  29 us (28%)
  Pallas kernels  27.5 us (27%)
  waiting for transfers between devices  26.4 us (26%)
  blocking collectives  16.2 us (16%)
  between operations  1.4 us (1%)
    pallas_call x1, Pallas kernels, per_device(): pl.pallas_call(pack_kernel, out_shape=(low(parts, img_dev * CHUNK, kv_wid...  18.5 us
    all_to_all x1, blocking collectives, after_scatter(): kv_cited = lax.all_to_all(cited, 'seq', 0, 0)  16.2 us
    ppermute x6, starting transfers between devices, moved(): return lax.ppermute(x, axis, [(i, i ^ step) for i in range(size)])  11.3 us
    all_to_all x1, waiting for transfers between devices, after_scatter(): owned = lax.all_to_all(summed, 'seq', 0, 0)  10.7 us
    all_to_all x1, waiting for transfers between devices, per_device(): chunks = lax.all_to_all(chunks, 'seq', 0, 0)  9.5 us
    pallas_call x6, Pallas kernels, call(): pl.pallas_call(kernel, out_shape=outs, in_specs=[SMEM()] * len(smem) + [V...  8.95 us
    all_to_all x1, starting transfers between devices, per_device(): chunks = lax.all_to_all(chunks, 'seq', 0, 0)  7.18 us
    all_to_all x1, starting transfers between devices, after_scatter(): owned = lax.all_to_all(summed, 'seq', 0, 0)  6.91 us
  transfers between devices with their start and end apart: 9, of which 4 were waited for; matrix products, arithmetic and copies ran while one was open for 0% of the time, Pallas kernels for 2%

profile of v7, /device:TPU:32, one launch (start us, length us, event | category | flops | bytes accessed | tf_op | source)
XLA Modules:
  0.0 101.2 jit_solution(18348332956445562208)
XLA Ops:
  0.6 18.5 %pack_chunks.1 = (bf16[16,64,256]{2,1,0:T(8,128)(2,1)}, s32[56]{0:T(128)}) custom-call(s32[6,16]{1,0:T(8,128)} %bitcast.9, s32[16]{0:T(128)} %counts_hbm.1, s32[1024]{0:T(1024)} %tiles_hbm.1, bf16[4,4,4,16,256]{4,3,2,1,0:T(8,128)(2,1)} %bitcast.8), custom_call_target="tpu_custom_call" | custom-call | tf_op jit(solution)/shard_map/pack_chunks/pallas_call | solution.py:429
  19.2 0.0 copy-start
  19.2 0.0 copy-start.1
  19.2 7.2 %all-to-all-start = ((bf16[16,64,256]{2,1,0:T(8,128)(2,1)}), bf16[16,64,256]{2,1,0:T(8,128)(2,1)S(1)}, u32[]{:S(2)}, u32[]{:S(2)}) async-start(bf16[16,64,256]{2,1,0:T(8,128)(2,1)} %get-tuple-element.22), calls=%async_computation | async-start | bytes 1048576 | tf_op jit(solution)/shard_map/all_to_all | solution.py:452
  27.0 0.0 copy-start.2
  27.1 0.6 copy-done.2
  27.7 0.7 prepare_rows.1
  28.4 9.5 %all-to-all-done.chunks_ref = bf16[16,64,256]{2,1,0:T(8,128)(2,1)S(1)} async-done(((bf16[16,64,256]{2,1,0:T(8,128)(2,1)}), bf16[16,64,256]{2,1,0:T(8,128)(2,1)S(1)}, u32[]{:S(2)}, u32[]{:S(2)}) %all-to-all-start) | async-done | bytes 524320 | tf_op jit(solution)/shard_map/all_to_all | solution.py:452
  37.9 0.7 select_cited.1
  38.5 16.2 %all_to_all.20.kv_ref = bf16[16,96,256]{2,1,0:T(8,128)(2,1)S(1)} all-to-all(bf16[16,96,256]{2,1,0:T(8,128)(2,1)S(1)} %select_cited.1), channel_id=1, replica_groups=mesh['dp'=16,'seq'=16] {'seq'}, dimensions={0} | all-to-all | bytes 1572864 | tf_op jit(solution)/shard_map/all_to_all | solution.py:373
  54.8 3.3 %attention.1 = (f32[128,1024]{1,0:T(8,128)S(1)}, f32[128,1024]{1,0:T(8,128)S(1)}, bf16[16,96,256]{2,1,0:T(8,128)(2,1)}, f32[8,128]{1,0:T(8,128)S(1)}) custom-call(s32[56]{0:T(128)S(1)} %copy-done.2, f32[1]{0:T(128)S(6)} %copy.11.gate, bf16[16,96,256]{2,1,0:T(8,128)(2,1)S(1)} %all_to_all.20.kv_ref, bf16[1024,128]{1,0:T(8,128)(2,1)S(1)} %get-tuple-element.27.query_rows, ...), custom_call_target="tpu_custom_call" | custom-call | tf_op jit(solution)/shard_map/attention/pallas_call | solution.py:339
  58.0 3.6 %all-to-all-start.2 = ((bf16[16,96,256]{2,1,0:T(8,128)(2,1)}), bf16[16,96,256]{2,1,0:T(8,128)(2,1)S(1)}, u32[]{:S(2)}, u32[]{:S(2)}) async-start(bf16[16,96,256]{2,1,0:T(8,128)(2,1)} %get-tuple-element.34), calls=%async_computation.2 | async-start | bytes 1572864 | tf_op jit(solution)/shard_map/all_to_all | solution.py:396
  61.7 0.1 collective-permute-start.2
  61.8 3.3 %collective-permute-start.1 = (f32[8,128]{1,0:T(8,128)S(1)}, f32[8,128]{1,0:T(8,128)S(1)}, u32[]{:S(2)}, u32[]{:S(2)}) collective-permute-start(f32[8,128]{1,0:T(8,128)S(1)} %get-tuple-element.35), channel_id=1, source_target_pairs={{0,32},{16,48},{32,0},{48,16},{64,96},{80,112},{96,64},{112,80},{1... | collective-permute-start | bytes 12296 | tf_op jit(solution)/shard_map/ppermute | solution.py:325
  65.1 1.6 %collective-permute-done.1 = f32[8,128]{1,0:T(8,128)S(1)} collective-permute-done((f32[8,128]{1,0:T(8,128)S(1)}, f32[8,128]{1,0:T(8,128)S(1)}, u32[]{:S(2)}, u32[]{:S(2)}) %collective-permute-start.1) | collective-permute-done | bytes 4128 | tf_op jit(solution)/shard_map/ppermute | solution.py:325
  66.7 5.0 %collective-permute-start.5 = (f32[8,128]{1,0:T(8,128)S(1)}, f32[8,128]{1,0:T(8,128)S(1)}, u32[]{:S(2)}, u32[]{:S(2)}) collective-permute-start(f32[8,128]{1,0:T(8,128)S(1)} %add_add_fusion.1), channel_id=1, source_target_pairs={{0,192},{16,208},{32,224},{48,240},{64,128},{80,144},{96,160},{112... | collective-permute-start | bytes 12296 | tf_op jit(solution)/shard_map/ppermute | solution.py:325
  71.6 2.5 %collective-permute-start.4 = (f32[8,128]{1,0:T(8,128)S(1)}, f32[8,128]{1,0:T(8,128)S(1)}, u32[]{:S(2)}, u32[]{:S(2)}) collective-permute-start(f32[8,128]{1,0:T(8,128)S(1)} %add_add_fusion.1), channel_id=1, source_target_pairs={{0,128},{16,144},{32,160},{48,176},{64,192},{80,208},{96,224},{112... | collective-permute-start | bytes 12296 | tf_op jit(solution)/shard_map/ppermute | solution.py:325
  74.1 0.5 collective-permute-start.3
  74.6 4.6 %collective-permute-done.4 = f32[8,128]{1,0:T(8,128)S(1)} collective-permute-done((f32[8,128]{1,0:T(8,128)S(1)}, f32[8,128]{1,0:T(8,128)S(1)}, u32[]{:S(2)}, u32[]{:S(2)}) %collective-permute-start.4) | collective-permute-done | bytes 4128 | tf_op jit(solution)/shard_map/ppermute | solution.py:325
  79.2 1.6 %sum_partials.1 = bf16[16,144,128]{2,1,0:T(8,128)(2,1)} custom-call(s32[56]{0:T(128)S(1)} %copy-done.2, bf16[16,96,256]{2,1,0:T(8,128)(2,1)S(1)} %all-to-all-done.2.partial_ref, f32[8,128]{1,0:T(8,128)S(1)} %add_add_fusion.gate_ref), custom_call_target="tpu_custom_call" | custom-call | tf_op jit(solution)/shard_map/sum_partials/pallas_call | solution.py:339
  80.8 6.9 %all-to-all-start.3 = ((bf16[16,144,128]{2,1,0:T(8,128)(2,1)}), bf16[16,144,128]{2,1,0:T(8,128)(2,1)S(1)}, u32[]{:S(2)}, u32[]{:S(2)}) async-start(bf16[16,144,128]{2,1,0:T(8,128)(2,1)} %sum_partials.1), calls=%async_computation.3 | async-start | bytes 1179648 | tf_op jit(solution)/shard_map/all_to_all | solution.py:409
  87.7 1.1 %finish_rows.1 = (bf16[128,1024]{1,0:T(8,128)(2,1)}, bf16[128,1024]{1,0:T(8,128)(2,1)}) custom-call(f32[1]{0:T(128)S(6)} %copy.11.gate, f32[128,1024]{1,0:T(8,128)S(1)} %get-tuple-element.30.attn_t, f32[128,1024]{1,0:T(8,128)S(1)} %get-tuple-element.31.dquery_t), custom_call_target="tpu_custom_call" | custom-call | tf_op jit(solution)/shard_map/finish_rows/pallas_call | solution.py:339
  88.8 10.7 %all-to-all-done.3.owned_ref = bf16[16,144,128]{2,1,0:T(8,128)(2,1)S(1)} async-done(((bf16[16,144,128]{2,1,0:T(8,128)(2,1)}), bf16[16,144,128]{2,1,0:T(8,128)(2,1)S(1)}, u32[]{:S(2)}, u32[]{:S(2)}) %all-to-all-start.3) | async-done | bytes 589856 | tf_op jit(solution)/shard_map/all_to_all | solution.py:409
  99.5 1.7 %unpack_grads.1 = (f32[4,256,256]{2,1,0:T(8,128)}, f32[1]{0:T(128)}) custom-call(s32[56]{0:T(128)S(1)} %copy-done.2, f32[1]{0:T(128)S(6)} %copy.11.gate, bf16[16,144,128]{2,1,0:T(8,128)(2,1)S(1)} %all-to-all-done.3.owned_ref), custom_call_target="tpu_custom_call" | custom-call | tf_op jit(solution)/shard_map/unpack_grads/pallas_call | solution.py:339
  (10 shorter events, 0.0 us)
Async XLA Ops:
  19.2 7.9 %copy-start = (bf16[1,128,1024]{2,1,0:T(8,128)(2,1)S(1)}, bf16[1,128,1024]{2,1,0:T(8,128)(2,1)}, u32[]{:S(2)}) copy-start(bf16[1,128,1024]{2,1,0:T(8,128)(2,1)} %param.7) | copy-start | bytes 786436
  19.2 7.9 %copy-start.1 = (bf16[1,128,1024]{2,1,0:T(8,128)(2,1)S(1)}, bf16[1,128,1024]{2,1,0:T(8,128)(2,1)}, u32[]{:S(2)}) copy-start(bf16[1,128,1024]{2,1,0:T(8,128)(2,1)} %param.8) | copy-start | bytes 786436
  19.2 18.7 %all-to-all-start = ((bf16[16,64,256]{2,1,0:T(8,128)(2,1)}), bf16[16,64,256]{2,1,0:T(8,128)(2,1)S(1)}, u32[]{:S(2)}, u32[]{:S(2)}) async-start(bf16[16,64,256]{2,1,0:T(8,128)(2,1)} %get-tuple-element.22), calls=%async_computation | async-start | bytes 1048576 | tf_op jit(solution)/shard_map/all_to_all | solution.py:452
  27.0 0.7 copy-start.2
  58.0 21.1 %all-to-all-start.2 = ((bf16[16,96,256]{2,1,0:T(8,128)(2,1)}), bf16[16,96,256]{2,1,0:T(8,128)(2,1)S(1)}, u32[]{:S(2)}, u32[]{:S(2)}) async-start(bf16[16,96,256]{2,1,0:T(8,128)(2,1)} %get-tuple-element.34), calls=%async_computation.2 | async-start | bytes 1572864 | tf_op jit(solution)/shard_map/all_to_all | solution.py:396
  61.7 3.4 %collective-permute-start.2 = (f32[8,128]{1,0:T(8,128)S(1)}, f32[8,128]{1,0:T(8,128)S(1)}, u32[]{:S(2)}, u32[]{:S(2)}) collective-permute-start(f32[8,128]{1,0:T(8,128)S(1)} %get-tuple-element.35), channel_id=1, source_target_pairs={{0,48},{16,32},{32,16},{48,0},{64,112},{80,96},{96,80},{112,64},{1... | collective-permute-start | bytes 12296 | tf_op jit(solution)/shard_map/ppermute | solution.py:325
  61.8 4.9 %collective-permute-start.1 = (f32[8,128]{1,0:T(8,128)S(1)}, f32[8,128]{1,0:T(8,128)S(1)}, u32[]{:S(2)}, u32[]{:S(2)}) collective-permute-start(f32[8,128]{1,0:T(8,128)S(1)} %get-tuple-element.35), channel_id=1, source_target_pairs={{0,32},{16,48},{32,0},{48,16},{64,96},{80,112},{96,64},{112,80},{1... | collective-permute-start | bytes 12296 | tf_op jit(solution)/shard_map/ppermute | solution.py:325
  65.1 1.6 %collective-permute-start = (f32[8,128]{1,0:T(8,128)S(1)}, f32[8,128]{1,0:T(8,128)S(1)}, u32[]{:S(2)}, u32[]{:S(2)}) collective-permute-start(f32[8,128]{1,0:T(8,128)S(1)} %get-tuple-element.35), channel_id=1, source_target_pairs={{0,16},{16,0},{32,48},{48,32},{64,80},{80,64},{96,112},{112,96},{1... | collective-permute-start | bytes 12296 | tf_op jit(solution)/shard_map/ppermute | solution.py:325
  66.7 7.9 %collective-permute-start.5 = (f32[8,128]{1,0:T(8,128)S(1)}, f32[8,128]{1,0:T(8,128)S(1)}, u32[]{:S(2)}, u32[]{:S(2)}) collective-permute-start(f32[8,128]{1,0:T(8,128)S(1)} %add_add_fusion.1), channel_id=1, source_target_pairs={{0,192},{16,208},{32,224},{48,240},{64,128},{80,144},{96,160},{112... | collective-permute-start | bytes 12296 | tf_op jit(solution)/shard_map/ppermute | solution.py:325
  71.6 7.5 %collective-permute-start.4 = (f32[8,128]{1,0:T(8,128)S(1)}, f32[8,128]{1,0:T(8,128)S(1)}, u32[]{:S(2)}, u32[]{:S(2)}) collective-permute-start(f32[8,128]{1,0:T(8,128)S(1)} %add_add_fusion.1), channel_id=1, source_target_pairs={{0,128},{16,144},{32,160},{48,176},{64,192},{80,208},{96,224},{112... | collective-permute-start | bytes 12296 | tf_op jit(solution)/shard_map/ppermute | solution.py:325
  74.1 5.0 %collective-permute-start.3 = (f32[8,128]{1,0:T(8,128)S(1)}, f32[8,128]{1,0:T(8,128)S(1)}, u32[]{:S(2)}, u32[]{:S(2)}) collective-permute-start(f32[8,128]{1,0:T(8,128)S(1)} %add_add_fusion.1), channel_id=1, source_target_pairs={{0,64},{16,80},{32,96},{48,112},{64,0},{80,16},{96,32},{112,48},{1... | collective-permute-start | bytes 12296 | tf_op jit(solution)/shard_map/ppermute | solution.py:325
  80.8 18.7 %all-to-all-start.3 = ((bf16[16,144,128]{2,1,0:T(8,128)(2,1)}), bf16[16,144,128]{2,1,0:T(8,128)(2,1)S(1)}, u32[]{:S(2)}, u32[]{:S(2)}) async-start(bf16[16,144,128]{2,1,0:T(8,128)(2,1)} %sum_partials.1), calls=%async_computation.3 | async-start | bytes 1179648 | tf_op jit(solution)/shard_map/all_to_all | solution.py:409

commit v8 on v6

--- a/solution.py
+++ b/solution.py
@@ -258,25 +258,26 @@
 
 def sum_kernel(slot_count, img_dev, plan, partial_ref, gate_ref, out_ref, sums):
     parts = partial_ref.shape[0]
-    width = out_ref.shape[2]
+    half = out_ref.shape[2]
     sent = out_ref.shape[1] - CHUNK
-    room = sent // CHUNK
+    room = sent // (2 * CHUNK)
     for number in range(partial_ref.shape[1] // CHUNK):
         at = slice(number * CHUNK, (number + 1) * CHUNK)
         total = partial_ref[0, at, :].astype(F32)
         for part in range(1, parts):
             total = total + partial_ref[part, at, :].astype(F32)
         sums[at, :] = total.astype(BF16)
-    out_ref[:, :sent, :] = jnp.zeros((parts, sent, width), BF16)
+    out_ref[:, :sent, :] = jnp.zeros((parts, sent, half), BF16)
     slots = read_plan(plan, slot_count)
     for slot, here, number in held_chunks(slots, parts // TILES):
 
         @pl.when(here)
         def _(slot=slot, number=number):
             place = position(slot, img_dev, room)
-            out_ref[slot.owner, chunk_rows(place), :] = sums[chunk_rows(number), :]
-
-    term = jnp.broadcast_to(gate_ref[0:1, 0:1], (CHUNK, width))
+            out_ref[slot.owner, chunk_rows(place), :] = sums[chunk_rows(number), :half]
+            out_ref[slot.owner, chunk_rows(place + room), :] = sums[chunk_rows(number), half:]
+
+    term = jnp.broadcast_to(gate_ref[0:1, :], (CHUNK, half))
     high = term.astype(BF16).astype(F32)
     middle = (term - high).astype(BF16).astype(F32)
     low = term - high - middle
@@ -289,8 +290,9 @@
 def unpack_kernel(slot_count, norm_factor, plan, gate, owned_ref, grads_ref, gate_ref):
     parts = owned_ref.shape[0]
     img_dev = grads_ref.shape[0]
+    half = owned_ref.shape[2]
     sent = owned_ref.shape[1] - CHUNK
-    room = sent // CHUNK
+    room = sent // (2 * CHUNK)
     quarters = parts // TILES
     slots = read_plan(plan, slot_count)
     for img in range(img_dev):
@@ -299,10 +301,11 @@
         for part in range(parts):
             tile = tile_of(part // quarters, start)
             to = chunk_rows(tile * quarters + part % quarters)
-            grads = owned_ref[part, chunk_rows(place), :].astype(F32)
-            if room < img_dev:
-                grads = jnp.where(cited, grads, jnp.zeros_like(grads))
-            grads_ref[img, to, :] = grads
+            for cols, row in ((slice(0, half), place), (slice(half, 2 * half), place + room)):
+                grads = owned_ref[part, chunk_rows(row), :].astype(F32)
+                if room < img_dev:
+                    grads = jnp.where(cited, grads, jnp.zeros_like(grads))
+                grads_ref[img, to, cols] = grads
     total = owned_ref[0, sent:, :].astype(F32)
     for part in range(1, parts):
         total = total + owned_ref[part, sent:, :].astype(F32)
@@ -317,14 +320,12 @@
     def moved(step):
         return lax.ppermute(x, axis, [(i, i ^ step) for i in range(size)])
 
-    step = 1
-    while step < size:
-        if 2 * step < size:
-            x = (x + moved(step)) + (moved(2 * step) + moved(3 * step))
-            step *= 4
-        else:
-            x = x + moved(step)
-            step *= 2
+    steps = [1 << bit for bit in range(size.bit_length() - 1)]
+    while len(steps) > 1:
+        near, far = steps.pop(0), steps.pop()
+        x = (x + moved(near)) + (moved(far) + moved(near + far))
+    for step in steps:
+        x = x + moved(step)
     return x
 
 
@@ -394,7 +395,7 @@
     summed = call(
         functools.partial(sum_kernel, slots, img_dev),
         "sum_partials",
-        low(parts, (room + 1) * CHUNK, kv_width),
+        low(parts, (2 * room + 1) * CHUNK, head_dim),
         (plan,),
         (partial, gate_sum),
         [pltpu.VMEM((sent, kv_width), BF16)],

time: 85.4 us -> 89.5 us (1.048)
  starting transfers between devices: 26.5 us -> 34.6 us
  Pallas kernels: 13.9 us -> 10.9 us
    ppermute x6, starting transfers between devices: 8.52 us -> 17 us  [moved(): return lax.ppermute(x, axis, [(i, i ^ step) for i in range(size)])]
    pallas_call x6, Pallas kernels: 12 us -> 8.94 us  [call(): pl.pallas_call(kernel, out_shape=outs, in_specs=[SMEM()] * len(smem) + [V...]
    all_to_all x1, waiting for transfers between devices: 10.7 us -> 9.32 us  [after_scatter(): owned = lax.all_to_all(summed, 'seq', 0, 0)]
    ppermute x6, waiting for transfers between devices: 5.29 us -> 6.45 us  [moved(): return lax.ppermute(x, axis, [(i, i ^ step) for i in range(size)])]
  transfers between devices with their start and end apart: 9 -> 9, of which waited for: 5 -> 6; matrix products, arithmetic and copies ran while one was open for 0% -> 0% of each run, Pallas kernels for 2% -> 2%
where the time goes in v8:
time: 89.5 us; the launch traced here: 89.1 us
  starting transfers between devices  34.6 us (39%)
  waiting for transfers between devices  25.3 us (28%)
  blocking collectives  16.2 us (18%)
  Pallas kernels  10.9 us (12%)
  between operations  1.38 us (2%)
    ppermute x6, starting transfers between devices, moved(): return lax.ppermute(x, axis, [(i, i ^ step) for i in range(size)])  17 us
    all_to_all x1, blocking collectives, after_scatter(): kv_cited = lax.all_to_all(cited, 'seq', 0, 0)  16.2 us
    all_to_all x1, waiting for transfers between devices, per_device(): chunks = lax.all_to_all(chunks, 'seq', 0, 0)  9.5 us
    all_to_all x1, waiting for transfers between devices, after_scatter(): owned = lax.all_to_all(summed, 'seq', 0, 0)  9.32 us
    pallas_call x6, Pallas kernels, call(): pl.pallas_call(kernel, out_shape=outs, in_specs=[SMEM()] * len(smem) + [V...  8.94 us
    all_to_all x1, starting transfers between devices, per_device(): chunks = lax.all_to_all(chunks, 'seq', 0, 0)  7.18 us
    all_to_all x1, starting transfers between devices, after_scatter(): owned = lax.all_to_all(summed, 'seq', 0, 0)  6.85 us
    ppermute x6, waiting for transfers between devices, moved(): return lax.ppermute(x, axis, [(i, i ^ step) for i in range(size)])  6.45 us
  transfers between devices with their start and end apart: 9, of which 6 were waited for; matrix products, arithmetic and copies ran while one was open for 0% of the time, Pallas kernels for 2%

profile of v8, /device:TPU:32, one launch (start us, length us, event | category | flops | bytes accessed | tf_op | source)
XLA Modules:
  0.0 89.1 jit_solution(9815446870696895506)
XLA Ops:
  0.6 2.0 %pack_chunks.1 = (bf16[16,64,256]{2,1,0:T(8,128)(2,1)}, s32[56]{0:T(128)}) custom-call(s32[6,16]{1,0:T(8,128)} %bitcast.7, s32[16]{0:T(128)} %counts_hbm.1, s32[1024]{0:T(1024)} %tiles_hbm.1, bf16[4,256,256]{2,1,0:T(8,128)(2,1)} %image_hbm.1), custom_call_target="tpu_custom_call" | custom-call | tf_op jit(solution)/shard_map/pack_chunks/pallas_call | solution.py:423
  2.6 7.2 %all-to-all-start = ((bf16[16,64,256]{2,1,0:T(8,128)(2,1)}), bf16[16,64,256]{2,1,0:T(8,128)(2,1)S(1)}, u32[]{:S(2)}, u32[]{:S(2)}) async-start(bf16[16,64,256]{2,1,0:T(8,128)(2,1)} %get-tuple-element.22), calls=%async_computation | async-start | bytes 1048576 | tf_op jit(solution)/shard_map/all_to_all | solution.py:441
  10.5 0.6 copy-done.2
  11.1 0.7 prepare_rows.1
  11.8 9.5 %all-to-all-done.chunks_ref = bf16[16,64,256]{2,1,0:T(8,128)(2,1)S(1)} async-done(((bf16[16,64,256]{2,1,0:T(8,128)(2,1)}), bf16[16,64,256]{2,1,0:T(8,128)(2,1)S(1)}, u32[]{:S(2)}, u32[]{:S(2)}) %all-to-all-start) | async-done | bytes 524320 | tf_op jit(solution)/shard_map/all_to_all | solution.py:441
  21.3 0.7 select_cited.1
  22.0 16.2 %all_to_all.20.kv_ref = bf16[16,96,256]{2,1,0:T(8,128)(2,1)S(1)} all-to-all(bf16[16,96,256]{2,1,0:T(8,128)(2,1)S(1)} %select_cited.1), channel_id=1, replica_groups=mesh['dp'=16,'seq'=16] {'seq'}, dimensions={0} | all-to-all | bytes 1572864 | tf_op jit(solution)/shard_map/all_to_all | solution.py:367
  38.2 3.3 %attention.1 = (f32[128,1024]{1,0:T(8,128)S(1)}, f32[128,1024]{1,0:T(8,128)S(1)}, bf16[16,96,256]{2,1,0:T(8,128)(2,1)}, f32[8,128]{1,0:T(8,128)S(1)}) custom-call(s32[56]{0:T(128)S(1)} %copy-done.2, f32[1]{0:T(128)S(6)} %copy.11.gate, bf16[16,96,256]{2,1,0:T(8,128)(2,1)S(1)} %all_to_all.20.kv_ref, bf16[1024,128]{1,0:T(8,128)(2,1)S(1)} %get-tuple-element.27.query_rows, ...), custom_call_target="tpu_custom_call" | custom-call | tf_op jit(solution)/shard_map/attention/pallas_call | solution.py:333
  41.5 3.6 %all-to-all-start.2 = ((bf16[16,96,256]{2,1,0:T(8,128)(2,1)}), bf16[16,96,256]{2,1,0:T(8,128)(2,1)S(1)}, u32[]{:S(2)}, u32[]{:S(2)}) async-start(bf16[16,96,256]{2,1,0:T(8,128)(2,1)} %get-tuple-element.34), calls=%async_computation.2 | async-start | bytes 1572864 | tf_op jit(solution)/shard_map/all_to_all | solution.py:390
  45.1 3.2 %collective-permute-start.2 = (f32[8,128]{1,0:T(8,128)S(1)}, f32[8,128]{1,0:T(8,128)S(1)}, u32[]{:S(2)}, u32[]{:S(2)}) collective-permute-start(f32[8,128]{1,0:T(8,128)S(1)} %get-tuple-element.35), channel_id=1, source_target_pairs={{0,144},{16,128},{32,176},{48,160},{64,208},{80,192},{96,240},{112... | collective-permute-start | bytes 12296 | tf_op jit(solution)/shard_map/ppermute | solution.py:321
  48.3 3.3 %collective-permute-start.1 = (f32[8,128]{1,0:T(8,128)S(1)}, f32[8,128]{1,0:T(8,128)S(1)}, u32[]{:S(2)}, u32[]{:S(2)}) collective-permute-start(f32[8,128]{1,0:T(8,128)S(1)} %get-tuple-element.35), channel_id=1, source_target_pairs={{0,128},{16,144},{32,160},{48,176},{64,192},{80,208},{96,224},{112... | collective-permute-start | bytes 12296 | tf_op jit(solution)/shard_map/ppermute | solution.py:321
  51.6 0.0 collective-permute-start
  51.6 0.5 collective-permute-done.2
  52.1 3.7 %collective-permute-done.1 = f32[8,128]{1,0:T(8,128)S(1)} collective-permute-done((f32[8,128]{1,0:T(8,128)S(1)}, f32[8,128]{1,0:T(8,128)S(1)}, u32[]{:S(2)}, u32[]{:S(2)}) %collective-permute-start.1) | collective-permute-done | bytes 4128 | tf_op jit(solution)/shard_map/ppermute | solution.py:321
  55.8 2.6 %collective-permute-start.5 = (f32[8,128]{1,0:T(8,128)S(1)}, f32[8,128]{1,0:T(8,128)S(1)}, u32[]{:S(2)}, u32[]{:S(2)}) collective-permute-start(f32[8,128]{1,0:T(8,128)S(1)} %add_add_fusion.1), channel_id=1, source_target_pairs={{0,96},{16,112},{32,64},{48,80},{64,32},{80,48},{96,0},{112,16},{1... | collective-permute-start | bytes 12296 | tf_op jit(solution)/shard_map/ppermute | solution.py:321
  58.4 6.5 %collective-permute-start.4 = (f32[8,128]{1,0:T(8,128)S(1)}, f32[8,128]{1,0:T(8,128)S(1)}, u32[]{:S(2)}, u32[]{:S(2)}) collective-permute-start(f32[8,128]{1,0:T(8,128)S(1)} %add_add_fusion.1), channel_id=1, source_target_pairs={{0,64},{16,80},{32,96},{48,112},{64,0},{80,16},{96,32},{112,48},{1... | collective-permute-start | bytes 12296 | tf_op jit(solution)/shard_map/ppermute | solution.py:321
  64.9 1.4 %collective-permute-start.3 = (f32[8,128]{1,0:T(8,128)S(1)}, f32[8,128]{1,0:T(8,128)S(1)}, u32[]{:S(2)}, u32[]{:S(2)}) collective-permute-start(f32[8,128]{1,0:T(8,128)S(1)} %add_add_fusion.1), channel_id=1, source_target_pairs={{0,32},{16,48},{32,0},{48,16},{64,96},{80,112},{96,64},{112,80},{1... | collective-permute-start | bytes 12296 | tf_op jit(solution)/shard_map/ppermute | solution.py:321
  66.3 0.2 collective-permute-done.4
  66.5 2.0 %collective-permute-done.3 = f32[8,128]{1,0:T(8,128)S(1)} collective-permute-done((f32[8,128]{1,0:T(8,128)S(1)}, f32[8,128]{1,0:T(8,128)S(1)}, u32[]{:S(2)}, u32[]{:S(2)}) %collective-permute-start.3) | collective-permute-done | bytes 4128 | tf_op jit(solution)/shard_map/ppermute | solution.py:321
  68.5 1.6 %sum_partials.1 = bf16[16,144,128]{2,1,0:T(8,128)(2,1)} custom-call(s32[56]{0:T(128)S(1)} %copy-done.2, bf16[16,96,256]{2,1,0:T(8,128)(2,1)S(1)} %all-to-all-done.2.partial_ref, f32[8,128]{1,0:T(8,128)S(1)} %add_add_fusion.gate_ref), custom_call_target="tpu_custom_call" | custom-call | tf_op jit(solution)/shard_map/sum_partials/pallas_call | solution.py:333
  70.1 6.8 %all-to-all-start.3 = ((bf16[16,144,128]{2,1,0:T(8,128)(2,1)}), bf16[16,144,128]{2,1,0:T(8,128)(2,1)S(1)}, u32[]{:S(2)}, u32[]{:S(2)}) async-start(bf16[16,144,128]{2,1,0:T(8,128)(2,1)} %sum_partials.1), calls=%async_computation.3 | async-start | bytes 1179648 | tf_op jit(solution)/shard_map/all_to_all | solution.py:403
  77.0 1.1 %finish_rows.1 = (bf16[128,1024]{1,0:T(8,128)(2,1)}, bf16[128,1024]{1,0:T(8,128)(2,1)}) custom-call(f32[1]{0:T(128)S(6)} %copy.11.gate, f32[128,1024]{1,0:T(8,128)S(1)} %get-tuple-element.30.attn_t, f32[128,1024]{1,0:T(8,128)S(1)} %get-tuple-element.31.dquery_t), custom_call_target="tpu_custom_call" | custom-call | tf_op jit(solution)/shard_map/finish_rows/pallas_call | solution.py:333
  78.1 9.3 %all-to-all-done.3.owned_ref = bf16[16,144,128]{2,1,0:T(8,128)(2,1)S(1)} async-done(((bf16[16,144,128]{2,1,0:T(8,128)(2,1)}), bf16[16,144,128]{2,1,0:T(8,128)(2,1)S(1)}, u32[]{:S(2)}, u32[]{:S(2)}) %all-to-all-start.3) | async-done | bytes 589856 | tf_op jit(solution)/shard_map/all_to_all | solution.py:403
  87.4 1.7 %unpack_grads.1 = (f32[4,256,256]{2,1,0:T(8,128)}, f32[1]{0:T(128)}) custom-call(s32[56]{0:T(128)S(1)} %copy-done.2, f32[1]{0:T(128)S(6)} %copy.11.gate, bf16[16,144,128]{2,1,0:T(8,128)(2,1)S(1)} %all-to-all-done.3.owned_ref), custom_call_target="tpu_custom_call" | custom-call | tf_op jit(solution)/shard_map/unpack_grads/pallas_call | solution.py:333
  (10 shorter events, 0.0 us)
Async XLA Ops:
  2.6 7.9 %copy-start = (bf16[1,128,1024]{2,1,0:T(8,128)(2,1)S(1)}, bf16[1,128,1024]{2,1,0:T(8,128)(2,1)}, u32[]{:S(2)}) copy-start(bf16[1,128,1024]{2,1,0:T(8,128)(2,1)} %param.7) | copy-start | bytes 786436
  2.6 7.9 %copy-start.1 = (bf16[1,128,1024]{2,1,0:T(8,128)(2,1)S(1)}, bf16[1,128,1024]{2,1,0:T(8,128)(2,1)}, u32[]{:S(2)}) copy-start(bf16[1,128,1024]{2,1,0:T(8,128)(2,1)} %param.8) | copy-start | bytes 786436
  2.6 18.7 %all-to-all-start = ((bf16[16,64,256]{2,1,0:T(8,128)(2,1)}), bf16[16,64,256]{2,1,0:T(8,128)(2,1)S(1)}, u32[]{:S(2)}, u32[]{:S(2)}) async-start(bf16[16,64,256]{2,1,0:T(8,128)(2,1)} %get-tuple-element.22), calls=%async_computation | async-start | bytes 1048576 | tf_op jit(solution)/shard_map/all_to_all | solution.py:441
  10.5 0.7 copy-start.2
  41.5 27.1 %all-to-all-start.2 = ((bf16[16,96,256]{2,1,0:T(8,128)(2,1)}), bf16[16,96,256]{2,1,0:T(8,128)(2,1)S(1)}, u32[]{:S(2)}, u32[]{:S(2)}) async-start(bf16[16,96,256]{2,1,0:T(8,128)(2,1)} %get-tuple-element.34), calls=%async_computation.2 | async-start | bytes 1572864 | tf_op jit(solution)/shard_map/all_to_all | solution.py:390
  45.1 7.0 %collective-permute-start.2 = (f32[8,128]{1,0:T(8,128)S(1)}, f32[8,128]{1,0:T(8,128)S(1)}, u32[]{:S(2)}, u32[]{:S(2)}) collective-permute-start(f32[8,128]{1,0:T(8,128)S(1)} %get-tuple-element.35), channel_id=1, source_target_pairs={{0,144},{16,128},{32,176},{48,160},{64,208},{80,192},{96,240},{112... | collective-permute-start | bytes 12296 | tf_op jit(solution)/shard_map/ppermute | solution.py:321
  48.3 7.5 %collective-permute-start.1 = (f32[8,128]{1,0:T(8,128)S(1)}, f32[8,128]{1,0:T(8,128)S(1)}, u32[]{:S(2)}, u32[]{:S(2)}) collective-permute-start(f32[8,128]{1,0:T(8,128)S(1)} %get-tuple-element.35), channel_id=1, source_target_pairs={{0,128},{16,144},{32,160},{48,176},{64,192},{80,208},{96,224},{112... | collective-permute-start | bytes 12296 | tf_op jit(solution)/shard_map/ppermute | solution.py:321
  51.6 4.2 %collective-permute-start = (f32[8,128]{1,0:T(8,128)S(1)}, f32[8,128]{1,0:T(8,128)S(1)}, u32[]{:S(2)}, u32[]{:S(2)}) collective-permute-start(f32[8,128]{1,0:T(8,128)S(1)} %get-tuple-element.35), channel_id=1, source_target_pairs={{0,16},{16,0},{32,48},{48,32},{64,80},{80,64},{96,112},{112,96},{1... | collective-permute-start | bytes 12296 | tf_op jit(solution)/shard_map/ppermute | solution.py:321
  55.8 10.5 %collective-permute-start.5 = (f32[8,128]{1,0:T(8,128)S(1)}, f32[8,128]{1,0:T(8,128)S(1)}, u32[]{:S(2)}, u32[]{:S(2)}) collective-permute-start(f32[8,128]{1,0:T(8,128)S(1)} %add_add_fusion.1), channel_id=1, source_target_pairs={{0,96},{16,112},{32,64},{48,80},{64,32},{80,48},{96,0},{112,16},{1... | collective-permute-start | bytes 12296 | tf_op jit(solution)/shard_map/ppermute | solution.py:321
  58.4 8.1 %collective-permute-start.4 = (f32[8,128]{1,0:T(8,128)S(1)}, f32[8,128]{1,0:T(8,128)S(1)}, u32[]{:S(2)}, u32[]{:S(2)}) collective-permute-start(f32[8,128]{1,0:T(8,128)S(1)} %add_add_fusion.1), channel_id=1, source_target_pairs={{0,64},{16,80},{32,96},{48,112},{64,0},{80,16},{96,32},{112,48},{1... | collective-permute-start | bytes 12296 | tf_op jit(solution)/shard_map/ppermute | solution.py:321
  64.9 3.6 %collective-permute-start.3 = (f32[8,128]{1,0:T(8,128)S(1)}, f32[8,128]{1,0:T(8,128)S(1)}, u32[]{:S(2)}, u32[]{:S(2)}) collective-permute-start(f32[8,128]{1,0:T(8,128)S(1)} %add_add_fusion.1), channel_id=1, source_target_pairs={{0,32},{16,48},{32,0},{48,16},{64,96},{80,112},{96,64},{112,80},{1... | collective-permute-start | bytes 12296 | tf_op jit(solution)/shard_map/ppermute | solution.py:321
  70.1 17.3 %all-to-all-start.3 = ((bf16[16,144,128]{2,1,0:T(8,128)(2,1)}), bf16[16,144,128]{2,1,0:T(8,128)(2,1)S(1)}, u32[]{:S(2)}, u32[]{:S(2)}) async-start(bf16[16,144,128]{2,1,0:T(8,128)(2,1)} %sum_partials.1), calls=%async_computation.3 | async-start | bytes 1179648 | tf_op jit(solution)/shard_map/all_to_all | solution.py:403

commit v9 on v8

--- a/solution.py
+++ b/solution.py
@@ -320,12 +320,13 @@
     def moved(step):
         return lax.ppermute(x, axis, [(i, i ^ step) for i in range(size)])
 
-    steps = [1 << bit for bit in range(size.bit_length() - 1)]
-    while len(steps) > 1:
-        near, far = steps.pop(0), steps.pop()
-        x = (x + moved(near)) + (moved(far) + moved(near + far))
-    for step in steps:
-        x = x + moved(step)
+    step = 1
+    if size >= 4:
+        x = (x + moved(1)) + (moved(2) + moved(3))
+        step = 4
+    while step < size:
+        x = x + moved(step if step < 8 else step + step // 2)
+        step *= 2
     return x
 
 

time: 89.5 us -> 85.8 us (0.959); the launches traced: 89.1 us -> 87.2 us
  waiting for transfers between devices: 25.3 us -> 23.6 us
  starting transfers between devices: 34.6 us -> 33 us
  Pallas kernels: 10.9 us -> 12.4 us
    ppermute x6 -> x5, starting transfers between devices: 17 us -> 15.1 us  [moved(): return lax.ppermute(x, axis, [(i, i ^ step) for i in range(size)])]
    ppermute x6 -> x5, waiting for transfers between devices: 6.45 us -> 4.74 us  [moved(): return lax.ppermute(x, axis, [(i, i ^ step) for i in range(size)])]
    pallas_call x6, Pallas kernels: 8.94 us -> 10.4 us  [call(): pl.pallas_call(kernel, out_shape=outs, in_specs=[SMEM()] * len(smem) + [V...]
  transfers between devices with their start and end apart: 9 -> 8, of which waited for: 6 -> 5; matrix products, arithmetic and copies ran while one was open for 0% -> 0% of each run, Pallas kernels for 2% -> 2%
where the time goes in v9:
time: 85.8 us; the launch traced here: 87.2 us
  starting transfers between devices  33 us (38%)
  waiting for transfers between devices  23.6 us (28%)
  blocking collectives  16.2 us (19%)
  Pallas kernels  12.4 us (14%)
  between operations  1.39 us (2%)
    all_to_all x1, blocking collectives, after_scatter(): kv_cited = lax.all_to_all(cited, 'seq', 0, 0)  16.2 us
    ppermute x5, starting transfers between devices, moved(): return lax.ppermute(x, axis, [(i, i ^ step) for i in range(size)])  15.1 us
    pallas_call x6, Pallas kernels, call(): pl.pallas_call(kernel, out_shape=outs, in_specs=[SMEM()] * len(smem) + [V...  10.4 us
    all_to_all x1, waiting for transfers between devices, per_device(): chunks = lax.all_to_all(chunks, 'seq', 0, 0)  9.5 us
    all_to_all x1, waiting for transfers between devices, after_scatter(): owned = lax.all_to_all(summed, 'seq', 0, 0)  9.32 us
    all_to_all x1, starting transfers between devices, per_device(): chunks = lax.all_to_all(chunks, 'seq', 0, 0)  7.18 us
    all_to_all x1, starting transfers between devices, after_scatter(): owned = lax.all_to_all(summed, 'seq', 0, 0)  7.12 us
    ppermute x5, waiting for transfers between devices, moved(): return lax.ppermute(x, axis, [(i, i ^ step) for i in range(size)])  4.74 us
  transfers between devices with their start and end apart: 8, of which 5 were waited for; matrix products, arithmetic and copies ran while one was open for 0% of the time, Pallas kernels for 2%

profile of v9, /device:TPU:32, one launch (start us, length us, event | category | flops | bytes accessed | tf_op | source)
XLA Modules:
  0.0 87.2 jit_solution(5035222736602963237)
XLA Ops:
  0.6 2.0 %pack_chunks.1 = (bf16[16,64,256]{2,1,0:T(8,128)(2,1)}, s32[56]{0:T(128)}) custom-call(s32[6,16]{1,0:T(8,128)} %bitcast.7, s32[16]{0:T(128)} %counts_hbm.1, s32[1024]{0:T(1024)} %tiles_hbm.1, bf16[4,256,256]{2,1,0:T(8,128)(2,1)} %image_hbm.1), custom_call_target="tpu_custom_call" | custom-call | tf_op jit(solution)/shard_map/pack_chunks/pallas_call | solution.py:424
  2.6 0.0 copy-start
  2.6 7.2 %all-to-all-start = ((bf16[16,64,256]{2,1,0:T(8,128)(2,1)}), bf16[16,64,256]{2,1,0:T(8,128)(2,1)S(1)}, u32[]{:S(2)}, u32[]{:S(2)}) async-start(bf16[16,64,256]{2,1,0:T(8,128)(2,1)} %get-tuple-element.22), calls=%async_computation | async-start | bytes 1048576 | tf_op jit(solution)/shard_map/all_to_all | solution.py:442
  10.5 0.0 copy-start.2
  10.5 0.6 copy-done.2
  11.1 0.7 prepare_rows.1
  11.8 9.5 %all-to-all-done.chunks_ref = bf16[16,64,256]{2,1,0:T(8,128)(2,1)S(1)} async-done(((bf16[16,64,256]{2,1,0:T(8,128)(2,1)}), bf16[16,64,256]{2,1,0:T(8,128)(2,1)S(1)}, u32[]{:S(2)}, u32[]{:S(2)}) %all-to-all-start) | async-done | bytes 524320 | tf_op jit(solution)/shard_map/all_to_all | solution.py:442
  21.3 0.7 select_cited.1
  22.0 16.2 %all_to_all.20.kv_ref = bf16[16,96,256]{2,1,0:T(8,128)(2,1)S(1)} all-to-all(bf16[16,96,256]{2,1,0:T(8,128)(2,1)S(1)} %select_cited.1), channel_id=1, replica_groups=mesh['dp'=16,'seq'=16] {'seq'}, dimensions={0} | all-to-all | bytes 1572864 | tf_op jit(solution)/shard_map/all_to_all | solution.py:368
  38.2 4.7 %attention.1 = (f32[128,1024]{1,0:T(8,128)S(1)}, f32[128,1024]{1,0:T(8,128)S(1)}, bf16[16,96,256]{2,1,0:T(8,128)(2,1)}, f32[8,128]{1,0:T(8,128)S(1)}) custom-call(s32[56]{0:T(128)S(1)} %copy-done.2, f32[1]{0:T(128)S(6)} %copy.11.gate, bf16[16,96,256]{2,1,0:T(8,128)(2,1)S(1)} %all_to_all.20.kv_ref, bf16[1024,128]{1,0:T(8,128)(2,1)S(1)} %get-tuple-element.27.query_rows, ...), custom_call_target="tpu_custom_call" | custom-call | tf_op jit(solution)/shard_map/attention/pallas_call | solution.py:334
  42.9 3.6 %all-to-all-start.2 = ((bf16[16,96,256]{2,1,0:T(8,128)(2,1)}), bf16[16,96,256]{2,1,0:T(8,128)(2,1)S(1)}, u32[]{:S(2)}, u32[]{:S(2)}) async-start(bf16[16,96,256]{2,1,0:T(8,128)(2,1)} %get-tuple-element.34), calls=%async_computation.2 | async-start | bytes 1572864 | tf_op jit(solution)/shard_map/all_to_all | solution.py:391
  46.6 0.1 collective-permute-start.2
  46.7 3.2 %collective-permute-start.1 = (f32[8,128]{1,0:T(8,128)S(1)}, f32[8,128]{1,0:T(8,128)S(1)}, u32[]{:S(2)}, u32[]{:S(2)}) collective-permute-start(f32[8,128]{1,0:T(8,128)S(1)} %get-tuple-element.35), channel_id=1, source_target_pairs={{0,32},{16,48},{32,0},{48,16},{64,96},{80,112},{96,64},{112,80},{1... | collective-permute-start | bytes 12296 | tf_op jit(solution)/shard_map/ppermute | solution.py:321
  49.9 0.0 collective-permute-start
  49.9 1.6 %collective-permute-done.1 = f32[8,128]{1,0:T(8,128)S(1)} collective-permute-done((f32[8,128]{1,0:T(8,128)S(1)}, f32[8,128]{1,0:T(8,128)S(1)}, u32[]{:S(2)}, u32[]{:S(2)}) %collective-permute-start.1) | collective-permute-done | bytes 4128 | tf_op jit(solution)/shard_map/ppermute | solution.py:321
  51.5 3.4 %collective-permute-start.3 = (f32[8,128]{1,0:T(8,128)S(1)}, f32[8,128]{1,0:T(8,128)S(1)}, u32[]{:S(2)}, u32[]{:S(2)}) collective-permute-start(f32[8,128]{1,0:T(8,128)S(1)} %add_add_fusion), channel_id=1, source_target_pairs={{0,64},{16,80},{32,96},{48,112},{64,0},{80,16},{96,32},{112,48},{1... | collective-permute-start | bytes 12296 | tf_op jit(solution)/shard_map/ppermute | solution.py:321
  54.8 1.6 %collective-permute-done.3 = f32[8,128]{1,0:T(8,128)S(1)} collective-permute-done((f32[8,128]{1,0:T(8,128)S(1)}, f32[8,128]{1,0:T(8,128)S(1)}, u32[]{:S(2)}, u32[]{:S(2)}) %collective-permute-start.3) | collective-permute-done | bytes 4128 | tf_op jit(solution)/shard_map/ppermute | solution.py:321
  56.4 8.4 %collective-permute-start.4 = (f32[8,128]{1,0:T(8,128)S(1)}, f32[8,128]{1,0:T(8,128)S(1)}, u32[]{:S(2)}, u32[]{:S(2)}) collective-permute-start(f32[8,128]{1,0:T(8,128)S(1)} %add.18), channel_id=1, source_target_pairs={{0,192},{16,208},{32,224},{48,240},{64,128},{80,144},{96,160},{112... | collective-permute-start | bytes 12296 | tf_op jit(solution)/shard_map/ppermute | solution.py:321
  64.8 1.6 %collective-permute-done.4 = f32[8,128]{1,0:T(8,128)S(1)} collective-permute-done((f32[8,128]{1,0:T(8,128)S(1)}, f32[8,128]{1,0:T(8,128)S(1)}, u32[]{:S(2)}, u32[]{:S(2)}) %collective-permute-start.4) | collective-permute-done | bytes 4128 | tf_op jit(solution)/shard_map/ppermute | solution.py:321
  66.4 1.6 %sum_partials.1 = bf16[16,144,128]{2,1,0:T(8,128)(2,1)} custom-call(s32[56]{0:T(128)S(1)} %copy-done.2, bf16[16,96,256]{2,1,0:T(8,128)(2,1)S(1)} %all-to-all-done.2.partial_ref, f32[8,128]{1,0:T(8,128)S(1)} %add.19.gate_ref), custom_call_target="tpu_custom_call" | custom-call | tf_op jit(solution)/shard_map/sum_partials/pallas_call | solution.py:334
  68.0 7.1 %all-to-all-start.3 = ((bf16[16,144,128]{2,1,0:T(8,128)(2,1)}), bf16[16,144,128]{2,1,0:T(8,128)(2,1)S(1)}, u32[]{:S(2)}, u32[]{:S(2)}) async-start(bf16[16,144,128]{2,1,0:T(8,128)(2,1)} %sum_partials.1), calls=%async_computation.3 | async-start | bytes 1179648 | tf_op jit(solution)/shard_map/all_to_all | solution.py:404
  75.1 1.1 %finish_rows.1 = (bf16[128,1024]{1,0:T(8,128)(2,1)}, bf16[128,1024]{1,0:T(8,128)(2,1)}) custom-call(f32[1]{0:T(128)S(6)} %copy.11.gate, f32[128,1024]{1,0:T(8,128)S(1)} %get-tuple-element.30.attn_t, f32[128,1024]{1,0:T(8,128)S(1)} %get-tuple-element.31.dquery_t), custom_call_target="tpu_custom_call" | custom-call | tf_op jit(solution)/shard_map/finish_rows/pallas_call | solution.py:334
  76.3 9.3 %all-to-all-done.3.owned_ref = bf16[16,144,128]{2,1,0:T(8,128)(2,1)S(1)} async-done(((bf16[16,144,128]{2,1,0:T(8,128)(2,1)}), bf16[16,144,128]{2,1,0:T(8,128)(2,1)S(1)}, u32[]{:S(2)}, u32[]{:S(2)}) %all-to-all-start.3) | async-done | bytes 589856 | tf_op jit(solution)/shard_map/all_to_all | solution.py:404
  85.6 1.7 %unpack_grads.1 = (f32[4,256,256]{2,1,0:T(8,128)}, f32[1]{0:T(128)}) custom-call(s32[56]{0:T(128)S(1)} %copy-done.2, f32[1]{0:T(128)S(6)} %copy.11.gate, bf16[16,144,128]{2,1,0:T(8,128)(2,1)S(1)} %all-to-all-done.3.owned_ref), custom_call_target="tpu_custom_call" | custom-call | tf_op jit(solution)/shard_map/unpack_grads/pallas_call | solution.py:334
  (9 shorter events, 0.0 us)
Async XLA Ops:
  2.6 7.9 %copy-start = (bf16[1,128,1024]{2,1,0:T(8,128)(2,1)S(1)}, bf16[1,128,1024]{2,1,0:T(8,128)(2,1)}, u32[]{:S(2)}) copy-start(bf16[1,128,1024]{2,1,0:T(8,128)(2,1)} %param.7) | copy-start | bytes 786436
  2.6 7.9 %copy-start.1 = (bf16[1,128,1024]{2,1,0:T(8,128)(2,1)S(1)}, bf16[1,128,1024]{2,1,0:T(8,128)(2,1)}, u32[]{:S(2)}) copy-start(bf16[1,128,1024]{2,1,0:T(8,128)(2,1)} %param.8) | copy-start | bytes 786436
  2.6 18.7 %all-to-all-start = ((bf16[16,64,256]{2,1,0:T(8,128)(2,1)}), bf16[16,64,256]{2,1,0:T(8,128)(2,1)S(1)}, u32[]{:S(2)}, u32[]{:S(2)}) async-start(bf16[16,64,256]{2,1,0:T(8,128)(2,1)} %get-tuple-element.22), calls=%async_computation | async-start | bytes 1048576 | tf_op jit(solution)/shard_map/all_to_all | solution.py:442
  10.5 0.7 copy-start.2
  42.9 23.5 %all-to-all-start.2 = ((bf16[16,96,256]{2,1,0:T(8,128)(2,1)}), bf16[16,96,256]{2,1,0:T(8,128)(2,1)S(1)}, u32[]{:S(2)}, u32[]{:S(2)}) async-start(bf16[16,96,256]{2,1,0:T(8,128)(2,1)} %get-tuple-element.34), calls=%async_computation.2 | async-start | bytes 1572864 | tf_op jit(solution)/shard_map/all_to_all | solution.py:391
  46.6 3.3 %collective-permute-start.2 = (f32[8,128]{1,0:T(8,128)S(1)}, f32[8,128]{1,0:T(8,128)S(1)}, u32[]{:S(2)}, u32[]{:S(2)}) collective-permute-start(f32[8,128]{1,0:T(8,128)S(1)} %get-tuple-element.35), channel_id=1, source_target_pairs={{0,48},{16,32},{32,16},{48,0},{64,112},{80,96},{96,80},{112,64},{1... | collective-permute-start | bytes 12296 | tf_op jit(solution)/shard_map/ppermute | solution.py:321
  46.7 4.8 %collective-permute-start.1 = (f32[8,128]{1,0:T(8,128)S(1)}, f32[8,128]{1,0:T(8,128)S(1)}, u32[]{:S(2)}, u32[]{:S(2)}) collective-permute-start(f32[8,128]{1,0:T(8,128)S(1)} %get-tuple-element.35), channel_id=1, source_target_pairs={{0,32},{16,48},{32,0},{48,16},{64,96},{80,112},{96,64},{112,80},{1... | collective-permute-start | bytes 12296 | tf_op jit(solution)/shard_map/ppermute | solution.py:321
  49.9 1.6 %collective-permute-start = (f32[8,128]{1,0:T(8,128)S(1)}, f32[8,128]{1,0:T(8,128)S(1)}, u32[]{:S(2)}, u32[]{:S(2)}) collective-permute-start(f32[8,128]{1,0:T(8,128)S(1)} %get-tuple-element.35), channel_id=1, source_target_pairs={{0,16},{16,0},{32,48},{48,32},{64,80},{80,64},{96,112},{112,96},{1... | collective-permute-start | bytes 12296 | tf_op jit(solution)/shard_map/ppermute | solution.py:321
  51.5 4.9 %collective-permute-start.3 = (f32[8,128]{1,0:T(8,128)S(1)}, f32[8,128]{1,0:T(8,128)S(1)}, u32[]{:S(2)}, u32[]{:S(2)}) collective-permute-start(f32[8,128]{1,0:T(8,128)S(1)} %add_add_fusion), channel_id=1, source_target_pairs={{0,64},{16,80},{32,96},{48,112},{64,0},{80,16},{96,32},{112,48},{1... | collective-permute-start | bytes 12296 | tf_op jit(solution)/shard_map/ppermute | solution.py:321
  56.4 10.0 %collective-permute-start.4 = (f32[8,128]{1,0:T(8,128)S(1)}, f32[8,128]{1,0:T(8,128)S(1)}, u32[]{:S(2)}, u32[]{:S(2)}) collective-permute-start(f32[8,128]{1,0:T(8,128)S(1)} %add.18), channel_id=1, source_target_pairs={{0,192},{16,208},{32,224},{48,240},{64,128},{80,144},{96,160},{112... | collective-permute-start | bytes 12296 | tf_op jit(solution)/shard_map/ppermute | solution.py:321
  68.0 17.6 %all-to-all-start.3 = ((bf16[16,144,128]{2,1,0:T(8,128)(2,1)}), bf16[16,144,128]{2,1,0:T(8,128)(2,1)S(1)}, u32[]{:S(2)}, u32[]{:S(2)}) async-start(bf16[16,144,128]{2,1,0:T(8,128)(2,1)} %sum_partials.1), calls=%async_computation.3 | async-start | bytes 1179648 | tf_op jit(solution)/shard_map/all_to_all | solution.py:404

commit v10 on v9

--- a/solution.py
+++ b/solution.py
@@ -324,8 +324,11 @@
     if size >= 4:
         x = (x + moved(1)) + (moved(2) + moved(3))
         step = 4
+    if size >= 16:
+        x = (x + moved(4)) + (moved(10) + moved(12))
+        step = 16
     while step < size:
-        x = x + moved(step if step < 8 else step + step // 2)
+        x = x + moved(step)
         step *= 2
     return x
 

time: 85.8 us -> 84.6 us (0.986); the launches traced: 87.2 us -> 84.3 us
  starting transfers between devices: 33 us -> 31.3 us
  Pallas kernels: 12.4 us -> 10.9 us
    ppermute x5 -> x6, starting transfers between devices: 15.1 us -> 13.4 us  [moved(): return lax.ppermute(x, axis, [(i, i ^ step) for i in range(size)])]
    pallas_call x6, Pallas kernels: 10.4 us -> 8.94 us  [call(): pl.pallas_call(kernel, out_shape=outs, in_specs=[SMEM()] * len(smem) + [V...]
    all_to_all x1, waiting for transfers between devices: 9.32 us -> 10.3 us  [after_scatter(): owned = lax.all_to_all(summed, 'seq', 0, 0)]
    ppermute x5 -> x6, waiting for transfers between devices: 4.74 us -> 3.97 us  [moved(): return lax.ppermute(x, axis, [(i, i ^ step) for i in range(size)])]
  transfers between devices with their start and end apart: 8 -> 9, of which waited for: 5 -> 4; matrix products, arithmetic and copies ran while one was open for 0% -> 0% of each run, Pallas kernels for 2% -> 2%
where the time goes in v10:
time: 84.6 us; the launch traced here: 84.3 us
  starting transfers between devices  31.3 us (37%)
  waiting for transfers between devices  23.8 us (28%)
  blocking collectives  16.2 us (19%)
  Pallas kernels  10.9 us (13%)
  between operations  1.4 us (2%)
    all_to_all x1, blocking collectives, after_scatter(): kv_cited = lax.all_to_all(cited, 'seq', 0, 0)  16.2 us
    ppermute x6, starting transfers between devices, moved(): return lax.ppermute(x, axis, [(i, i ^ step) for i in range(size)])  13.4 us
    all_to_all x1, waiting for transfers between devices, after_scatter(): owned = lax.all_to_all(summed, 'seq', 0, 0)  10.3 us
    all_to_all x1, waiting for transfers between devices, per_device(): chunks = lax.all_to_all(chunks, 'seq', 0, 0)  9.5 us
    pallas_call x6, Pallas kernels, call(): pl.pallas_call(kernel, out_shape=outs, in_specs=[SMEM()] * len(smem) + [V...  8.94 us
    all_to_all x1, starting transfers between devices, per_device(): chunks = lax.all_to_all(chunks, 'seq', 0, 0)  7.18 us
    all_to_all x1, starting transfers between devices, after_scatter(): owned = lax.all_to_all(summed, 'seq', 0, 0)  7.12 us
    ppermute x6, waiting for transfers between devices, moved(): return lax.ppermute(x, axis, [(i, i ^ step) for i in range(size)])  3.97 us
  transfers between devices with their start and end apart: 9, of which 4 were waited for; matrix products, arithmetic and copies ran while one was open for 0% of the time, Pallas kernels for 2%

profile of v10, /device:TPU:32, one launch (start us, length us, event | category | flops | bytes accessed | tf_op | source)
XLA Modules:
  0.0 84.3 jit_solution(14215901430991531313)
XLA Ops:
  0.6 2.0 %pack_chunks.1 = (bf16[16,64,256]{2,1,0:T(8,128)(2,1)}, s32[56]{0:T(128)}) custom-call(s32[6,16]{1,0:T(8,128)} %bitcast.7, s32[16]{0:T(128)} %counts_hbm.1, s32[1024]{0:T(1024)} %tiles_hbm.1, bf16[4,256,256]{2,1,0:T(8,128)(2,1)} %image_hbm.1), custom_call_target="tpu_custom_call" | custom-call | tf_op jit(solution)/shard_map/pack_chunks/pallas_call | solution.py:427
  2.6 0.0 copy-start
  2.6 7.2 %all-to-all-start = ((bf16[16,64,256]{2,1,0:T(8,128)(2,1)}), bf16[16,64,256]{2,1,0:T(8,128)(2,1)S(1)}, u32[]{:S(2)}, u32[]{:S(2)}) async-start(bf16[16,64,256]{2,1,0:T(8,128)(2,1)} %get-tuple-element.22), calls=%async_computation | async-start | bytes 1048576 | tf_op jit(solution)/shard_map/all_to_all | solution.py:445
  10.5 0.0 copy-start.2
  10.5 0.6 copy-done.2
  11.1 0.7 prepare_rows.1
  11.8 9.5 %all-to-all-done.chunks_ref = bf16[16,64,256]{2,1,0:T(8,128)(2,1)S(1)} async-done(((bf16[16,64,256]{2,1,0:T(8,128)(2,1)}), bf16[16,64,256]{2,1,0:T(8,128)(2,1)S(1)}, u32[]{:S(2)}, u32[]{:S(2)}) %all-to-all-start) | async-done | bytes 524320 | tf_op jit(solution)/shard_map/all_to_all | solution.py:445
  21.3 0.7 select_cited.1
  22.0 16.2 %all_to_all.20.kv_ref = bf16[16,96,256]{2,1,0:T(8,128)(2,1)S(1)} all-to-all(bf16[16,96,256]{2,1,0:T(8,128)(2,1)S(1)} %select_cited.1), channel_id=1, replica_groups=mesh['dp'=16,'seq'=16] {'seq'}, dimensions={0} | all-to-all | bytes 1572864 | tf_op jit(solution)/shard_map/all_to_all | solution.py:371
  38.2 3.3 %attention.1 = (f32[128,1024]{1,0:T(8,128)S(1)}, f32[128,1024]{1,0:T(8,128)S(1)}, bf16[16,96,256]{2,1,0:T(8,128)(2,1)}, f32[8,128]{1,0:T(8,128)S(1)}) custom-call(s32[56]{0:T(128)S(1)} %copy-done.2, f32[1]{0:T(128)S(6)} %copy.11.gate, bf16[16,96,256]{2,1,0:T(8,128)(2,1)S(1)} %all_to_all.20.kv_ref, bf16[1024,128]{1,0:T(8,128)(2,1)S(1)} %get-tuple-element.27.query_rows, ...), custom_call_target="tpu_custom_call" | custom-call | tf_op jit(solution)/shard_map/attention/pallas_call | solution.py:337
  41.4 3.6 %all-to-all-start.2 = ((bf16[16,96,256]{2,1,0:T(8,128)(2,1)}), bf16[16,96,256]{2,1,0:T(8,128)(2,1)S(1)}, u32[]{:S(2)}, u32[]{:S(2)}) async-start(bf16[16,96,256]{2,1,0:T(8,128)(2,1)} %get-tuple-element.34), calls=%async_computation.2 | async-start | bytes 1572864 | tf_op jit(solution)/shard_map/all_to_all | solution.py:394
  45.1 0.1 collective-permute-start.2
  45.2 6.2 %collective-permute-start.1 = (f32[8,128]{1,0:T(8,128)S(1)}, f32[8,128]{1,0:T(8,128)S(1)}, u32[]{:S(2)}, u32[]{:S(2)}) collective-permute-start(f32[8,128]{1,0:T(8,128)S(1)} %get-tuple-element.35), channel_id=1, source_target_pairs={{0,32},{16,48},{32,0},{48,16},{64,96},{80,112},{96,64},{112,80},{1... | collective-permute-start | bytes 12296 | tf_op jit(solution)/shard_map/ppermute | solution.py:321
  51.3 0.0 collective-permute-start
  51.4 1.6 %collective-permute-done.1 = f32[8,128]{1,0:T(8,128)S(1)} collective-permute-done((f32[8,128]{1,0:T(8,128)S(1)}, f32[8,128]{1,0:T(8,128)S(1)}, u32[]{:S(2)}, u32[]{:S(2)}) %collective-permute-start.1) | collective-permute-done | bytes 4128 | tf_op jit(solution)/shard_map/ppermute | solution.py:321
  52.9 2.9 %collective-permute-start.5 = (f32[8,128]{1,0:T(8,128)S(1)}, f32[8,128]{1,0:T(8,128)S(1)}, u32[]{:S(2)}, u32[]{:S(2)}) collective-permute-start(f32[8,128]{1,0:T(8,128)S(1)} %add_add_fusion.1), channel_id=1, source_target_pairs={{0,192},{16,208},{32,224},{48,240},{64,128},{80,144},{96,160},{112... | collective-permute-start | bytes 12296 | tf_op jit(solution)/shard_map/ppermute | solution.py:321
  55.9 1.6 %collective-permute-start.4 = (f32[8,128]{1,0:T(8,128)S(1)}, f32[8,128]{1,0:T(8,128)S(1)}, u32[]{:S(2)}, u32[]{:S(2)}) collective-permute-start(f32[8,128]{1,0:T(8,128)S(1)} %add_add_fusion.1), channel_id=1, source_target_pairs={{0,160},{16,176},{32,128},{48,144},{64,224},{80,240},{96,192},{112... | collective-permute-start | bytes 12296 | tf_op jit(solution)/shard_map/ppermute | solution.py:321
  57.5 2.6 %collective-permute-start.3 = (f32[8,128]{1,0:T(8,128)S(1)}, f32[8,128]{1,0:T(8,128)S(1)}, u32[]{:S(2)}, u32[]{:S(2)}) collective-permute-start(f32[8,128]{1,0:T(8,128)S(1)} %add_add_fusion.1), channel_id=1, source_target_pairs={{0,64},{16,80},{32,96},{48,112},{64,0},{80,16},{96,32},{112,48},{1... | collective-permute-start | bytes 12296 | tf_op jit(solution)/shard_map/ppermute | solution.py:321
  60.1 2.4 %collective-permute-done.4 = f32[8,128]{1,0:T(8,128)S(1)} collective-permute-done((f32[8,128]{1,0:T(8,128)S(1)}, f32[8,128]{1,0:T(8,128)S(1)}, u32[]{:S(2)}, u32[]{:S(2)}) %collective-permute-start.4) | collective-permute-done | bytes 4128 | tf_op jit(solution)/shard_map/ppermute | solution.py:321
  62.5 1.6 %sum_partials.1 = bf16[16,144,128]{2,1,0:T(8,128)(2,1)} custom-call(s32[56]{0:T(128)S(1)} %copy-done.2, bf16[16,96,256]{2,1,0:T(8,128)(2,1)S(1)} %all-to-all-done.2.partial_ref, f32[8,128]{1,0:T(8,128)S(1)} %add_add_fusion.gate_ref), custom_call_target="tpu_custom_call" | custom-call | tf_op jit(solution)/shard_map/sum_partials/pallas_call | solution.py:337
  64.1 7.1 %all-to-all-start.3 = ((bf16[16,144,128]{2,1,0:T(8,128)(2,1)}), bf16[16,144,128]{2,1,0:T(8,128)(2,1)S(1)}, u32[]{:S(2)}, u32[]{:S(2)}) async-start(bf16[16,144,128]{2,1,0:T(8,128)(2,1)} %sum_partials.1), calls=%async_computation.3 | async-start | bytes 1179648 | tf_op jit(solution)/shard_map/all_to_all | solution.py:407
  71.2 1.1 %finish_rows.1 = (bf16[128,1024]{1,0:T(8,128)(2,1)}, bf16[128,1024]{1,0:T(8,128)(2,1)}) custom-call(f32[1]{0:T(128)S(6)} %copy.11.gate, f32[128,1024]{1,0:T(8,128)S(1)} %get-tuple-element.30.attn_t, f32[128,1024]{1,0:T(8,128)S(1)} %get-tuple-element.31.dquery_t), custom_call_target="tpu_custom_call" | custom-call | tf_op jit(solution)/shard_map/finish_rows/pallas_call | solution.py:337
  72.3 10.3 %all-to-all-done.3.owned_ref = bf16[16,144,128]{2,1,0:T(8,128)(2,1)S(1)} async-done(((bf16[16,144,128]{2,1,0:T(8,128)(2,1)}), bf16[16,144,128]{2,1,0:T(8,128)(2,1)S(1)}, u32[]{:S(2)}, u32[]{:S(2)}) %all-to-all-start.3) | async-done | bytes 589856 | tf_op jit(solution)/shard_map/all_to_all | solution.py:407
  82.7 1.7 %unpack_grads.1 = (f32[4,256,256]{2,1,0:T(8,128)}, f32[1]{0:T(128)}) custom-call(s32[56]{0:T(128)S(1)} %copy-done.2, f32[1]{0:T(128)S(6)} %copy.11.gate, bf16[16,144,128]{2,1,0:T(8,128)(2,1)S(1)} %all-to-all-done.3.owned_ref), custom_call_target="tpu_custom_call" | custom-call | tf_op jit(solution)/shard_map/unpack_grads/pallas_call | solution.py:337
  (10 shorter events, 0.0 us)
Async XLA Ops:
  2.6 7.9 %copy-start = (bf16[1,128,1024]{2,1,0:T(8,128)(2,1)S(1)}, bf16[1,128,1024]{2,1,0:T(8,128)(2,1)}, u32[]{:S(2)}) copy-start(bf16[1,128,1024]{2,1,0:T(8,128)(2,1)} %param.7) | copy-start | bytes 786436
  2.6 7.9 %copy-start.1 = (bf16[1,128,1024]{2,1,0:T(8,128)(2,1)S(1)}, bf16[1,128,1024]{2,1,0:T(8,128)(2,1)}, u32[]{:S(2)}) copy-start(bf16[1,128,1024]{2,1,0:T(8,128)(2,1)} %param.8) | copy-start | bytes 786436
  2.6 18.7 %all-to-all-start = ((bf16[16,64,256]{2,1,0:T(8,128)(2,1)}), bf16[16,64,256]{2,1,0:T(8,128)(2,1)S(1)}, u32[]{:S(2)}, u32[]{:S(2)}) async-start(bf16[16,64,256]{2,1,0:T(8,128)(2,1)} %get-tuple-element.22), calls=%async_computation | async-start | bytes 1048576 | tf_op jit(solution)/shard_map/all_to_all | solution.py:445
  10.5 0.7 copy-start.2
  41.4 21.1 %all-to-all-start.2 = ((bf16[16,96,256]{2,1,0:T(8,128)(2,1)}), bf16[16,96,256]{2,1,0:T(8,128)(2,1)S(1)}, u32[]{:S(2)}, u32[]{:S(2)}) async-start(bf16[16,96,256]{2,1,0:T(8,128)(2,1)} %get-tuple-element.34), calls=%async_computation.2 | async-start | bytes 1572864 | tf_op jit(solution)/shard_map/all_to_all | solution.py:394
  45.1 6.3 %collective-permute-start.2 = (f32[8,128]{1,0:T(8,128)S(1)}, f32[8,128]{1,0:T(8,128)S(1)}, u32[]{:S(2)}, u32[]{:S(2)}) collective-permute-start(f32[8,128]{1,0:T(8,128)S(1)} %get-tuple-element.35), channel_id=1, source_target_pairs={{0,48},{16,32},{32,16},{48,0},{64,112},{80,96},{96,80},{112,64},{1... | collective-permute-start | bytes 12296 | tf_op jit(solution)/shard_map/ppermute | solution.py:321
  45.2 7.7 %collective-permute-start.1 = (f32[8,128]{1,0:T(8,128)S(1)}, f32[8,128]{1,0:T(8,128)S(1)}, u32[]{:S(2)}, u32[]{:S(2)}) collective-permute-start(f32[8,128]{1,0:T(8,128)S(1)} %get-tuple-element.35), channel_id=1, source_target_pairs={{0,32},{16,48},{32,0},{48,16},{64,96},{80,112},{96,64},{112,80},{1... | collective-permute-start | bytes 12296 | tf_op jit(solution)/shard_map/ppermute | solution.py:321
  51.3 1.6 %collective-permute-start = (f32[8,128]{1,0:T(8,128)S(1)}, f32[8,128]{1,0:T(8,128)S(1)}, u32[]{:S(2)}, u32[]{:S(2)}) collective-permute-start(f32[8,128]{1,0:T(8,128)S(1)} %get-tuple-element.35), channel_id=1, source_target_pairs={{0,16},{16,0},{32,48},{48,32},{64,80},{80,64},{96,112},{112,96},{1... | collective-permute-start | bytes 12296 | tf_op jit(solution)/shard_map/ppermute | solution.py:321
  52.9 7.1 %collective-permute-start.5 = (f32[8,128]{1,0:T(8,128)S(1)}, f32[8,128]{1,0:T(8,128)S(1)}, u32[]{:S(2)}, u32[]{:S(2)}) collective-permute-start(f32[8,128]{1,0:T(8,128)S(1)} %add_add_fusion.1), channel_id=1, source_target_pairs={{0,192},{16,208},{32,224},{48,240},{64,128},{80,144},{96,160},{112... | collective-permute-start | bytes 12296 | tf_op jit(solution)/shard_map/ppermute | solution.py:321
  55.9 6.6 %collective-permute-start.4 = (f32[8,128]{1,0:T(8,128)S(1)}, f32[8,128]{1,0:T(8,128)S(1)}, u32[]{:S(2)}, u32[]{:S(2)}) collective-permute-start(f32[8,128]{1,0:T(8,128)S(1)} %add_add_fusion.1), channel_id=1, source_target_pairs={{0,160},{16,176},{32,128},{48,144},{64,224},{80,240},{96,192},{112... | collective-permute-start | bytes 12296 | tf_op jit(solution)/shard_map/ppermute | solution.py:321
  57.5 5.0 %collective-permute-start.3 = (f32[8,128]{1,0:T(8,128)S(1)}, f32[8,128]{1,0:T(8,128)S(1)}, u32[]{:S(2)}, u32[]{:S(2)}) collective-permute-start(f32[8,128]{1,0:T(8,128)S(1)} %add_add_fusion.1), channel_id=1, source_target_pairs={{0,64},{16,80},{32,96},{48,112},{64,0},{80,16},{96,32},{112,48},{1... | collective-permute-start | bytes 12296 | tf_op jit(solution)/shard_map/ppermute | solution.py:321
  64.1 18.6 %all-to-all-start.3 = ((bf16[16,144,128]{2,1,0:T(8,128)(2,1)}), bf16[16,144,128]{2,1,0:T(8,128)(2,1)S(1)}, u32[]{:S(2)}, u32[]{:S(2)}) async-start(bf16[16,144,128]{2,1,0:T(8,128)(2,1)} %sum_partials.1), calls=%async_computation.3 | async-start | bytes 1179648 | tf_op jit(solution)/shard_map/all_to_all | solution.py:407

commit v11 on v9

--- a/solution.py
+++ b/solution.py
@@ -136,8 +136,38 @@
         out_ref[part] = held[...]
 
 
-def prepare_kernel(gate, plan, query_ref, cot_ref, query_rows, dattn_rows, cot_t):
+def size_class(docs, counts, tiles, img_dev, classes):
+    def add_document(document, most):
+        live_tiles, crowd = jnp.int32(0), jnp.int32(0)
+        owners = []
+        for index in range(docs.shape[0]):
+            live = index < counts[document]
+            image = jnp.where(live, docs[index, document], 0)
+            live_tiles = live_tiles + jnp.where(live, tiles[image], 0)
+            owner = jnp.where(live, lax.div(image, img_dev), -1 - index)
+            rank = jnp.int32(1)
+            for other in owners:
+                rank = rank + jnp.where(other == owner, 1, 0)
+            owners.append(owner)
+            crowd = jnp.maximum(crowd, rank)
+        return jnp.maximum(most[0], live_tiles), jnp.maximum(most[1], crowd)
+
+    live_tiles, crowd = lax.fori_loop(
+        0, counts.shape[0], add_document, (jnp.int32(0), jnp.int32(0))
+    )
+    chosen = jnp.int32(len(classes) - 1)
+    for index in range(len(classes) - 2, -1, -1):
+        blocks, room = classes[index]
+        chosen = jnp.where((live_tiles <= blocks * TILES) & (crowd <= room), index, chosen)
+    return chosen
+
+
+def prepare_kernel(
+    img_dev, classes, gate, plan, docs, counts, tiles,
+    query_ref, cot_ref, query_rows, dattn_rows, cot_t, class_ref,
+):
     del plan
+    class_ref[0] = size_class(docs, counts, tiles, img_dev, classes)
     tok = query_ref.shape[0]
     head_dim = query_rows.shape[1]
     tanh_gate = jnp.tanh(jnp.full((1, head_dim), gate[0], F32))
@@ -440,16 +470,31 @@
         name="pack_chunks",
     )(doc_images.T, doc_counts, image_tiles, image_kv)
     chunks = lax.all_to_all(chunks, "seq", 0, 0)
-    prepared = call(
-        prepare_kernel,
+    classes = ((4, 2), (5, 2), (slots, img_dev))
+    *prepared, chosen = call(
+        functools.partial(prepare_kernel, img_dev, classes),
         "prepare_rows",
-        (low(rows, head_dim), low(rows, head_dim), full(head_dim, rows)),
-        (gate, plan),
+        (
+            low(rows, head_dim),
+            low(rows, head_dim),
+            full(head_dim, rows),
+            jax.ShapeDtypeStruct((1,), jnp.int32),
+        ),
+        (gate, plan, doc_images.T, doc_counts, image_tiles),
         (queries[0], grad_out[0]),
+        out_specs=(VMEM(), VMEM(), VMEM(), SMEM()),
     )
     chunks, prepared = lax.optimization_barrier((chunks, prepared))
-    gated, dquery, grads, grad_gate = after_scatter(
-        slots, slots, img_dev, img_dev, tok, width, prepared, chunks, gate, plan
+    gated, dquery, grads, grad_gate = lax.switch(
+        chosen[0],
+        [
+            functools.partial(after_scatter, slots, blocks, room, img_dev, tok, width)
+            for blocks, room in classes
+        ],
+        tuple(prepared),
+        chunks,
+        gate,
+        plan,
     )
     return gated[None], dquery[None], grads, grad_gate
 

time: 85.8 us -> 86.8 us (1.012); the launches traced: 87.2 us -> 86.5 us
  starting transfers between devices: 33 us -> 27.1 us
  Pallas kernels: 12.4 us -> 15.7 us
    ppermute x5, starting transfers between devices: 15.1 us -> 9.15 us  [moved(): return lax.ppermute(x, axis, [(i, i ^ step) for i in range(size)])]
    ppermute x5, waiting for transfers between devices: 4.74 us -> 8.23 us  [moved(): return lax.ppermute(x, axis, [(i, i ^ step) for i in range(size)])]
    pallas_call x6, Pallas kernels: 10.4 us -> 13.7 us  [call(): pl.pallas_call(kernel, out_shape=outs, in_specs=[SMEM()] * len(smem) + [V...]
    all_to_all x1, waiting for transfers between devices: 9.5 us -> 7.44 us  [per_device(): chunks = lax.all_to_all(chunks, 'seq', 0, 0)]
  transfers between devices with their start and end apart: 8 -> 8, of which waited for: 5 -> 5; matrix products, arithmetic and copies ran while one was open for 0% -> 0% of each run, Pallas kernels for 2% -> 4%
where the time goes in v11:
time: 86.8 us; the launch traced here: 86.5 us
  starting transfers between devices  27.1 us (31%)
  waiting for transfers between devices  24.3 us (28%)
  blocking collectives  16.2 us (19%)
  Pallas kernels  15.7 us (18%)
  between operations  2.21 us (3%)
    all_to_all x1, blocking collectives, after_scatter(): kv_cited = lax.all_to_all(cited, 'seq', 0, 0)  16.2 us
    pallas_call x6, Pallas kernels, call(): pl.pallas_call(kernel, out_shape=outs, in_specs=[SMEM()] * len(smem) + [V...  13.7 us
    ppermute x5, starting transfers between devices, moved(): return lax.ppermute(x, axis, [(i, i ^ step) for i in range(size)])  9.15 us
    all_to_all x1, waiting for transfers between devices, after_scatter(): owned = lax.all_to_all(summed, 'seq', 0, 0)  8.67 us
    ppermute x5, waiting for transfers between devices, moved(): return lax.ppermute(x, axis, [(i, i ^ step) for i in range(size)])  8.23 us
    all_to_all x1, waiting for transfers between devices, per_device(): chunks = lax.all_to_all(chunks, 'seq', 0, 0)  7.44 us
    all_to_all x1, starting transfers between devices, per_device(): chunks = lax.all_to_all(chunks, 'seq', 0, 0)  7.18 us
    all_to_all x1, starting transfers between devices, after_scatter(): owned = lax.all_to_all(summed, 'seq', 0, 0)  7.12 us
  transfers between devices with their start and end apart: 8, of which 5 were waited for; matrix products, arithmetic and copies ran while one was open for 0% of the time, Pallas kernels for 4%

profile of v11, /device:TPU:32, one launch (start us, length us, event | category | flops | bytes accessed | tf_op | source)
XLA Modules:
  0.0 86.5 jit_solution(3342976097486304049)
XLA Ops:
  0.6 2.0 %pack_chunks.1 = (bf16[16,64,256]{2,1,0:T(8,128)(2,1)}, s32[56]{0:T(128)S(1)}) custom-call(s32[6,16]{1,0:T(8,128)} %bitcast.8, s32[16]{0:T(128)} %counts.1, s32[1024]{0:T(1024)} %tiles.1, bf16[4,256,256]{2,1,0:T(8,128)(2,1)} %image_hbm.1), custom_call_target="tpu_custom_call" | custom-call | tf_op jit(solution)/shard_map/pack_chunks/pallas_call | solution.py:454
  2.6 0.0 copy-start.3
  2.6 7.2 %all-to-all-start.9 = ((bf16[16,64,256]{2,1,0:T(8,128)(2,1)}), bf16[16,64,256]{2,1,0:T(8,128)(2,1)S(1)}, u32[]{:S(2)}, u32[]{:S(2)}) async-start(bf16[16,64,256]{2,1,0:T(8,128)(2,1)} %get-tuple-element.98), calls=%async_computation.9 | async-start | bytes 1048576 | tf_op jit(solution)/shard_map/all_to_all | solution.py:472
  10.6 0.6 copy-done.4
  11.2 2.1 %prepare_rows.1 = (bf16[1024,128]{1,0:T(8,128)(2,1)S(1)}, bf16[1024,128]{1,0:T(8,128)(2,1)S(1)}, f32[128,1024]{1,0:T(8,128)S(1)}, s32[1]{0:T(128)}) custom-call(f32[1]{0:T(128)S(6)} %copy.23.gate, s32[56]{0:T(128)S(1)} %get-tuple-element.96.plan, s32[6,16]{1,0:T(8,128)S(1)} %bitcast.9, s32[16]{0:T(128)S(1)} %copy-done.4, s32[1024]{0:T(1024)S(1)} %copy-done.3, ...), custom_call_target="tpu_custom_call" | custom-call | tf_op jit(solution)/shard_map/prepare_rows/pallas_call | solution.py:364
  13.9 7.4 %all-to-all-done.9 = bf16[16,64,256]{2,1,0:T(8,128)(2,1)S(1)} async-done(((bf16[16,64,256]{2,1,0:T(8,128)(2,1)}), bf16[16,64,256]{2,1,0:T(8,128)(2,1)S(1)}, u32[]{:S(2)}, u32[]{:S(2)}) %all-to-all-start.9) | async-done | bytes 524320 | tf_op jit(solution)/shard_map/all_to_all | solution.py:472
  21.3 65.0 %conditional.1 = (bf16[128,1024]{1,0:T(8,128)(2,1)}, bf16[128,1024]{1,0:T(8,128)(2,1)}, f32[4,256,256]{2,1,0:T(8,128)}, f32[1]{0:T(128)}) conditional(s32[]{:T(128)} %bitcast.3, (s32[56]{0:T(128)S(1)}, bf16[16,64,256]{2,1,0:T(8,128)(2,1)S(1)}, f32[1]{0:T(128)}, bf16[1024,128]{1,0:T(8,128)(2,1)S(1)}, bf16[1024,128]{1,0:T(8,128)(2,1)S(1)}, ...), branch_computations={%region_0.0_spmd, %region_1.0_spmd, %region_2.0_spmd} | conditional | flops 5120 | bytes 5828904 | solution.py:488
  21.3 0.7 select_cited.5
  22.0 16.2 %all_to_all.43.kv_ref = bf16[16,96,256]{2,1,0:T(8,128)(2,1)S(1)} all-to-all(bf16[16,96,256]{2,1,0:T(8,128)(2,1)S(1)} %select_cited.5), channel_id=1, replica_groups=mesh['dp'=16,'seq'=16] {'seq'}, dimensions={0} | all-to-all | bytes 1572864 | tf_op jit(solution)/shard_map/cond/branch_2_fun/all_to_all | solution.py:398
  38.2 5.4 %attention.5 = (f32[128,1024]{1,0:T(8,128)S(1)}, f32[128,1024]{1,0:T(8,128)S(1)}, bf16[16,96,256]{2,1,0:T(8,128)(2,1)}, f32[8,128]{1,0:T(8,128)S(1)}) custom-call(s32[56]{0:T(128)S(1)} %get-tuple-element.65.plan, f32[1]{0:T(128)} %get-tuple-element.64.gate, bf16[16,96,256]{2,1,0:T(8,128)(2,1)S(1)} %all_to_all.43.kv_ref, ...), custom_call_target="tpu_custom_call" | custom-call | tf_op jit(solution)/shard_map/cond/branch_2_fun/attention/pallas_call | solution.py:364
  43.6 3.6 %all-to-all-start.7 = ((bf16[16,96,256]{2,1,0:T(8,128)(2,1)}), bf16[16,96,256]{2,1,0:T(8,128)(2,1)S(1)}, u32[]{:S(2)}, u32[]{:S(2)}) async-start(bf16[16,96,256]{2,1,0:T(8,128)(2,1)} %get-tuple-element.74), calls=%async_computation.7 | async-start | bytes 1572864 | tf_op jit(solution)/shard_map/cond/branch_2_fun/all_to_all | solution.py:421
  47.2 0.1 collective-permute-start.12
  47.3 3.1 %collective-permute-start.11 = (f32[8,128]{1,0:T(8,128)S(1)}, f32[8,128]{1,0:T(8,128)S(1)}, u32[]{:S(2)}, u32[]{:S(2)}) collective-permute-start(f32[8,128]{1,0:T(8,128)S(1)} %get-tuple-element.75), channel_id=1, source_target_pairs={{0,32},{16,48},{32,0},{48,16},{64,96},{80,112},{96,64},{112,80},{1... | collective-permute-start | bytes 12296 | tf_op jit(solution)/shard_map/cond/branch_2_fun/ppermute | solution.py:351
  50.4 0.0 collective-permute-start.10
  50.4 1.6 %collective-permute-done.11 = f32[8,128]{1,0:T(8,128)S(1)} collective-permute-done((f32[8,128]{1,0:T(8,128)S(1)}, f32[8,128]{1,0:T(8,128)S(1)}, u32[]{:S(2)}, u32[]{:S(2)}) %collective-permute-start.11) | collective-permute-done | bytes 4128 | tf_op jit(solution)/shard_map/cond/branch_2_fun/ppermute | solution.py:351
  52.0 5.3 %collective-permute-start.13 = (f32[8,128]{1,0:T(8,128)S(1)}, f32[8,128]{1,0:T(8,128)S(1)}, u32[]{:S(2)}, u32[]{:S(2)}) collective-permute-start(f32[8,128]{1,0:T(8,128)S(1)} %add_add_fusion.2), channel_id=1, source_target_pairs={{0,64},{16,80},{32,96},{48,112},{64,0},{80,16},{96,32},{112,48},{1... | collective-permute-start | bytes 12296 | tf_op jit(solution)/shard_map/cond/branch_2_fun/ppermute | solution.py:351
  57.3 1.6 %collective-permute-done.13 = f32[8,128]{1,0:T(8,128)S(1)} collective-permute-done((f32[8,128]{1,0:T(8,128)S(1)}, f32[8,128]{1,0:T(8,128)S(1)}, u32[]{:S(2)}, u32[]{:S(2)}) %collective-permute-start.13) | collective-permute-done | bytes 4128 | tf_op jit(solution)/shard_map/cond/branch_2_fun/ppermute | solution.py:351
  58.9 0.6 collective-permute-start.14
  59.5 5.1 %collective-permute-done.14 = f32[8,128]{1,0:T(8,128)S(1)} collective-permute-done((f32[8,128]{1,0:T(8,128)S(1)}, f32[8,128]{1,0:T(8,128)S(1)}, u32[]{:S(2)}, u32[]{:S(2)}) %collective-permute-start.14) | collective-permute-done | bytes 4128 | tf_op jit(solution)/shard_map/cond/branch_2_fun/ppermute | solution.py:351
  64.6 1.6 %sum_partials.5 = bf16[16,144,128]{2,1,0:T(8,128)(2,1)} custom-call(s32[56]{0:T(128)S(1)} %get-tuple-element.65.plan, bf16[16,96,256]{2,1,0:T(8,128)(2,1)S(1)} %all-to-all-done.7.partial_ref, f32[8,128]{1,0:T(8,128)S(1)} %add.44.gate_ref), custom_call_target="tpu_custom_call" | custom-call | tf_op jit(solution)/shard_map/cond/branch_2_fun/sum_partials/pallas_call | solution.py:364
  66.2 7.1 %all-to-all-start.8 = ((bf16[16,144,128]{2,1,0:T(8,128)(2,1)}), bf16[16,144,128]{2,1,0:T(8,128)(2,1)S(1)}, u32[]{:S(2)}, u32[]{:S(2)}) async-start(bf16[16,144,128]{2,1,0:T(8,128)(2,1)} %sum_partials.5), calls=%async_computation.8 | async-start | bytes 1179648 | tf_op jit(solution)/shard_map/cond/branch_2_fun/all_to_all | solution.py:434
  73.3 1.8 %finish_rows.5 = (bf16[128,1024]{1,0:T(8,128)(2,1)}, bf16[128,1024]{1,0:T(8,128)(2,1)}) custom-call(f32[1]{0:T(128)} %get-tuple-element.64.gate, f32[128,1024]{1,0:T(8,128)S(1)} %get-tuple-element.70.attn_t, f32[128,1024]{1,0:T(8,128)S(1)} %get-tuple-element.71.dquery_t), custom_call_target="tpu_custom_call" | custom-call | tf_op jit(solution)/shard_map/cond/branch_2_fun/finish_rows/pallas_call | solution.py:364
  75.1 8.7 %all-to-all-done.8.owned_ref = bf16[16,144,128]{2,1,0:T(8,128)(2,1)S(1)} async-done(((bf16[16,144,128]{2,1,0:T(8,128)(2,1)}), bf16[16,144,128]{2,1,0:T(8,128)(2,1)S(1)}, u32[]{:S(2)}, u32[]{:S(2)}) %all-to-all-start.8) | async-done | bytes 589856 | tf_op jit(solution)/shard_map/cond/branch_2_fun/all_to_all | solution.py:434
  83.8 2.3 %unpack_grads.5 = (f32[4,256,256]{2,1,0:T(8,128)}, f32[1]{0:T(128)}) custom-call(s32[56]{0:T(128)S(1)} %get-tuple-element.65.plan, f32[1]{0:T(128)} %get-tuple-element.64.gate, bf16[16,144,128]{2,1,0:T(8,128)(2,1)S(1)} %all-to-all-done.8.owned_ref), custom_call_target="tpu_custom_call" | custom-call | tf_op jit(solution)/shard_map/cond/branch_2_fun/unpack_grads/pallas_call | solution.py:364
  (14 shorter events, 0.0 us)
Async XLA Ops:
  2.6 7.9 %copy-start = (bf16[1,128,1024]{2,1,0:T(8,128)(2,1)S(1)}, bf16[1,128,1024]{2,1,0:T(8,128)(2,1)}, u32[]{:S(2)}) copy-start(bf16[1,128,1024]{2,1,0:T(8,128)(2,1)} %param.10) | copy-start | bytes 786436
  2.6 7.9 %copy-start.1 = (bf16[1,128,1024]{2,1,0:T(8,128)(2,1)S(1)}, bf16[1,128,1024]{2,1,0:T(8,128)(2,1)}, u32[]{:S(2)}) copy-start(bf16[1,128,1024]{2,1,0:T(8,128)(2,1)} %param.11) | copy-start | bytes 786436
  2.6 7.9 %copy-start.3 = (s32[1024]{0:T(1024)S(1)}, s32[1024]{0:T(1024)}, u32[]{:S(2)}) copy-start(s32[1024]{0:T(1024)} %tiles.1) | copy-start | bytes 12292
  2.6 18.7 %all-to-all-start.9 = ((bf16[16,64,256]{2,1,0:T(8,128)(2,1)}), bf16[16,64,256]{2,1,0:T(8,128)(2,1)S(1)}, u32[]{:S(2)}, u32[]{:S(2)}) async-start(bf16[16,64,256]{2,1,0:T(8,128)(2,1)} %get-tuple-element.98), calls=%async_computation.9 | async-start | bytes 1048576 | tf_op jit(solution)/shard_map/all_to_all | solution.py:472
  9.8 0.7 copy-start.2
  10.5 0.7 copy-start.4
  43.6 21.0 %all-to-all-start.7 = ((bf16[16,96,256]{2,1,0:T(8,128)(2,1)}), bf16[16,96,256]{2,1,0:T(8,128)(2,1)S(1)}, u32[]{:S(2)}, u32[]{:S(2)}) async-start(bf16[16,96,256]{2,1,0:T(8,128)(2,1)} %get-tuple-element.74), calls=%async_computation.7 | async-start | bytes 1572864 | tf_op jit(solution)/shard_map/cond/branch_2_fun/all_to_all | solution.py:421
  47.2 3.2 %collective-permute-start.12 = (f32[8,128]{1,0:T(8,128)S(1)}, f32[8,128]{1,0:T(8,128)S(1)}, u32[]{:S(2)}, u32[]{:S(2)}) collective-permute-start(f32[8,128]{1,0:T(8,128)S(1)} %get-tuple-element.75), channel_id=1, source_target_pairs={{0,48},{16,32},{32,16},{48,0},{64,112},{80,96},{96,80},{112,64},{1... | collective-permute-start | bytes 12296 | tf_op jit(solution)/shard_map/cond/branch_2_fun/ppermute | solution.py:351
  47.3 4.7 %collective-permute-start.11 = (f32[8,128]{1,0:T(8,128)S(1)}, f32[8,128]{1,0:T(8,128)S(1)}, u32[]{:S(2)}, u32[]{:S(2)}) collective-permute-start(f32[8,128]{1,0:T(8,128)S(1)} %get-tuple-element.75), channel_id=1, source_target_pairs={{0,32},{16,48},{32,0},{48,16},{64,96},{80,112},{96,64},{112,80},{1... | collective-permute-start | bytes 12296 | tf_op jit(solution)/shard_map/cond/branch_2_fun/ppermute | solution.py:351
  50.4 1.6 %collective-permute-start.10 = (f32[8,128]{1,0:T(8,128)S(1)}, f32[8,128]{1,0:T(8,128)S(1)}, u32[]{:S(2)}, u32[]{:S(2)}) collective-permute-start(f32[8,128]{1,0:T(8,128)S(1)} %get-tuple-element.75), channel_id=1, source_target_pairs={{0,16},{16,0},{32,48},{48,32},{64,80},{80,64},{96,112},{112,96},{1... | collective-permute-start | bytes 12296 | tf_op jit(solution)/shard_map/cond/branch_2_fun/ppermute | solution.py:351
  52.0 6.9 %collective-permute-start.13 = (f32[8,128]{1,0:T(8,128)S(1)}, f32[8,128]{1,0:T(8,128)S(1)}, u32[]{:S(2)}, u32[]{:S(2)}) collective-permute-start(f32[8,128]{1,0:T(8,128)S(1)} %add_add_fusion.2), channel_id=1, source_target_pairs={{0,64},{16,80},{32,96},{48,112},{64,0},{80,16},{96,32},{112,48},{1... | collective-permute-start | bytes 12296 | tf_op jit(solution)/shard_map/cond/branch_2_fun/ppermute | solution.py:351
  58.9 5.7 %collective-permute-start.14 = (f32[8,128]{1,0:T(8,128)S(1)}, f32[8,128]{1,0:T(8,128)S(1)}, u32[]{:S(2)}, u32[]{:S(2)}) collective-permute-start(f32[8,128]{1,0:T(8,128)S(1)} %add.43), channel_id=1, source_target_pairs={{0,192},{16,208},{32,224},{48,240},{64,128},{80,144},{96,160},{112... | collective-permute-start | bytes 12296 | tf_op jit(solution)/shard_map/cond/branch_2_fun/ppermute | solution.py:351
  66.2 17.6 %all-to-all-start.8 = ((bf16[16,144,128]{2,1,0:T(8,128)(2,1)}), bf16[16,144,128]{2,1,0:T(8,128)(2,1)S(1)}, u32[]{:S(2)}, u32[]{:S(2)}) async-start(bf16[16,144,128]{2,1,0:T(8,128)(2,1)} %sum_partials.5), calls=%async_computation.8 | async-start | bytes 1179648 | tf_op jit(solution)/shard_map/cond/branch_2_fun/all_to_all | solution.py:434
